TPU v7x, 32 devices: a whole 2x2x4 slice. The times are simulated.
32 devices in a mesh: section: 2 (over x), replica: 2 (over core), shard: 8 (over z, y).
Axes of the slice: x: 2, y: 2, z: 4, core: 2. Of those that a mesh axis runs over, the one named last changes fastest.
Arguments:
- tokens: bfloat16 [4, 1024, 768], P('replica', 'shard'), may hold values from -6 to 6
- cotangent: bfloat16 [4, 1024, 768], P('replica', 'shard'), may hold values from -6 to 6
- group_order: int32 [4, 8], P('replica'), may hold values from 0 to 7, each once within a row
- norm_gains: bfloat16 [2, 2, 768], P('section', None, 'shard'), may hold values from 0.099609375 to 1.8984375
- norm_biases: bfloat16 [2, 2, 768], P('section', None, 'shard'), may hold values from -3 to 3
- w_qkv: bfloat16 [2, 768, 2304], P('section', 'shard'), may hold values from -0.21875 to 0.21875
- qv_bias: bfloat16 [2, 2, 768], P('section', None, 'shard'), may hold values from -3 to 3
- w_out: bfloat16 [2, 768, 768], P('section', 'shard'), may hold values from -1.25 to 1.25
- out_bias: bfloat16 [2, 768], P('section', 'shard'), may hold values from -3 to 3
- w_fc: bfloat16 [2, 768, 3072], P('section', 'shard'), may hold values from -0.21875 to 0.21875
- fc_bias: bfloat16 [2, 3072], P('section', 'shard'), may hold values from -3 to 3
- w_proj: bfloat16 [2, 3072, 768], P('section', 'shard'), may hold values from -0.109375 to 0.109375
- proj_bias: bfloat16 [2, 768], P('section', 'shard'), may hold values from -3 to 3
Outputs:
- acts: bfloat16 [2, 4, 1024, 768], P('section', 'replica', 'shard')
- in_grads: float32 [2, 4, 1024, 768], P('section', 'replica', 'shard')
- norm_gains_grad: float32 [2, 2, 768], P('section', None, 'shard')
- norm_biases_grad: float32 [2, 2, 768], P('section', None, 'shard')
- w_qkv_grad: float32 [2, 768, 2304], P('section', 'shard')
- qv_bias_grad: float32 [2, 2, 768], P('section', None, 'shard')
- w_out_grad: float32 [2, 768, 768], P('section', 'shard')
- out_bias_grad: float32 [2, 768], P('section', 'shard')
- w_fc_grad: float32 [2, 768, 3072], P('section', 'shard')
- fc_bias_grad: float32 [2, 3072], P('section', 'shard')
- w_proj_grad: float32 [2, 3072, 768], P('section', 'shard')
- proj_bias_grad: float32 [2, 768], P('section', 'shard')
Inputs may be any that keep to these rules, and one draw needn't show every extreme that they name: Each row of group_order holds every number 0 to 7 once.
All inputs are finite; a program needn't handle non-finite values.
Results may differ from a plain program's by a relative error of at most 0.02.
Values may be sent and summed in bfloat16 or wider, within the bound.
No kernel may reach another device: no remote copies, remote signals or barrier semaphores. Data moves between devices by JAX's collectives and lax.ppermute only.
A program may use at most 192 MiB of HBM per device.

v0:
```python
import math

import jax
import jax.numpy as jnp
from jax import lax
from jax.sharding import PartitionSpec as P

HEADS = 12
HEAD = 64


EPSILON = 1e-05
SCALING = 0.125
FLOOR = -1e30


def shifted(x, axis, by):
    peers = lax.axis_size(axis)
    pairs = [(i, i + by) for i in range(peers) if 0 <= i + by < peers]
    return lax.ppermute(x, axis, pairs)


def normalize(values, gain_row, offset):
    average = jnp.mean(values, axis=-1, keepdims=True)
    centred = values - average
    variance = jnp.mean(centred * centred, axis=-1, keepdims=True)
    return centred * lax.rsqrt(variance + EPSILON) * gain_row + offset


def gelu_tanh(values):
    return jax.nn.gelu(values, approximate=True)


def block_rows(segment, shard_count):
    return segment * math.gcd(shard_count, max(1, 512 // segment))


def row_positions(order_row, segment, shard_count):
    all_rows = jnp.arange(segment * shard_count, dtype=jnp.int32)
    groups = all_rows // segment
    group_ids = jnp.arange(shard_count, dtype=jnp.int32)
    owners = jnp.sum(
        jnp.where(groups[:, None] == group_ids[None, :], order_row[None, :], 0), axis=1
    )
    return owners * segment + all_rows % segment


def split_blocks(all_keys, all_values, key_pos, key_rows):
    blocks = all_keys.shape[0] // key_rows
    return (
        all_keys.reshape(blocks, key_rows, HEADS, HEAD),
        all_values.reshape(blocks, key_rows, HEADS, HEAD),
        key_pos.reshape(blocks, key_rows),
    )


def block_scores(query_heads, key_block, pos_block, query_pos):
    scores = (
        jnp.einsum("ihd,jhd->hij", query_heads, key_block, preferred_element_type=jnp.float32)
        * SCALING
    )
    visible = pos_block[None, None, :] <= query_pos[None, :, None]
    return (scores, visible)


def attend_forward(queries, all_keys, all_values, query_pos, key_pos, key_rows):
    length = queries.shape[0]
    query_heads = queries.reshape(length, HEADS, HEAD)
    key_blocks, value_blocks, pos_blocks = split_blocks(all_keys, all_values, key_pos, key_rows)
    latest = jnp.max(query_pos)

    def first_pass(running, key_pair):
        key_block, pos_block = key_pair

        def first_compute_block(kept_state):
            highest, denominator = kept_state
            scores, visible = block_scores(query_heads, key_block, pos_block, query_pos)
            scores = jnp.where(visible, scores, FLOOR)
            raised = jnp.maximum(highest, jnp.max(scores, axis=-1))
            exp_terms = jnp.where(visible, jnp.exp(scores - raised[:, :, None]), 0.0)
            return (raised, denominator * jnp.exp(highest - raised) + jnp.sum(exp_terms, axis=-1))

        return (
            lax.cond(
                jnp.min(pos_block) > latest,
                lambda kept_state: kept_state,
                first_compute_block,
                running,
            ),
            None,
        )

    initial = (
        jnp.full((HEADS, length), FLOOR, jnp.float32),
        jnp.zeros((HEADS, length), jnp.float32),
    )
    (highest, denominator), _ = lax.scan(first_pass, initial, (key_blocks, pos_blocks))
    log_total = highest + jnp.log(denominator)

    def second_pass(running, triple):
        key_block, value_block, pos_block = triple

        def second_compute_block(summed):
            scores, visible = block_scores(query_heads, key_block, pos_block, query_pos)
            weights = jnp.where(visible, jnp.exp(scores - log_total[:, :, None]), 0.0).astype(
                jnp.bfloat16
            )
            return summed + jnp.einsum(
                "hij,jhd->ihd", weights, value_block, preferred_element_type=jnp.float32
            )

        return (
            lax.cond(
                jnp.min(pos_block) > latest, lambda summed: summed, second_compute_block, running
            ),
            None,
        )

    attended, _ = lax.scan(
        second_pass,
        jnp.zeros((length, HEADS, HEAD), jnp.float32),
        (key_blocks, value_blocks, pos_blocks),
    )
    return (attended.reshape(length, HEADS * HEAD), log_total)


def attend_backward(
    queries, all_keys, all_values, query_pos, key_pos, key_rows, log_total, grad_attended, row_dots
):
    length = queries.shape[0]
    model_width = queries.shape[1]
    query_heads = queries.reshape(length, HEADS, HEAD)
    grad_heads = grad_attended.reshape(length, HEADS, HEAD)
    key_blocks, value_blocks, pos_blocks = split_blocks(all_keys, all_values, key_pos, key_rows)
    latest = jnp.max(query_pos)

    def one_step(running, triple):
        key_block, value_block, pos_block = triple

        def one_compute_block(summed):
            scores, visible = block_scores(query_heads, key_block, pos_block, query_pos)
            weights = jnp.where(visible, jnp.exp(scores - log_total[:, :, None]), 0.0)
            grad_weights = jnp.einsum(
                "ihd,jhd->hij", grad_heads, value_block, preferred_element_type=jnp.float32
            )
            grad_scores = (weights * (grad_weights - row_dots[:, :, None])).astype(jnp.bfloat16)
            grad_keys = (
                jnp.einsum(
                    "hij,ihd->jhd", grad_scores, query_heads, preferred_element_type=jnp.float32
                )
                * SCALING
            )
            grad_values = jnp.einsum(
                "hij,ihd->jhd",
                weights.astype(jnp.bfloat16),
                grad_heads,
                preferred_element_type=jnp.float32,
            )
            summed = summed + jnp.einsum(
                "hij,jhd->ihd", grad_scores, key_block, preferred_element_type=jnp.float32
            )
            return (
                summed,
                jnp.concatenate(
                    [
                        grad_keys.reshape(key_rows, model_width),
                        grad_values.reshape(key_rows, model_width),
                    ],
                    axis=1,
                ),
            )

        def skipped(summed):
            return (summed, jnp.zeros((key_rows, 2 * model_width), jnp.float32))

        return lax.cond(jnp.min(pos_block) > latest, skipped, one_compute_block, running)

    grad_queries, key_terms = lax.scan(
        one_step,
        jnp.zeros((length, HEADS, HEAD), jnp.float32),
        (key_blocks, value_blocks, pos_blocks),
    )
    return (
        grad_queries.reshape(length, model_width) * SCALING,
        key_terms.reshape(all_keys.shape[0], 2 * model_width),
    )


def layer_forward(inputs, order_row, shard_index, weights):
    gain_rows, offset_rows, w_qkv, qv_bias, w_out, out_bias, w_fc, fc_bias, w_proj, proj_bias = (
        weights
    )
    segment, model_width = inputs.shape
    shard_count = lax.axis_size("shard")
    normed = normalize(
        inputs, gain_rows[0].astype(jnp.float32), offset_rows[0].astype(jnp.float32)
    ).astype(jnp.bfloat16)
    joined = jnp.dot(normed, w_qkv, preferred_element_type=jnp.float32)
    queries = (joined[:, :model_width] + qv_bias[0].astype(jnp.float32)).astype(jnp.bfloat16)
    key_local = joined[:, model_width : 2 * model_width].astype(jnp.bfloat16)
    value_local = (joined[:, 2 * model_width :] + qv_bias[1].astype(jnp.float32)).astype(
        jnp.bfloat16
    )
    all_keys, all_values = (
        lax.all_gather(key_local, "shard", axis=0, tiled=True),
        lax.all_gather(value_local, "shard", axis=0, tiled=True),
    )
    key_pos = row_positions(order_row, segment, shard_count)
    query_pos = lax.dynamic_slice_in_dim(key_pos, shard_index * segment, segment)
    attended, log_total = attend_forward(
        queries, all_keys, all_values, query_pos, key_pos, block_rows(segment, shard_count)
    )
    middle = (
        inputs
        + jnp.dot(attended.astype(jnp.bfloat16), w_out, preferred_element_type=jnp.float32)
        + out_bias.astype(jnp.float32)
    )
    normed_two = normalize(
        middle, gain_rows[1].astype(jnp.float32), offset_rows[1].astype(jnp.float32)
    ).astype(jnp.bfloat16)
    hidden = jnp.dot(normed_two, w_fc, preferred_element_type=jnp.float32) + fc_bias.astype(
        jnp.float32
    )
    active = gelu_tanh(hidden).astype(jnp.bfloat16)
    output = (
        middle
        + jnp.dot(active, w_proj, preferred_element_type=jnp.float32)
        + proj_bias.astype(jnp.float32)
    )
    return (
        output,
        (
            inputs,
            normed,
            queries,
            key_local,
            value_local,
            attended,
            log_total,
            middle,
            normed_two,
            hidden,
            active,
        ),
    )


def layer_backward(arriving, saved_state, order_row, shard_index, weights):
    gain_rows, offset_rows, w_qkv, qv_bias, w_out, out_bias, w_fc, fc_bias, w_proj, proj_bias = (
        weights
    )
    (
        inputs,
        normed,
        queries,
        key_local,
        value_local,
        attended,
        log_total,
        middle,
        normed_two,
        hidden,
        active,
    ) = saved_state
    segment, model_width = inputs.shape
    shard_count = lax.axis_size("shard")
    grad_branch = arriving.astype(jnp.bfloat16)
    grad_active = jnp.einsum("td,fd->tf", grad_branch, w_proj, preferred_element_type=jnp.float32)
    grad_hidden = jax.vjp(gelu_tanh, hidden)[1](grad_active)[0].astype(jnp.bfloat16)
    grad_normed_two = jnp.einsum("tf,df->td", grad_hidden, w_fc, preferred_element_type=jnp.float32)
    grad_middle_norm, gain_two_term, offset_two_term = jax.vjp(
        normalize, middle, gain_rows[1].astype(jnp.float32), offset_rows[1].astype(jnp.float32)
    )[1](grad_normed_two)
    proj_term = jnp.einsum("tf,td->fd", active, grad_branch, preferred_element_type=jnp.float32)
    proj_bias_term = jnp.sum(grad_branch.astype(jnp.float32), axis=0)
    fc_term = jnp.einsum("td,tf->df", normed_two, grad_hidden, preferred_element_type=jnp.float32)
    fc_bias_term = jnp.sum(grad_hidden.astype(jnp.float32), axis=0)
    fc_sum, fc_bias_sum, proj_sum, proj_bias_sum = (
        lax.psum_scatter(
            fc_term[None].astype(jnp.bfloat16), "shard", scatter_dimension=1, tiled=True
        ).astype(jnp.float32),
        lax.psum_scatter(
            fc_bias_term[None].astype(jnp.bfloat16), "shard", scatter_dimension=1, tiled=True
        ).astype(jnp.float32),
        lax.psum_scatter(
            proj_term[None].astype(jnp.bfloat16), "shard", scatter_dimension=1, tiled=True
        ).astype(jnp.float32),
        lax.psum_scatter(
            proj_bias_term[None].astype(jnp.bfloat16), "shard", scatter_dimension=1, tiled=True
        ).astype(jnp.float32),
    )
    grad_middle = arriving + grad_middle_norm
    grad_out_branch = grad_middle.astype(jnp.bfloat16)
    attended_low = attended.astype(jnp.bfloat16)
    grad_attended = jnp.einsum(
        "td,ed->te", grad_out_branch, w_out, preferred_element_type=jnp.float32
    ).astype(jnp.bfloat16)
    row_dots = jnp.sum(
        (grad_attended.astype(jnp.float32) * attended).reshape(segment, HEADS, HEAD), axis=2
    ).T
    all_keys, all_values = (
        lax.all_gather(key_local, "shard", axis=0, tiled=True),
        lax.all_gather(value_local, "shard", axis=0, tiled=True),
    )
    key_pos = row_positions(order_row, segment, shard_count)
    query_pos = lax.dynamic_slice_in_dim(key_pos, shard_index * segment, segment)
    grad_queries, key_terms = attend_backward(
        queries,
        all_keys,
        all_values,
        query_pos,
        key_pos,
        block_rows(segment, shard_count),
        log_total,
        grad_attended,
        row_dots,
    )
    key_grads = lax.psum_scatter(
        key_terms.astype(jnp.bfloat16), "shard", scatter_dimension=0, tiled=True
    ).astype(jnp.float32)
    grad_query_low = grad_queries.astype(jnp.bfloat16)
    grad_key_low = key_grads[:, :model_width].astype(jnp.bfloat16)
    grad_value_low = key_grads[:, model_width:].astype(jnp.bfloat16)
    grad_joined = jnp.concatenate([grad_query_low, grad_key_low, grad_value_low], axis=1)
    grad_normed = jnp.einsum("tc,dc->td", grad_joined, w_qkv, preferred_element_type=jnp.float32)
    grad_input_norm, gain_one_term, offset_one_term = jax.vjp(
        normalize, inputs, gain_rows[0].astype(jnp.float32), offset_rows[0].astype(jnp.float32)
    )[1](grad_normed)
    gain_terms = jnp.stack([gain_one_term, gain_two_term])
    offset_terms = jnp.stack([offset_one_term, offset_two_term])
    out_term = jnp.einsum(
        "te,td->ed", attended_low, grad_out_branch, preferred_element_type=jnp.float32
    )
    out_bias_term = jnp.sum(grad_out_branch.astype(jnp.float32), axis=0)
    qkv_term = jnp.einsum("td,tc->dc", normed, grad_joined, preferred_element_type=jnp.float32)
    qv_bias_term = jnp.stack(
        [
            jnp.sum(grad_query_low.astype(jnp.float32), axis=0),
            jnp.sum(grad_value_low.astype(jnp.float32), axis=0),
        ]
    )
    gain_sum, offset_sum, qkv_sum, qv_bias_sum, out_sum, out_bias_sum = (
        lax.psum_scatter(
            gain_terms[None].astype(jnp.bfloat16), "shard", scatter_dimension=2, tiled=True
        ).astype(jnp.float32),
        lax.psum_scatter(
            offset_terms[None].astype(jnp.bfloat16), "shard", scatter_dimension=2, tiled=True
        ).astype(jnp.float32),
        lax.psum_scatter(
            qkv_term[None].astype(jnp.bfloat16), "shard", scatter_dimension=1, tiled=True
        ).astype(jnp.float32),
        lax.psum_scatter(
            qv_bias_term[None].astype(jnp.bfloat16), "shard", scatter_dimension=2, tiled=True
        ).astype(jnp.float32),
        lax.psum_scatter(
            out_term[None].astype(jnp.bfloat16), "shard", scatter_dimension=1, tiled=True
        ).astype(jnp.float32),
        lax.psum_scatter(
            out_bias_term[None].astype(jnp.bfloat16), "shard", scatter_dimension=1, tiled=True
        ).astype(jnp.float32),
    )
    return (
        grad_middle + grad_input_norm,
        (
            gain_sum,
            offset_sum,
            qkv_sum,
            qv_bias_sum,
            out_sum,
            out_bias_sum,
            fc_sum,
            fc_bias_sum,
            proj_sum,
            proj_bias_sum,
        ),
    )


def on_device(
    tokens,
    cotangent,
    group_order,
    norm_gains,
    norm_biases,
    w_qkv,
    qv_bias,
    w_out,
    out_bias,
    w_fc,
    fc_bias,
    w_proj,
    proj_bias,
):
    section_count = lax.axis_size("section")
    section_index = lax.axis_index("section")
    shard_index = lax.axis_index("shard")
    micro_count = tokens.shape[0]
    segment = tokens.shape[1]
    model_width = tokens.shape[2]
    rounds = micro_count + section_count - 1
    last_section = section_count - 1
    gathered = (
        lax.all_gather(norm_gains, "shard", axis=2, tiled=True),
        lax.all_gather(norm_biases, "shard", axis=2, tiled=True),
        lax.all_gather(w_qkv, "shard", axis=1, tiled=True),
        lax.all_gather(qv_bias, "shard", axis=2, tiled=True),
        lax.all_gather(w_out, "shard", axis=1, tiled=True),
        lax.all_gather(out_bias, "shard", axis=1, tiled=True),
        lax.all_gather(w_fc, "shard", axis=1, tiled=True),
        lax.all_gather(fc_bias, "shard", axis=1, tiled=True),
        lax.all_gather(w_proj, "shard", axis=1, tiled=True),
        lax.all_gather(proj_bias, "shard", axis=1, tiled=True),
    )
    forward_weights = tuple((gathered_part[0] for gathered_part in gathered))
    incoming = jnp.zeros((segment, model_width), jnp.bfloat16)
    results = []
    states = []
    for round_index in range(rounds):
        member = jnp.clip(round_index - section_index, 0, micro_count - 1)
        own_tokens = lax.dynamic_index_in_dim(tokens, member, 0, keepdims=False)
        source = jnp.where(section_index == 0, own_tokens, incoming)
        order_row = lax.dynamic_index_in_dim(group_order, member, 0, keepdims=False)
        output, saved_state = layer_forward(
            source.astype(jnp.float32), order_row, shard_index, forward_weights
        )
        outgoing = output.astype(jnp.bfloat16)
        results.append(outgoing)
        states.append(saved_state)
        if round_index + 1 < rounds:
            incoming = shifted(outgoing, "section", 1)
    regathered = (
        lax.all_gather(norm_gains, "shard", axis=2, tiled=True),
        lax.all_gather(norm_biases, "shard", axis=2, tiled=True),
        lax.all_gather(w_qkv, "shard", axis=1, tiled=True),
        lax.all_gather(qv_bias, "shard", axis=2, tiled=True),
        lax.all_gather(w_out, "shard", axis=1, tiled=True),
        lax.all_gather(out_bias, "shard", axis=1, tiled=True),
        lax.all_gather(w_fc, "shard", axis=1, tiled=True),
        lax.all_gather(fc_bias, "shard", axis=1, tiled=True),
        lax.all_gather(w_proj, "shard", axis=1, tiled=True),
        lax.all_gather(proj_bias, "shard", axis=1, tiled=True),
    )
    backward_weights = tuple((gathered_part[0] for gathered_part in regathered))
    stacked = jax.tree.map(lambda *members: jnp.stack(members), *states)
    incoming_grad = jnp.zeros((segment, model_width), jnp.bfloat16)
    grad_inputs = []
    sums = None
    for round_index in range(rounds):
        member = round_index - (last_section - section_index)
        in_range = (member >= 0) & (member < micro_count)
        member = jnp.clip(member, 0, micro_count - 1)
        upstream = lax.dynamic_index_in_dim(cotangent, member, 0, keepdims=False)
        upstream = jnp.where(in_range, upstream, jnp.zeros_like(upstream))
        arriving = jnp.where(section_index == last_section, upstream, incoming_grad)
        saved_state = jax.tree.map(
            lambda member_stack: lax.dynamic_index_in_dim(
                member_stack, member + section_index, 0, keepdims=False
            ),
            stacked,
        )
        order_row = lax.dynamic_index_in_dim(group_order, member, 0, keepdims=False)
        grad_input, weight_grads = layer_backward(
            arriving.astype(jnp.float32), saved_state, order_row, shard_index, backward_weights
        )
        grad_inputs.append(grad_input)
        sums = weight_grads if sums is None else jax.tree.map(jnp.add, sums, weight_grads)
        if round_index + 1 < rounds:
            incoming_grad = shifted(grad_input.astype(jnp.bfloat16), "section", -1)
    totals = (
        lax.psum(sums[0].astype(jnp.bfloat16), "replica").astype(jnp.float32),
        lax.psum(sums[1].astype(jnp.bfloat16), "replica").astype(jnp.float32),
        lax.psum(sums[2].astype(jnp.bfloat16), "replica").astype(jnp.float32),
        lax.psum(sums[3].astype(jnp.bfloat16), "replica").astype(jnp.float32),
        lax.psum(sums[4].astype(jnp.bfloat16), "replica").astype(jnp.float32),
        lax.psum(sums[5].astype(jnp.bfloat16), "replica").astype(jnp.float32),
        lax.psum(sums[6].astype(jnp.bfloat16), "replica").astype(jnp.float32),
        lax.psum(sums[7].astype(jnp.bfloat16), "replica").astype(jnp.float32),
        lax.psum(sums[8].astype(jnp.bfloat16), "replica").astype(jnp.float32),
        lax.psum(sums[9].astype(jnp.bfloat16), "replica").astype(jnp.float32),
    )
    acts = lax.dynamic_slice_in_dim(jnp.stack(results), section_index, micro_count, 0)[None]
    in_grads = lax.dynamic_slice_in_dim(
        jnp.stack(grad_inputs), last_section - section_index, micro_count, 0
    )[None]
    return (
        acts,
        in_grads,
        totals[0],
        totals[1],
        totals[2],
        totals[3],
        totals[4],
        totals[5],
        totals[6],
        totals[7],
        totals[8],
        totals[9],
    )


def solution(mesh):
    in_specs = (
        P("replica", "shard", None),
        P("replica", "shard", None),
        P("replica", None),
        P("section", None, "shard"),
        P("section", None, "shard"),
        P("section", "shard", None),
        P("section", None, "shard"),
        P("section", "shard", None),
        P("section", "shard"),
        P("section", "shard", None),
        P("section", "shard"),
        P("section", "shard", None),
        P("section", "shard"),
    )
    out_specs = (
        P("section", "replica", "shard", None),
        P("section", "replica", "shard", None),
        P("section", None, "shard"),
        P("section", None, "shard"),
        P("section", "shard", None),
        P("section", None, "shard"),
        P("section", "shard", None),
        P("section", "shard"),
        P("section", "shard", None),
        P("section", "shard"),
        P("section", "shard", None),
        P("section", "shard"),
    )
    return jax.shard_map(
        on_device, mesh=mesh, in_specs=in_specs, out_specs=out_specs, check_vma=False
    )
```

profile of v0, /device:TPU:0, one launch (start us, length us, event | category | flops | bytes accessed | tf_op | source)
XLA Modules:
  0.0 3398.1 jit_solution(2142036697207267246)
XLA Ops:
  224.1 78.8 %all-gather.31.cloned.1.call-done = bf16[1,768,3072]{2,1,0:T(8,128)(2,1)} async-done(((bf16[1,96,3072]{2,1,0:T(8,128)(2,1)}), bf16[1,768,3072]{2,1,0:T(8,128)(2,1)}) %all-gather.31.cloned.1.call-update) | async-done | bytes 4718608 | tf_op jit(solution)/shard_map/all_gather | solution.py:409
  306.1 76.8 %all-gather.33.cloned.1.call-done = bf16[1,3072,768]{2,1,0:T(8,128)(2,1)} async-done(((bf16[1,384,768]{2,1,0:T(8,128)(2,1)}), bf16[1,3072,768]{2,1,0:T(8,128)(2,1)}) %all-gather.33.cloned.1.call-update) | async-done | bytes 4718608 | tf_op jit(solution)/shard_map/all_gather | solution.py:411
  806.1 66.9 %reduce-scatter.70.cloned.1.call-done = bf16[128,1536]{1,0:T(8,128)(2,1)} async-done(((bf16[1024,1536]{1,0:T(8,128)(2,1)}), bf16[128,1536]{1,0:T(8,128)(2,1)}) %reduce-scatter.70.cloned.1.call-update) | async-done | bytes 393232 | tf_op jit(solution)/shard_map/reduce_scatter | solution.py:318
  975.9 64.1 %reduce-scatter.72.cloned.1.call-done = bf16[128,1536]{1,0:T(8,128)(2,1)} async-done(((bf16[1024,1536]{1,0:T(8,128)(2,1)}), bf16[128,1536]{1,0:T(8,128)(2,1)}) %reduce-scatter.72.cloned.1.call-update) | async-done | bytes 393232 | tf_op jit(solution)/shard_map/reduce_scatter | solution.py:318
  1296.7 63.4 %reduce-scatter.124.cloned.1.call-done = bf16[384,1]{1,0:T(8,128)(2,1)} async-done(((bf16[3072,1]{1,0:T(8,128)(2,1)}), bf16[384,1]{1,0:T(8,128)(2,1)}) %reduce-scatter.124.cloned.1.call-update) | async-done | bytes 784
  1362.9 60.8 %reduce-scatter.100.cloned.1.call-done = bf16[96,2]{1,0:T(8,128)(2,1)} async-done(((bf16[768,2]{1,0:T(8,128)(2,1)}), bf16[96,2]{1,0:T(8,128)(2,1)}) %reduce-scatter.100.cloned.1.call-update) | async-done | bytes 400
  1426.6 60.7 %reduce-scatter.106.cloned.1.call-done = bf16[96,2]{1,0:T(8,128)(2,1)} async-done(((bf16[768,2]{1,0:T(8,128)(2,1)}), bf16[96,2]{1,0:T(8,128)(2,1)}) %reduce-scatter.106.cloned.1.call-update) | async-done | bytes 400
  1490.2 60.9 %reduce-scatter.112.cloned.1.call-done = bf16[96,2]{1,0:T(8,128)(2,1)} async-done(((bf16[768,2]{1,0:T(8,128)(2,1)}), bf16[96,2]{1,0:T(8,128)(2,1)}) %reduce-scatter.112.cloned.1.call-update) | async-done | bytes 400
  1553.9 60.8 %reduce-scatter.120.cloned.1.call-done = bf16[96,1]{1,0:T(8,128)(2,1)} async-done(((bf16[768,1]{1,0:T(8,128)(2,1)}), bf16[96,1]{1,0:T(8,128)(2,1)}) %reduce-scatter.120.cloned.1.call-update) | async-done | bytes 208
  1616.1 62.2 %reduce-scatter.132.cloned.1.call-done = bf16[96,1]{1,0:T(8,128)(2,1)} async-done(((bf16[768,1]{1,0:T(8,128)(2,1)}), bf16[96,1]{1,0:T(8,128)(2,1)}) %reduce-scatter.132.cloned.1.call-update) | async-done | bytes 208
  1679.6 64.5 %reduce-scatter.126.cloned.1.call-done = bf16[384,1]{1,0:T(8,128)(2,1)} async-done(((bf16[3072,1]{1,0:T(8,128)(2,1)}), bf16[384,1]{1,0:T(8,128)(2,1)}) %reduce-scatter.126.cloned.1.call-update) | async-done | bytes 784
  1745.6 61.8 %reduce-scatter.102.cloned.1.call-done = bf16[96,2]{1,0:T(8,128)(2,1)} async-done(((bf16[768,2]{1,0:T(8,128)(2,1)}), bf16[96,2]{1,0:T(8,128)(2,1)}) %reduce-scatter.102.cloned.1.call-update) | async-done | bytes 400
  1810.2 60.5 %reduce-scatter.108.cloned.1.call-done = bf16[96,2]{1,0:T(8,128)(2,1)} async-done(((bf16[768,2]{1,0:T(8,128)(2,1)}), bf16[96,2]{1,0:T(8,128)(2,1)}) %reduce-scatter.108.cloned.1.call-update) | async-done | bytes 400
  1873.5 60.6 %reduce-scatter.114.cloned.1.call-done = bf16[96,2]{1,0:T(8,128)(2,1)} async-done(((bf16[768,2]{1,0:T(8,128)(2,1)}), bf16[96,2]{1,0:T(8,128)(2,1)}) %reduce-scatter.114.cloned.1.call-update) | async-done | bytes 400
  1937.6 59.9 %reduce-scatter.122.cloned.1.call-done = bf16[96,1]{1,0:T(8,128)(2,1)} async-done(((bf16[768,1]{1,0:T(8,128)(2,1)}), bf16[96,1]{1,0:T(8,128)(2,1)}) %reduce-scatter.122.cloned.1.call-update) | async-done | bytes 208
  1998.3 62.4 %reduce-scatter.134.cloned.1.call-done = bf16[96,1]{1,0:T(8,128)(2,1)} async-done(((bf16[768,1]{1,0:T(8,128)(2,1)}), bf16[96,1]{1,0:T(8,128)(2,1)}) %reduce-scatter.134.cloned.1.call-update) | async-done | bytes 208
  2064.5 61.7 %reduce-scatter.128.cloned.1.call-done = bf16[384,1]{1,0:T(8,128)(2,1)} async-done(((bf16[3072,1]{1,0:T(8,128)(2,1)}), bf16[384,1]{1,0:T(8,128)(2,1)}) %reduce-scatter.128.cloned.1.call-update) | async-done | bytes 784
  2128.5 64.5 %reduce-scatter.82.cloned.1.call-done = bf16[1,96,768]{2,1,0:T(8,128)(2,1)} async-done(((bf16[1,768,768]{2,1,0:T(8,128)(2,1)}), bf16[1,96,768]{2,1,0:T(8,128)(2,1)}) %reduce-scatter.82.cloned.1.call-update) | async-done | bytes 147472 | tf_op jit(solution)/shard_map/reduce_scatter | solution.py:355
  2193.0 66.7 %reduce-scatter.84.cloned.1.call-done = bf16[1,96,768]{2,1,0:T(8,128)(2,1)} async-done(((bf16[1,768,768]{2,1,0:T(8,128)(2,1)}), bf16[1,96,768]{2,1,0:T(8,128)(2,1)}) %reduce-scatter.84.cloned.1.call-update) | async-done | bytes 147472 | tf_op jit(solution)/shard_map/reduce_scatter | solution.py:355
  2259.7 67.3 %reduce-scatter.86.cloned.1.call-done = bf16[1,96,768]{2,1,0:T(8,128)(2,1)} async-done(((bf16[1,768,768]{2,1,0:T(8,128)(2,1)}), bf16[1,96,768]{2,1,0:T(8,128)(2,1)}) %reduce-scatter.86.cloned.1.call-update) | async-done | bytes 147472 | tf_op jit(solution)/shard_map/reduce_scatter | solution.py:355
  2338.8 86.6 %reduce-scatter.88.cloned.1.call-done = bf16[1,96,3072]{2,1,0:T(8,128)(2,1)} async-done(((bf16[1,768,3072]{2,1,0:T(8,128)(2,1)}), bf16[1,96,3072]{2,1,0:T(8,128)(2,1)}) %reduce-scatter.88.cloned.1.call-update) | async-done | bytes 589840 | tf_op jit(solution)/shard_map/reduce_scatter | solution.py:279
  2425.4 99.0 %reduce-scatter.90.cloned.1.call-done = bf16[1,96,3072]{2,1,0:T(8,128)(2,1)} async-done(((bf16[1,768,3072]{2,1,0:T(8,128)(2,1)}), bf16[1,96,3072]{2,1,0:T(8,128)(2,1)}) %reduce-scatter.90.cloned.1.call-update) | async-done | bytes 589840 | tf_op jit(solution)/shard_map/reduce_scatter | solution.py:279
  2524.4 99.3 %reduce-scatter.92.cloned.1.call-done = bf16[1,96,3072]{2,1,0:T(8,128)(2,1)} async-done(((bf16[1,768,3072]{2,1,0:T(8,128)(2,1)}), bf16[1,96,3072]{2,1,0:T(8,128)(2,1)}) %reduce-scatter.92.cloned.1.call-update) | async-done | bytes 589840 | tf_op jit(solution)/shard_map/reduce_scatter | solution.py:279
  2626.1 96.8 %reduce-scatter.94.cloned.1.call-done = bf16[1,384,768]{2,1,0:T(8,128)(2,1)} async-done(((bf16[1,3072,768]{2,1,0:T(8,128)(2,1)}), bf16[1,384,768]{2,1,0:T(8,128)(2,1)}) %reduce-scatter.94.cloned.1.call-update) | async-done | bytes 589840 | tf_op jit(solution)/shard_map/reduce_scatter | solution.py:285
  2722.9 99.3 %reduce-scatter.96.cloned.1.call-done = bf16[1,384,768]{2,1,0:T(8,128)(2,1)} async-done(((bf16[1,3072,768]{2,1,0:T(8,128)(2,1)}), bf16[1,384,768]{2,1,0:T(8,128)(2,1)}) %reduce-scatter.96.cloned.1.call-update) | async-done | bytes 589840 | tf_op jit(solution)/shard_map/reduce_scatter | solution.py:285
  2822.2 99.1 %reduce-scatter.98.cloned.1.call-done = bf16[1,384,768]{2,1,0:T(8,128)(2,1)} async-done(((bf16[1,3072,768]{2,1,0:T(8,128)(2,1)}), bf16[1,384,768]{2,1,0:T(8,128)(2,1)}) %reduce-scatter.98.cloned.1.call-update) | async-done | bytes 589840 | tf_op jit(solution)/shard_map/reduce_scatter | solution.py:285
  2923.8 80.5 %reduce-scatter.76.cloned.1.call-done = bf16[1,96,2304]{2,1,0:T(8,128)(2,1)} async-done(((bf16[1,768,2304]{2,1,0:T(8,128)(2,1)}), bf16[1,96,2304]{2,1,0:T(8,128)(2,1)}) %reduce-scatter.76.cloned.1.call-update) | async-done | bytes 442384 | tf_op jit(solution)/shard_map/reduce_scatter | solution.py:349
  3004.3 82.6 %reduce-scatter.78.cloned.1.call-done = bf16[1,96,2304]{2,1,0:T(8,128)(2,1)} async-done(((bf16[1,768,2304]{2,1,0:T(8,128)(2,1)}), bf16[1,96,2304]{2,1,0:T(8,128)(2,1)}) %reduce-scatter.78.cloned.1.call-update) | async-done | bytes 442384 | tf_op jit(solution)/shard_map/reduce_scatter | solution.py:349
  3086.9 82.6 %reduce-scatter.80.cloned.1.call-done = bf16[1,96,2304]{2,1,0:T(8,128)(2,1)} async-done(((bf16[1,768,2304]{2,1,0:T(8,128)(2,1)}), bf16[1,96,2304]{2,1,0:T(8,128)(2,1)}) %reduce-scatter.80.cloned.1.call-update) | async-done | bytes 442384 | tf_op jit(solution)/shard_map/reduce_scatter | solution.py:349
  3174.4 59.9 %reduce-scatter.104.cloned.1.call-done = bf16[96,2]{1,0:T(8,128)(2,1)} async-done(((bf16[768,2]{1,0:T(8,128)(2,1)}), bf16[96,2]{1,0:T(8,128)(2,1)}) %reduce-scatter.104.cloned.1.call-update) | async-done | bytes 400
  3235.2 62.8 %reduce-scatter.110.cloned.1.call-done = bf16[96,2]{1,0:T(8,128)(2,1)} async-done(((bf16[768,2]{1,0:T(8,128)(2,1)}), bf16[96,2]{1,0:T(8,128)(2,1)}) %reduce-scatter.110.cloned.1.call-update) | async-done | bytes 400
  3298.8 62.8 %reduce-scatter.116.cloned.1.call-done = bf16[96,2]{1,0:T(8,128)(2,1)} async-done(((bf16[768,2]{1,0:T(8,128)(2,1)}), bf16[96,2]{1,0:T(8,128)(2,1)}) %reduce-scatter.116.cloned.1.call-update) | async-done | bytes 400
  (1086 shorter events, 1277.7 us)
Async XLA Ops:
  128.5 312.0 %all-gather.35.cloned.1.call-start = ((), (), s32[]{:S(2)}) async-start(), calls=%async_computation.39 | async-start | bytes 1769472 | tf_op jit(solution)/shard_map/all_gather | solution.py:205
  532.2 264.4 %all-gather.49.cloned.1.call-start = ((), (), s32[]{:S(2)}) async-start(), calls=%async_computation.61 | async-start | bytes 1769472 | tf_op jit(solution)/shard_map/all_gather | solution.py:303
  538.5 334.5 %reduce-scatter.70.cloned.1.call-start = ((), (), s32[]{:S(2)}) async-start(), calls=%async_computation.43 | async-start | bytes 3538944 | tf_op jit(solution)/shard_map/reduce_scatter | solution.py:318
  770.6 269.3 %reduce-scatter.72.cloned.1.call-start = ((), (), s32[]{:S(2)}) async-start(), calls=%async_computation.44 | async-start | bytes 3538944 | tf_op jit(solution)/shard_map/reduce_scatter | solution.py:318
  1099.7 324.1 %reduce-scatter.100.cloned.1.call-start = ((), (), s32[]{:S(2)}) async-start(), calls=%async_computation.64 | async-start | bytes 221184
  1101.0 386.4 %reduce-scatter.106.cloned.1.call-start = ((), (), s32[]{:S(2)}) async-start(), calls=%async_computation.67 | async-start | bytes 221184
  1102.3 448.8 %reduce-scatter.112.cloned.1.call-start = ((), (), s32[]{:S(2)}) async-start(), calls=%async_computation.70 | async-start | bytes 221184
  1103.6 511.2 %reduce-scatter.120.cloned.1.call-start = ((), (), s32[]{:S(2)}) async-start(), calls=%async_computation.74 | async-start | bytes 221184
  1104.5 573.8 %reduce-scatter.132.cloned.1.call-start = ((), (), s32[]{:S(2)}) async-start(), calls=%async_computation.80 | async-start | bytes 221184
  1105.5 638.6 %reduce-scatter.126.cloned.1.call-start = ((), (), s32[]{:S(2)}) async-start(), calls=%async_computation.77 | async-start | bytes 884736
  1107.0 700.4 %reduce-scatter.102.cloned.1.call-start = ((), (), s32[]{:S(2)}) async-start(), calls=%async_computation.65 | async-start | bytes 221184
  1108.3 762.4 %reduce-scatter.108.cloned.1.call-start = ((), (), s32[]{:S(2)}) async-start(), calls=%async_computation.68 | async-start | bytes 221184
  1109.6 824.5 %reduce-scatter.114.cloned.1.call-start = ((), (), s32[]{:S(2)}) async-start(), calls=%async_computation.71 | async-start | bytes 221184
  1110.9 886.6 %reduce-scatter.122.cloned.1.call-start = ((), (), s32[]{:S(2)}) async-start(), calls=%async_computation.75 | async-start | bytes 221184
  1111.8 948.9 %reduce-scatter.134.cloned.1.call-start = ((), (), s32[]{:S(2)}) async-start(), calls=%async_computation.81 | async-start | bytes 221184
  1112.7 1013.5 %reduce-scatter.128.cloned.1.call-start = ((), (), s32[]{:S(2)}) async-start(), calls=%async_computation.78 | async-start | bytes 884736
  1114.2 1078.8 %reduce-scatter.82.cloned.1.call-start = ((), (), s32[]{:S(2)}) async-start(), calls=%async_computation.49 | async-start | bytes 1327104 | tf_op jit(solution)/shard_map/reduce_scatter | solution.py:355
  1115.8 1143.9 %reduce-scatter.84.cloned.1.call-start = ((), (), s32[]{:S(2)}) async-start(), calls=%async_computation.50 | async-start | bytes 1327104 | tf_op jit(solution)/shard_map/reduce_scatter | solution.py:355
  1117.5 1209.5 %reduce-scatter.86.cloned.1.call-start = ((), (), s32[]{:S(2)}) async-start(), calls=%async_computation.51 | async-start | bytes 1327104 | tf_op jit(solution)/shard_map/reduce_scatter | solution.py:355
  1119.1 1306.3 %reduce-scatter.88.cloned.1.call-start = ((), (), s32[]{:S(2)}) async-start(), calls=%async_computation.52 | async-start | bytes 5308416 | tf_op jit(solution)/shard_map/reduce_scatter | solution.py:279
  1123.8 1400.5 %reduce-scatter.90.cloned.1.call-start = ((), (), s32[]{:S(2)}) async-start(), calls=%async_computation.53 | async-start | bytes 5308416 | tf_op jit(solution)/shard_map/reduce_scatter | solution.py:279
  1128.6 1495.0 %reduce-scatter.92.cloned.1.call-start = ((), (), s32[]{:S(2)}) async-start(), calls=%async_computation.54 | async-start | bytes 5308416 | tf_op jit(solution)/shard_map/reduce_scatter | solution.py:279
  1133.3 1589.6 %reduce-scatter.94.cloned.1.call-start = ((), (), s32[]{:S(2)}) async-start(), calls=%async_computation.55 | async-start | bytes 5308416 | tf_op jit(solution)/shard_map/reduce_scatter | solution.py:285
  1140.9 1681.3 %reduce-scatter.96.cloned.1.call-start = ((), (), s32[]{:S(2)}) async-start(), calls=%async_computation.56 | async-start | bytes 5308416 | tf_op jit(solution)/shard_map/reduce_scatter | solution.py:285
  1145.4 1775.9 %reduce-scatter.98.cloned.1.call-start = ((), (), s32[]{:S(2)}) async-start(), calls=%async_computation.57 | async-start | bytes 5308416 | tf_op jit(solution)/shard_map/reduce_scatter | solution.py:285
  1149.9 1854.4 %reduce-scatter.76.cloned.1.call-start = ((), (), s32[]{:S(2)}) async-start(), calls=%async_computation.46 | async-start | bytes 3981312 | tf_op jit(solution)/shard_map/reduce_scatter | solution.py:349
  1154.1 1932.8 %reduce-scatter.78.cloned.1.call-start = ((), (), s32[]{:S(2)}) async-start(), calls=%async_computation.47 | async-start | bytes 3981312 | tf_op jit(solution)/shard_map/reduce_scatter | solution.py:349
  1158.0 2011.5 %reduce-scatter.80.cloned.1.call-start = ((), (), s32[]{:S(2)}) async-start(), calls=%async_computation.48 | async-start | bytes 3981312 | tf_op jit(solution)/shard_map/reduce_scatter | solution.py:349
  1172.5 2061.8 %reduce-scatter.104.cloned.1.call-start = ((), (), s32[]{:S(2)}) async-start(), calls=%async_computation.66 | async-start | bytes 221184
  2335.3 962.7 %reduce-scatter.110.cloned.1.call-start = ((), (), s32[]{:S(2)}) async-start(), calls=%async_computation.69 | async-start | bytes 221184
  2337.5 1024.1 %reduce-scatter.116.cloned.1.call-start = ((), (), s32[]{:S(2)}) async-start(), calls=%async_computation.72 | async-start | bytes 221184
  2338.7 1046.7 %all-reduce.7.cloned.1.call-start = ((), (), s32[]{:S(2)}) async-start(), calls=%async_computation.82 | async-start | bytes 3538944 | tf_op jit(solution)/shard_map/psum | solution.py:472
  (246 other events, 11500.8 us)
Sparse Core Ops, SparseCore 0:
  10.2 75.7 all-gather.22
  224.2 78.6 all-gather.30
  304.9 78.0 all-gather.32
  800.0 72.9 reduce-scatter.69
  966.9 73.0 reduce-scatter.71
  1095.2 73.2 reduce-scatter.73
  1171.6 60.3 reduce-scatter.129
  1235.2 60.0 reduce-scatter.117
  1298.7 61.4 reduce-scatter.123
  1490.9 60.1 reduce-scatter.111
  1554.6 60.1 reduce-scatter.119
  1682.5 61.5 reduce-scatter.125
  1810.6 60.0 reduce-scatter.107
  1873.9 60.1 reduce-scatter.113
  1937.4 60.1 reduce-scatter.121
  2000.6 60.0 reduce-scatter.133
  2064.6 61.5 reduce-scatter.127
  2130.0 63.0 reduce-scatter.81
  2196.6 63.0 reduce-scatter.83
  2263.9 63.0 reduce-scatter.85
  2331.1 94.2 reduce-scatter.87
  2429.3 95.0 reduce-scatter.89
  2528.5 95.1 reduce-scatter.91
  2627.7 95.1 reduce-scatter.93
  2727.0 95.1 reduce-scatter.95
  2826.2 95.1 reduce-scatter.97
  2925.4 78.8 reduce-scatter.75
  3008.3 78.6 reduce-scatter.77
  3090.8 78.6 reduce-scatter.79
  3173.6 60.7 reduce-scatter.103
  3237.7 60.1 reduce-scatter.109
  3301.4 60.1 reduce-scatter.115
  (18 shorter events, 820.4 us)
where the time goes:
time: 3410 us; the launch traced here: 3400 us
  waiting for transfers between devices  2720 us (80%)
  local copies, waits for them, and re-layouts  190 us (6%)
  matrix products  179 us (5%)
  blocking collectives  147 us (4%)
  other arithmetic  105 us (3%)
    unnamed x68, waiting for transfers between devices  1110 us
    reduce_scatter x3, waiting for transfers between devices, layer_backward(): lax.psum_scatter(proj_term[None].astype(jnp.bfloat16), 'shard', scatter_d...  295 us
    reduce_scatter x3, waiting for transfers between devices, layer_backward(): lax.psum_scatter(fc_term[None].astype(jnp.bfloat16), 'shard', scatter_dim...  285 us
    reduce_scatter x3, waiting for transfers between devices, layer_backward(): lax.psum_scatter(qkv_term[None].astype(jnp.bfloat16), 'shard', scatter_di...  246 us
    reduce_scatter x3, waiting for transfers between devices, layer_backward(): lax.psum_scatter(out_term[None].astype(jnp.bfloat16), 'shard', scatter_di...  199 us
    reduce_scatter x3, waiting for transfers between devices, layer_backward(): lax.psum_scatter(key_terms.astype(jnp.bfloat16), 'shard', scatter_dimensi...  140 us
    all_gather x3, waiting for transfers between devices, layer_backward(): lax.all_gather(value_local, 'shard', axis=0, tiled=True)  82.4 us
    all_gather x1, waiting for transfers between devices, on_device(): lax.all_gather(w_fc, 'shard', axis=1, tiled=True)  78.8 us
  transfers between devices with their start and end apart: 54, of which 50 were waited for; matrix products, arithmetic and copies ran while one was open for 11% of the time, Pallas kernels for 0%

commit v1 on v0

v1 whole, which is shorter than its diff:
```python
import math

import jax
import jax.numpy as jnp
import numpy as np
from jax import lax
from jax.sharding import PartitionSpec as P

HEADS = 12
HEAD = 64
EPSILON = 1e-05
SCALING = 0.125
FLOOR = -1e30
LOW = jnp.bfloat16
F32 = jnp.float32


def ring_order(count):
    return list(range(0, count, 2)) + list(range(count - 1, 0, -2))


def ring_pairs(count):
    order = ring_order(count)
    right = [(order[i], order[(i + 1) % count]) for i in range(count)]
    return right, [(b, a) for a, b in right]


def ring_gather(chunk, count):
    right, left = ring_pairs(count)
    got = {0: chunk}
    from_left = from_right = chunk
    cut = chunk.shape[0] // 32 * 16
    for step in range(1, count // 2 + 1):
        if step == count // 2:
            got[step] = jnp.concatenate(
                [
                    lax.ppermute(from_left[:cut], "shard", right),
                    lax.ppermute(from_right[cut:], "shard", left),
                ],
                axis=0,
            )
        else:
            from_left = lax.ppermute(from_left, "shard", right)
            from_right = lax.ppermute(from_right, "shard", left)
            got[count - step] = from_left
            got[step] = from_right
    return [got[k] for k in range(count)]


def ring_scatter(piece, rows, count):
    right, left = ring_pairs(count)
    cut = rows // 32 * 16
    half = count // 2
    far = piece(half)
    to_right = lax.ppermute(far[:cut], "shard", right)
    to_left = lax.ppermute(far[cut:], "shard", left)
    for distance in range(half - 1, 0, -1):
        first, second = piece(distance), piece(count - distance)
        if distance == half - 1:
            first = jnp.concatenate([add_low(first[:cut], to_right), first[cut:]], axis=0)
            second = jnp.concatenate([second[:cut], add_low(second[cut:], to_left)], axis=0)
        else:
            first = add_low(first, to_right)
            second = add_low(second, to_left)
        to_right = lax.ppermute(first, "shard", right)
        to_left = lax.ppermute(second, "shard", left)
    return piece(0).astype(F32) + to_right.astype(F32) + to_left.astype(F32)


def add_low(a, b):
    return (a.astype(F32) + b.astype(F32)).astype(LOW)


def swap(x, axis):
    return lax.ppermute(x, axis, [(0, 1), (1, 0)])


def normalize(values, gain_row, offset):
    average = jnp.mean(values, axis=-1, keepdims=True)
    centred = values - average
    variance = jnp.mean(centred * centred, axis=-1, keepdims=True)
    return centred * lax.rsqrt(variance + EPSILON) * gain_row + offset


def gelu_tanh(values):
    return jax.nn.gelu(values, approximate=True)


def dot(a, b):
    return jnp.dot(a, b, preferred_element_type=F32)


def dot_t(a, b):
    return jnp.einsum("tc,dc->td", a, b, preferred_element_type=F32)


def dot_rows(a, b):
    return jnp.einsum("ta,tb->ab", a, b, preferred_element_type=F32)


class Plan:
    def __init__(self, count, segment):
        self.count = count
        self.segment = segment
        self.splits = count // math.gcd(HEADS, count)
        self.units = HEADS * self.splits // count
        self.part = segment // self.splits
        self.first = [self.units * q // self.splits for q in range(count)]
        self.slots = max(
            (self.units * q + self.units - 1) // self.splits - self.first[q] + 1
            for q in range(count)
        )
        self.groups = [
            [r * count + h * (count // 2) + i for r in range(2) for i in range(count // 2)]
            for h in range(2)
        ]

    def exchange(self, blocks):
        return lax.all_to_all(
            blocks, ("replica", "shard"), 0, 0, tiled=True, axis_index_groups=self.groups
        )

    def pack_units(self, heads):
        parts = heads.reshape(self.splits, self.part, HEADS, HEAD)
        parts = parts.transpose(2, 0, 1, 3).reshape(
            self.count, self.units * self.part, HEAD
        )
        return self.fold(parts)

    def fold(self, parts):
        rows = parts.shape[1] // 2
        return jnp.concatenate([parts[:, :rows], parts[:, rows:]], axis=2)

    def unfold(self, folded):
        return jnp.concatenate([folded[..., :HEAD], folded[..., HEAD:]], axis=1)

    def unpack_units(self, folded):
        parts = self.unfold(folded).reshape(HEADS, self.splits, self.part, HEAD)
        return parts.transpose(1, 2, 0, 3).reshape(self.segment, HEADS * HEAD)

    def gather_units(self, folded):
        parts = self.unfold(folded).reshape(self.count, self.units, self.part, HEAD)
        return parts.transpose(1, 0, 2, 3).reshape(self.units, self.count * self.part, HEAD)

    def scatter_units(self, values):
        parts = values.reshape(self.units, self.count, self.part, HEAD).transpose(1, 0, 2, 3)
        return self.fold(parts.reshape(self.count, self.units * self.part, HEAD))

    def head_slots(self, rows):
        blocks = []
        for q in range(self.count):
            cols = []
            for slot in range(self.slots):
                head = min(self.first[q] + slot, HEADS - 1)
                cols.append(rows[:, head * HEAD : (head + 1) * HEAD])
            blocks.append(jnp.concatenate(cols, axis=1))
        return jnp.stack(blocks)

    def sum_slots(self, blocks):
        cols = []
        for head in range(HEADS):
            total = None
            for q in range(self.count):
                last = (self.units * (q + 1) - 1) // self.splits
                if self.first[q] <= head <= last:
                    slot = head - self.first[q]
                    term = blocks[q, :, slot * HEAD : (slot + 1) * HEAD].astype(F32)
                    total = term if total is None else total + term
            cols.append(total)
        return jnp.concatenate(cols, axis=1)


def widen(units, slot, slots):
    wide = jnp.concatenate([units] * slots, axis=2)
    lane_slot = jnp.arange(slots * HEAD, dtype=jnp.int32) // HEAD
    return jnp.where(lane_slot[None, None, :] == slot[:, None, None], wide, jnp.zeros_like(wide))


def narrow(wide, slot, slots):
    lane_slot = jnp.arange(slots * HEAD, dtype=jnp.int32) // HEAD
    wide = jnp.where(lane_slot[None, None, :] == slot[:, None, None], wide, jnp.zeros_like(wide))
    return sum(wide[:, :, s * HEAD : (s + 1) * HEAD] for s in range(slots))


def attend_forward(queries, keys, values, query_pos, key_pos):
    scores = jnp.einsum("uid,jd->uij", queries, keys, preferred_element_type=F32) * SCALING
    visible = key_pos[None, None, :] <= query_pos[:, :, None]
    scores = jnp.where(visible, scores, FLOOR)
    highest = jnp.max(scores, axis=-1, keepdims=True)
    terms = jnp.exp(scores - highest)
    total = jnp.sum(terms, axis=-1, keepdims=True)
    weights = (terms / total).astype(LOW)
    attended = jnp.einsum("uij,jd->uid", weights, values, preferred_element_type=F32)
    return attended, highest + jnp.log(total)


def attend_backward(queries, keys, values, query_pos, key_pos, log_total, grad, row_dots):
    scores = jnp.einsum("uid,jd->uij", queries, keys, preferred_element_type=F32) * SCALING
    visible = key_pos[None, None, :] <= query_pos[:, :, None]
    weights = jnp.where(visible, jnp.exp(scores - log_total), 0.0)
    grad_weights = jnp.einsum("uid,jd->uij", grad, values, preferred_element_type=F32)
    grad_scores = (weights * (grad_weights - row_dots)).astype(LOW)
    grad_queries = (
        jnp.einsum("uij,jd->uid", grad_scores, keys, preferred_element_type=F32) * SCALING
    )
    grad_keys = (
        jnp.einsum("uij,uid->jd", grad_scores, queries, preferred_element_type=F32) * SCALING
    )
    grad_values = jnp.einsum("uij,uid->jd", weights.astype(LOW), grad, preferred_element_type=F32)
    return grad_queries, grad_keys, grad_values


def layer_forward(inputs, weights, plan, place):
    normed = normalize(inputs, weights["gains"][0], weights["offsets"][0]).astype(LOW)
    queries = (dot(normed, weights["q"]) + weights["q_bias"]).astype(LOW)
    keys = dot(normed, weights["k"]).astype(LOW)
    values = (dot(normed, weights["v"]) + weights["v_bias"]).astype(LOW)
    segment = inputs.shape[0]
    width = plan.slots * HEAD
    sent = jnp.concatenate(
        [
            plan.head_slots(keys),
            plan.head_slots(values),
            plan.pack_units(queries.reshape(segment, HEADS, HEAD)).reshape(
                plan.count, -1, width
            ),
        ],
        axis=1,
    )
    arrived = plan.exchange(sent)
    length = plan.count * segment
    all_keys = arrived[:, :segment].reshape(length, width)
    all_values = arrived[:, segment : 2 * segment].reshape(length, width)
    units = plan.gather_units(arrived[:, 2 * segment :].reshape(plan.count, -1, 2 * HEAD))
    units = widen(units, place["slot"], plan.slots)
    attended, log_total = attend_forward(
        units, all_keys, all_values, place["query_pos"], place["key_pos"]
    )
    attended = narrow(attended, place["slot"], plan.slots)
    returned = plan.exchange(plan.scatter_units(attended.astype(LOW)))
    attended_low = plan.unpack_units(returned)
    middle = inputs + dot(attended_low, weights["o"]) + weights["out_bias"]
    normed_two = normalize(middle, weights["gains"][1], weights["offsets"][1]).astype(LOW)
    hidden = dot(normed_two, weights["fc"]) + weights["fc_bias"]
    active = gelu_tanh(hidden).astype(LOW)
    output = middle + dot(active, weights["proj"]) + weights["proj_bias"]
    saved = dict(
        inputs=inputs, normed=normed, units=units, keys=all_keys, values=all_values,
        attended=attended, log_total=log_total, attended_low=attended_low, middle=middle,
        normed_two=normed_two, hidden=hidden, active=active,
    )
    return output, saved


def layer_backward(arriving, saved, weights, plan, place):
    segment, model_width = arriving.shape
    grad_branch = arriving.astype(LOW)
    grad_active = dot_t(grad_branch, weights["proj"])
    grad_hidden = jax.vjp(gelu_tanh, saved["hidden"])[1](grad_active)[0].astype(LOW)
    grad_normed_two = dot_t(grad_hidden, weights["fc"])
    grad_middle_norm, gain_two, offset_two = jax.vjp(
        normalize, saved["middle"], weights["gains"][1], weights["offsets"][1]
    )[1](grad_normed_two)
    grads = dict(
        proj=dot_rows(saved["active"], grad_branch),
        proj_bias=jnp.sum(grad_branch.astype(F32), axis=0),
        fc=dot_rows(saved["normed_two"], grad_hidden),
        fc_bias=jnp.sum(grad_hidden.astype(F32), axis=0),
    )
    grad_middle = arriving + grad_middle_norm
    grad_out = grad_middle.astype(LOW)
    grad_attended = dot_t(grad_out, weights["o"]).astype(LOW)
    arrived = plan.exchange(plan.pack_units(grad_attended.reshape(segment, HEADS, HEAD)))
    grad_units = plan.gather_units(arrived)
    row_dots = jnp.sum(grad_units.astype(F32) * saved["attended"], axis=-1, keepdims=True)
    grad_queries, grad_keys, grad_values = attend_backward(
        saved["units"], saved["keys"], saved["values"], place["query_pos"], place["key_pos"],
        saved["log_total"], widen(grad_units, place["slot"], plan.slots), row_dots,
    )
    grad_queries = narrow(grad_queries, place["slot"], plan.slots).astype(LOW)
    width = plan.slots * HEAD
    sent = jnp.concatenate(
        [
            grad_keys.astype(LOW).reshape(plan.count, segment, width),
            grad_values.astype(LOW).reshape(plan.count, segment, width),
            plan.scatter_units(grad_queries).reshape(plan.count, -1, width),
        ],
        axis=1,
    )
    returned = plan.exchange(sent)
    grad_k = plan.sum_slots(returned[:, :segment]).astype(LOW)
    grad_v = plan.sum_slots(returned[:, segment : 2 * segment]).astype(LOW)
    grad_q = plan.unpack_units(returned[:, 2 * segment :].reshape(plan.count, -1, 2 * HEAD))
    grad_normed = (
        dot_t(grad_q, weights["q"]) + dot_t(grad_k, weights["k"]) + dot_t(grad_v, weights["v"])
    )
    grad_input_norm, gain_one, offset_one = jax.vjp(
        normalize, saved["inputs"], weights["gains"][0], weights["offsets"][0]
    )[1](grad_normed)
    grads.update(
        gains=jnp.stack([gain_one, gain_two]),
        offsets=jnp.stack([offset_one, offset_two]),
        q=dot_rows(saved["normed"], grad_q),
        k=dot_rows(saved["normed"], grad_k),
        v=dot_rows(saved["normed"], grad_v),
        qv_bias=jnp.stack([jnp.sum(grad_q.astype(F32), axis=0), jnp.sum(grad_v.astype(F32), axis=0)]),
        o=dot_rows(saved["attended_low"], grad_out),
        out_bias=jnp.sum(grad_out.astype(F32), axis=0),
    )
    return grad_middle + grad_input_norm, grads


def on_device(
    tokens, cotangent, group_order, norm_gains, norm_biases, w_qkv, qv_bias, w_out, out_bias,
    w_fc, fc_bias, w_proj, proj_bias,
):
    count = lax.axis_size("shard")
    section = lax.axis_index("section")
    replica = lax.axis_index("replica")
    shard = lax.axis_index("shard")
    segment, model_width = tokens.shape[1], tokens.shape[2]
    rows = w_qkv.shape[1]
    half = count // 2
    plan = Plan(count, segment)
    order = ring_order(count)
    position_of = np.argsort(np.array(order))
    position = jnp.asarray(position_of, jnp.int32)[shard]
    order_table = jnp.asarray(order, jnp.int32)

    def owner(offset):
        return order_table[lax.rem(position + offset, count)]

    home = shard // half
    keeps = home == replica
    crossing = []
    for s in range(half):
        crossing += [(count + s, s + half), (s + half, count + s)]

    def reshard(x):
        moved = lax.ppermute(x, ("replica", "shard"), crossing)
        return jnp.where(keeps, x, moved)

    def pick(x):
        return lax.dynamic_index_in_dim(x, section, 0, keepdims=False)

    order_row = pick(group_order).astype(LOW)
    order_row = jnp.broadcast_to(
        jnp.concatenate([order_row, jnp.zeros((model_width - count,), LOW)])[None], (16, model_width)
    )
    packed = reshard(jnp.concatenate([pick(tokens), order_row], axis=0))
    current = packed[:segment].astype(F32)
    blocks_at = packed[segment, :count].astype(jnp.int32)
    upstream = reshard(pick(cotangent))
    seat = replica * half + lax.rem(shard, half)
    key_pos = (
        blocks_at[:, None] * segment + jnp.arange(segment, dtype=jnp.int32)[None, :]
    )
    unit_ids = plan.units * seat + jnp.arange(plan.units, dtype=jnp.int32)
    unit_part = lax.rem(unit_ids, plan.splits)
    parts_pos = key_pos.reshape(count, plan.splits, plan.part)
    query_pos = jnp.stack(
        [
            lax.dynamic_index_in_dim(parts_pos, unit_part[u], 1, keepdims=False).reshape(-1)
            for u in range(plan.units)
        ]
    )
    place = dict(
        slot=unit_ids // plan.splits - (plan.units * seat) // plan.splits,
        query_pos=query_pos,
        key_pos=key_pos.reshape(-1),
    )

    small = jnp.concatenate(
        [
            norm_gains[0], norm_biases[0], qv_bias[0], out_bias, fc_bias.reshape(4, rows), proj_bias,
        ],
        axis=0,
    ).reshape(-1)
    small_rows = -(-small.shape[0] // (16 * model_width)) * 16
    small = jnp.concatenate(
        [small, jnp.zeros((small_rows * model_width - small.shape[0],), LOW)]
    ).reshape(small_rows, model_width)
    qkv = w_qkv[0]
    attn_sets = (
        jnp.concatenate([qkv[:, :model_width], qkv[:, model_width : 2 * model_width], small], axis=0),
        jnp.concatenate([qkv[:, 2 * model_width :], w_out[0], small], axis=0),
    )
    fc_blocks = w_fc[0].reshape(rows, 4, model_width).transpose(1, 0, 2).reshape(4 * rows, model_width)
    ffn_sets = (fc_blocks, w_proj[0])

    def gathered(sets):
        own = jnp.where(replica == 0, sets[0], sets[1])
        other_layer = swap(own, "section")
        layers = []
        for layer in range(2):
            chunk = jnp.where(section == layer, own, other_layer)
            chunks = ring_gather(chunk, count)
            buffer = jnp.zeros((2, count) + chunk.shape, LOW)
            for offset in range(count):
                twin = swap(chunks[offset], "replica")
                at = owner(offset)
                buffer = lax.dynamic_update_slice(buffer, chunks[offset][None, None], (replica, at, 0, 0))
                buffer = lax.dynamic_update_slice(buffer, twin[None, None], (1 - replica, at, 0, 0))
            layers.append(buffer)
        return layers

    attn = gathered(attn_sets)
    ffn = gathered(ffn_sets)

    def block(buffer, which, at):
        return buffer[which, :, at * rows : (at + 1) * rows].reshape(count * rows, model_width)

    def unpacked(layer):
        a, f = attn[layer], ffn[layer]
        vec = a[0, :, 2 * rows :].reshape(count, -1)[:, : 12 * rows].reshape(count, 12, rows).astype(F32)

        def row(i):
            return vec[:, i].reshape(-1)

        return dict(
            q=block(a, 0, 0), k=block(a, 0, 1), v=block(a, 1, 0), o=block(a, 1, 1),
            fc=jnp.concatenate([block(f, 0, i) for i in range(4)], axis=1),
            proj=f[1].reshape(count * 4 * rows, model_width),
            gains=(row(0), row(1)), offsets=(row(2), row(3)), q_bias=row(4), v_bias=row(5),
            out_bias=row(6), fc_bias=vec[:, 7:11].reshape(-1), proj_bias=row(11),
        )

    weights = [unpacked(0), unpacked(1)]
    outputs, states = [], []
    for layer in range(2):
        output, saved = layer_forward(current, weights[layer], plan, place)
        outputs.append(output.astype(LOW))
        states.append(saved)
        current = outputs[-1].astype(F32)
    grad_inputs, totals = [None, None], [None, None]
    arriving = upstream.astype(F32)

    def pieces(attn_rows, layer_grads, which):
        pass

    def blocks_of(grad, cols):
        return grad.astype(LOW).reshape(count, -1, cols)

    def scattered(sets):
        own = jnp.where(replica == 0, sets[0], sets[1])
        other = jnp.where(replica == 0, sets[1], sets[0])
        paired = add_low(own, swap(other, "replica"))
        return ring_scatter(
            lambda k: lax.dynamic_index_in_dim(paired, owner(k), 0, keepdims=False),
            paired.shape[1], count,
        )

    scattered_attn, scattered_ffn = [None, None], [None, None]
    for layer in (1, 0):
        grad_input, grads = layer_backward(arriving, states[layer], weights[layer], plan, place)
        grad_inputs[layer] = grad_input
        arriving = grad_input.astype(LOW).astype(F32)
        vec = jnp.concatenate(
            [
                grads["gains"], grads["offsets"], grads["qv_bias"], grads["out_bias"][None],
            ], axis=0,
        ).reshape(7, count, rows).transpose(1, 0, 2)
        vec = jnp.concatenate(
            [vec, grads["fc_bias"].reshape(count, 4, rows), grads["proj_bias"].reshape(count, 1, rows)],
            axis=1,
        ).astype(LOW).reshape(count, 12 * rows)
        vec = jnp.concatenate(
            [vec, jnp.zeros((count, small_rows * model_width - 12 * rows), LOW)], axis=1
        ).reshape(count, small_rows, model_width)
        scattered_ffn[layer] = scattered(
            (
                jnp.concatenate(
                    [blocks_of(grads["fc"][:, i * model_width : (i + 1) * model_width], model_width) for i in range(4)],
                    axis=1,
                ),
                blocks_of(grads["proj"], model_width),
            )
        )
        scattered_attn[layer] = scattered(
            (
                jnp.concatenate([blocks_of(grads["q"], model_width), blocks_of(grads["k"], model_width), vec], axis=1),
                jnp.concatenate([blocks_of(grads["v"], model_width), blocks_of(grads["o"], model_width), vec], axis=1),
            )
        )

    def finished(parts):
        own = jnp.where(section == 0, parts[0], parts[1])
        other = jnp.where(section == 0, parts[1], parts[0]).astype(LOW)
        total = (own + swap(other, "section").astype(F32)).astype(LOW)
        twin = swap(total, "replica")
        return (
            jnp.where(replica == 0, total, twin).astype(F32),
            jnp.where(replica == 0, twin, total).astype(F32),
        )

    ffn_total = finished(scattered_ffn)
    attn_total = finished(scattered_attn)
    fc_grad = ffn_total[0].reshape(4, rows, model_width).transpose(1, 0, 2).reshape(rows, 4 * model_width)
    proj_grad = ffn_total[1]
    qkv_grad = jnp.concatenate(
        [attn_total[0][:rows], attn_total[0][rows : 2 * rows], attn_total[1][:rows]], axis=1
    )
    out_grad = attn_total[1][rows : 2 * rows]
    vec = attn_total[0][2 * rows :].reshape(-1)[: 12 * rows].reshape(12, rows)

    def by_owner(per_layer):
        low = [reshard(v.astype(LOW)) for v in per_layer]
        own = jnp.where(section == 0, low[0], low[1])
        other = jnp.where(section == 0, low[1], low[0])
        got = swap(other, "section")
        return jnp.stack([jnp.where(section == 0, own, got), jnp.where(section == 0, got, own)])[None]

    acts = by_owner(outputs)
    in_grads = by_owner(grad_inputs).astype(F32)
    return (
        acts,
        in_grads,
        vec[0:2][None],
        vec[2:4][None],
        qkv_grad[None],
        vec[4:6][None],
        out_grad[None],
        vec[6][None],
        fc_grad[None],
        vec[7:11].reshape(1, 4 * rows),
        proj_grad[None],
        vec[11][None],
    )


def solution(mesh):
    in_specs = (
        P("replica", "shard", None),
        P("replica", "shard", None),
        P("replica", None),
        P("section", None, "shard"),
        P("section", None, "shard"),
        P("section", "shard", None),
        P("section", None, "shard"),
        P("section", "shard", None),
        P("section", "shard"),
        P("section", "shard", None),
        P("section", "shard"),
        P("section", "shard", None),
        P("section", "shard"),
    )
    out_specs = (
        P("section", "replica", "shard", None),
        P("section", "replica", "shard", None),
        P("section", None, "shard"),
        P("section", None, "shard"),
        P("section", "shard", None),
        P("section", None, "shard"),
        P("section", "shard", None),
        P("section", "shard"),
        P("section", "shard", None),
        P("section", "shard"),
        P("section", "shard", None),
        P("section", "shard"),
    )
    return jax.shard_map(
        on_device, mesh=mesh, in_specs=in_specs, out_specs=out_specs, check_vma=False
    )
```

time: 3410 us -> 887 us (0.26)
  waiting for transfers between devices: 2720 us -> 214 us
  blocking collectives: 147 us -> 0 us
  starting transfers between devices: 12.6 us -> 147 us
  local copies, waits for them, and re-layouts: 190 us -> 276 us
  matrix products: 179 us -> 112 us
    reduce_scatter x15 -> x0, waiting for transfers between devices: 1160 us -> none  [the longest x3 295 us: layer_backward(): lax.psum_scatter(proj_term[None].astype(jnp.bfloat16), 'shard', scatter_d...]
    unnamed x68 -> x0, waiting for transfers between devices: 1110 us -> none
    all_gather x16 -> x0, waiting for transfers between devices: 413 us -> none  [the longest x3 82.4 us: layer_backward(): lax.all_gather(value_local, 'shard', axis=0, tiled=True)]
    ppermute x4 -> x114, waiting for transfers between devices: 19.7 us -> 211 us  [the longest x12 58.6 us: ring_scatter(): to_right = lax.ppermute(first, 'shard', right)]
    all_gather x4 -> x0, blocking collectives: 124 us -> none  [the longest x1 34 us: on_device(): lax.all_gather(norm_biases, 'shard', axis=2, tiled=True)]
    ppermute x4 -> x114, starting transfers between devices: 9.32 us -> 110 us  [the longest x44 23.2 us: swap(): return lax.ppermute(x, axis, [(0, 1), (1, 0)])]
    dot_general x78 -> x48, matrix products: 179 us -> 112 us  [the longest x12 30 us: dot_rows(): return jnp.einsum('ta,tb->ab', a, b, preferred_element_type=F32)]
    dynamic_update_slice x12 -> x61, local copies, waits for them, and re-layouts: 11.8 us -> 77 us  [the longest x32 42.4 us: gathered(): lax.dynamic_update_slice(buffer, twin[None, None], (1 - replica, at, 0, 0))]
  transfers between devices with their start and end apart: 54 -> 122, of which waited for: 50 -> 45; matrix products, arithmetic and copies ran while one was open for 11% -> 50% of each run, Pallas kernels for 0% -> 0%
where the time goes in v1:
time: 887 us; the launch traced here: 872 us
  local copies, waits for them, and re-layouts  276 us (31%)
  waiting for transfers between devices  214 us (24%)
  starting transfers between devices  147 us (17%)
  matrix products  112 us (13%)
  other arithmetic  89.9 us (10%)
  between operations  32.5 us (4%)
    unnamed x428, local copies, waits for them, and re-layouts  68.5 us
    ppermute x12, waiting for transfers between devices, ring_scatter(): to_right = lax.ppermute(first, 'shard', right)  58.6 us
    ppermute x12, waiting for transfers between devices, ring_gather(): from_left = lax.ppermute(from_left, 'shard', right)  42.9 us
    dynamic_update_slice x32, local copies, waits for them, and re-layouts, gathered(): lax.dynamic_update_slice(buffer, twin[None, None], (1 - replica, at, 0, 0))  42.4 us
    all_to_all x8, starting transfers between devices, exchange(): lax.all_to_all(blocks, ('replica', 'shard'), 0, 0, tiled=True, axis_index...  36.9 us
    dynamic_update_slice x29, local copies, waits for them, and re-layouts, gathered(): lax.dynamic_update_slice(buffer, chunks[offset][None, None], (replica, at...  34.6 us
    dot_general x12, matrix products, dot_rows(): return jnp.einsum('ta,tb->ab', a, b, preferred_element_type=F32)  30 us
    ppermute x12, waiting for transfers between devices, ring_gather(): from_right = lax.ppermute(from_right, 'shard', left)  29.4 us
  transfers between devices with their start and end apart: 122, of which 45 were waited for; matrix products, arithmetic and copies ran while one was open for 50% of the time, Pallas kernels for 0%

profile of v1, /device:TPU:0, one launch (start us, length us, event | category | flops | bytes accessed | tf_op | source)
XLA Modules:
  0.0 871.9 jit_solution(17760006586220767938)
XLA Ops:
  46.3 6.0 collective-permute-start.36
  79.9 6.1 collective-permute-done.5
  90.3 8.4 collective-permute-done.20
  102.5 8.5 collective-permute-done.53
  127.6 5.3 collective-permute-done.11
  136.7 12.0 %collective-permute-done.46 = bf16[96,768]{1,0:T(8,128)(2,1)S(1)} collective-permute-done((bf16[96,768]{1,0:T(8,128)(2,1)S(1)}, bf16[96,768]{1,0:T(8,128)(2,1)S(1)}, u32[]{:S(2)}, u32[]{:S(2)}) %collective-permute-start.46) | collective-permute-done | bytes 147488 | tf_op jit(solution)/shard_map/ppermute | solution.py:37
  169.0 12.4 %dynamic_update_slice.207 = bf16[2,8,208,768]{3,1,2,0:T(8,128)(2,1)} dynamic-update-slice(bf16[2,8,208,768]{3,1,2,0:T(8,128)(2,1)} %copy.281, bf16[1,1,208,768]{3,1,2,0:T(2,128)(2,1)S(1)} %copy.282, s32[]{:T(128)S(6)} %select_n.556, s32[]{:T(128)S(6)} %select_n.570, s32[]{:T(128)} %constant.223.clone.1, s32[]{:T(128)} %constant.223.clone.1) | dynamic-update-slice | bytes 638980 | tf_op jit(solution)/shard_map/dynamic_update_slice | solution.py:403
  225.5 11.0 %collective-permute-done.60 = bf16[384,768]{1,0:T(8,128)(2,1)} collective-permute-done((bf16[384,768]{1,0:T(8,128)(2,1)}, bf16[384,768]{1,0:T(8,128)(2,1)}, u32[]{:S(2)}, u32[]{:S(2)}) %collective-permute-start.60) | collective-permute-done | bytes 589856 | tf_op jit(solution)/shard_map/ppermute | solution.py:43
  246.3 10.5 %collective-permute-done.28 = bf16[384,768]{1,0:T(8,128)(2,1)} collective-permute-done((bf16[384,768]{1,0:T(8,128)(2,1)}, bf16[384,768]{1,0:T(8,128)(2,1)}, u32[]{:S(2)}, u32[]{:S(2)}) %collective-permute-start.28) | collective-permute-done | bytes 589856 | tf_op jit(solution)/shard_map/ppermute | solution.py:43
  259.3 10.2 %collective-permute-done.61 = bf16[384,768]{1,0:T(8,128)(2,1)} collective-permute-done((bf16[384,768]{1,0:T(8,128)(2,1)}, bf16[384,768]{1,0:T(8,128)(2,1)}, u32[]{:S(2)}, u32[]{:S(2)}) %collective-permute-start.61) | collective-permute-done | bytes 589856 | tf_op jit(solution)/shard_map/ppermute | solution.py:43
  325.9 5.2 slice.1151
  404.0 4.8 slice.1187
  435.0 5.6 all-to-all-start.4
  454.6 5.5 fusion.43
  460.0 5.1 multiply_convert_fusion.1
  470.8 6.2 all-to-all-start.5
  484.1 6.9 broadcast_select_fusion
  571.1 4.9 fusion.201
  614.5 5.5 fusion.40
  620.0 5.1 multiply_convert_fusion
  637.2 6.7 broadcast_select_fusion.1
  688.4 5.3 collective-permute-done.85
  721.0 6.0 collective-permute-done.76
  746.2 10.3 %collective-permute-done.105 = bf16[384,768]{1,0:T(8,128)(2,1)S(1)} collective-permute-done((bf16[384,768]{1,0:T(8,128)(2,1)S(1)}, bf16[384,768]{1,0:T(8,128)(2,1)S(1)}, u32[]{:S(2)}, u32[]{:S(2)}) %collective-permute-start.105) | collective-permute-done | bytes 589856 | tf_op jit(solution)/shard_map/ppermute | solution.py:65
  760.7 8.5 collective-permute-done.96
  773.0 8.8 %collective-permute-done.106 = bf16[384,768]{1,0:T(8,128)(2,1)S(1)} collective-permute-done((bf16[384,768]{1,0:T(8,128)(2,1)S(1)}, bf16[384,768]{1,0:T(8,128)(2,1)S(1)}, u32[]{:S(2)}, u32[]{:S(2)}) %collective-permute-start.106) | collective-permute-done | bytes 589856 | tf_op jit(solution)/shard_map/ppermute | solution.py:65
  791.8 7.5 collective-permute-done.97
  801.1 5.5 collective-permute-start.107
  812.3 7.8 collective-permute-done.101
  820.2 6.1 collective-permute-start.98
  836.1 9.4 %collective-permute-done.102 = bf16[384,768]{1,0:T(8,128)(2,1)} collective-permute-done((bf16[384,768]{1,0:T(8,128)(2,1)}, bf16[384,768]{1,0:T(8,128)(2,1)}, u32[]{:S(2)}, u32[]{:S(2)}) %collective-permute-start.102) | collective-permute-done | bytes 589856 | tf_op jit(solution)/shard_map/ppermute | solution.py:66
  850.9 13.0 %collective-permute-done.112 = bf16[384,768]{1,0:T(8,128)(2,1)} collective-permute-done((bf16[384,768]{1,0:T(8,128)(2,1)}, bf16[384,768]{1,0:T(8,128)(2,1)}, u32[]{:S(2)}, u32[]{:S(2)}) %collective-permute-start.112) | collective-permute-done | bytes 589856 | tf_op jit(solution)/shard_map/ppermute | solution.py:75
  (1089 shorter events, 599.3 us)
Async XLA Ops:
  5.3 40.5 %collective-permute-start.1 = (bf16[208,768]{1,0:T(8,128)(2,1)S(1)}, bf16[208,768]{1,0:T(8,128)(2,1)S(1)}, u32[]{:S(2)}, u32[]{:S(2)}) collective-permute-start(bf16[208,768]{1,0:T(8,128)(2,1)S(1)} %fusion.108), channel_id=1, source_target_pairs={{0,16},{16,0},{1,17},{17,1},{2,18},{18,2},{3,19},{19,3},{4,20},{20... | collective-permute-start | bytes 958472 | tf_op jit(solution)/shard_map/ppermute | solution.py:75
  9.1 35.3 %collective-permute-start = (bf16[144,768]{1,0:T(8,128)(2,1)S(1)}, bf16[144,768]{1,0:T(8,128)(2,1)S(1)}, u32[]{:S(2)}, u32[]{:S(2)}) collective-permute-start(bf16[144,768]{1,0:T(8,128)(2,1)S(1)} %pad_maximum_fusion.32), channel_id=1, source_target_pairs={{8,4},{4,8},{9,5},{5,9},{10,6},{6,10},{11,7},{7,11},{24,20},{20,24... | collective-permute-start | bytes 663560 | tf_op jit(solution)/shard_map/ppermute | solution.py:340
  11.7 43.1 %collective-permute-start.18 = (bf16[384,768]{1,0:T(8,128)(2,1)S(1)}, bf16[384,768]{1,0:T(8,128)(2,1)S(1)}, u32[]{:S(2)}, u32[]{:S(2)}) collective-permute-start(bf16[384,768]{1,0:T(8,128)(2,1)S(1)} %bitcast_select_fusion), channel_id=1, source_target_pairs={{0,16},{16,0},{1,17},{17,1},{2,18},{18,2},{3,19},{19,3},{4,20},{20... | collective-permute-start | bytes 1769480 | tf_op jit(solution)/shard_map/ppermute | solution.py:75
  11.9 31.8 %collective-permute-start.70 = (bf16[128,768]{1,0:T(8,128)(2,1)S(1)}, bf16[128,768]{1,0:T(8,128)(2,1)}, u32[]{:S(2)}, u32[]{:S(2)}) collective-permute-start(bf16[128,768]{1,0:T(8,128)(2,1)S(1)} %dynamic-slice_bitcast_fusion.12), channel_id=1, source_target_pairs={{8,4},{4,8},{9,5},{5,9},{10,6},{6,10},{11,7},{7,11},{24,20},{20,24... | collective-permute-start | bytes 589832 | tf_op jit(solution)/shard_map/ppermute | solution.py:340
  53.8 34.9 %collective-permute-start.43 = (bf16[208,768]{1,0:T(8,128)(2,1)S(1)}, bf16[208,768]{1,0:T(8,128)(2,1)}, u32[]{:S(2)}, u32[]{:S(2)}) collective-permute-start(bf16[208,768]{1,0:T(8,128)(2,1)S(1)} %get-tuple-element.71), channel_id=1, source_target_pairs={{0,2},{2,4},{4,6},{6,7},{7,5},{5,3},{3,1},{1,0},{8,10},{10,12},{12... | collective-permute-start | bytes 958472 | tf_op jit(solution)/shard_map/ppermute | solution.py:43
  86.0 121.1 %collective-permute-start.26 = (bf16[384,768]{1,0:T(8,128)(2,1)}, bf16[384,768]{1,0:T(8,128)(2,1)}, u32[]{:S(2)}, u32[]{:S(2)}) collective-permute-start(bf16[384,768]{1,0:T(8,128)(2,1)} %get-tuple-element.67), channel_id=1, source_target_pairs={{0,2},{2,4},{4,6},{6,7},{7,5},{5,3},{3,1},{1,0},{8,10},{10,12},{12... | collective-permute-start | bytes 1769480 | tf_op jit(solution)/shard_map/ppermute | solution.py:43
  126.1 81.3 %collective-permute-start.59 = (bf16[384,768]{1,0:T(8,128)(2,1)}, bf16[384,768]{1,0:T(8,128)(2,1)}, u32[]{:S(2)}, u32[]{:S(2)}) collective-permute-start(bf16[384,768]{1,0:T(8,128)(2,1)} %get-tuple-element.65), channel_id=1, source_target_pairs={{0,2},{2,4},{4,6},{6,7},{7,5},{5,3},{3,1},{1,0},{8,10},{10,12},{12... | collective-permute-start | bytes 1769480 | tf_op jit(solution)/shard_map/ppermute | solution.py:43
  151.5 38.2 %collective-permute-start.51 = (bf16[208,768]{1,0:T(8,128)(2,1)}, bf16[208,768]{1,0:T(8,128)(2,1)S(1)}, u32[]{:S(2)}, u32[]{:S(2)}) collective-permute-start(bf16[208,768]{1,0:T(8,128)(2,1)} %collective-permute-done.43), channel_id=1, source_target_pairs={{0,8},{8,0},{1,9},{9,1},{2,10},{10,2},{3,11},{11,3},{4,12},{12,4},... | collective-permute-start | bytes 958472 | tf_op jit(solution)/shard_map/ppermute | solution.py:75
  162.9 44.9 %collective-permute-start.22 = (bf16[384,768]{1,0:T(8,128)(2,1)}, bf16[384,768]{1,0:T(8,128)(2,1)}, u32[]{:S(2)}, u32[]{:S(2)}) collective-permute-start(bf16[384,768]{1,0:T(8,128)(2,1)} %collective-permute-done.20), channel_id=1, source_target_pairs={{2,0},{4,2},{6,4},{7,6},{5,7},{3,5},{1,3},{0,1},{10,8},{12,10},{14... | collective-permute-start | bytes 1769480 | tf_op jit(solution)/shard_map/ppermute | solution.py:44
  207.8 28.7 %collective-permute-start.60 = (bf16[384,768]{1,0:T(8,128)(2,1)}, bf16[384,768]{1,0:T(8,128)(2,1)}, u32[]{:S(2)}, u32[]{:S(2)}) collective-permute-start(bf16[384,768]{1,0:T(8,128)(2,1)} %collective-permute-done.59), channel_id=1, source_target_pairs={{0,2},{2,4},{4,6},{6,7},{7,5},{5,3},{3,1},{1,0},{8,10},{10,12},{12... | collective-permute-start | bytes 1769480 | tf_op jit(solution)/shard_map/ppermute | solution.py:43
  208.3 34.5 %collective-permute-start.23 = (bf16[384,768]{1,0:T(8,128)(2,1)}, bf16[384,768]{1,0:T(8,128)(2,1)}, u32[]{:S(2)}, u32[]{:S(2)}) collective-permute-start(bf16[384,768]{1,0:T(8,128)(2,1)} %collective-permute-done.22), channel_id=1, source_target_pairs={{0,8},{8,0},{1,9},{9,1},{2,10},{10,2},{3,11},{11,3},{4,12},{12,4},... | collective-permute-start | bytes 1769480 | tf_op jit(solution)/shard_map/ppermute | solution.py:75
  219.0 73.5 %all-to-all-start = ((bf16[8,352,128]{2,1,0:T(8,128)(2,1)}), bf16[8,352,128]{2,1,0:T(8,128)(2,1)}, u32[]{:S(2)}, u32[]{:S(2)}) async-start(bf16[8,352,128]{2,1,0:T(8,128)(2,1)} %maximum_maximum_fusion), calls=%async_computation | async-start | bytes 1441792 | tf_op jit(solution)/shard_map/all_to_all | solution.py:119
  223.2 34.6 %collective-permute-start.24 = (bf16[384,768]{1,0:T(8,128)(2,1)}, bf16[384,768]{1,0:T(8,128)(2,1)}, u32[]{:S(2)}, u32[]{:S(2)}) collective-permute-start(bf16[384,768]{1,0:T(8,128)(2,1)} %collective-permute-done.22), channel_id=1, source_target_pairs={{2,0},{4,2},{6,4},{7,6},{5,7},{3,5},{1,3},{0,1},{10,8},{12,10},{14... | collective-permute-start | bytes 1769480 | tf_op jit(solution)/shard_map/ppermute | solution.py:44
  225.1 48.9 %collective-permute-start.56 = (bf16[384,768]{1,0:T(8,128)(2,1)}, bf16[384,768]{1,0:T(8,128)(2,1)}, u32[]{:S(2)}, u32[]{:S(2)}) collective-permute-start(bf16[384,768]{1,0:T(8,128)(2,1)} %collective-permute-done.55), channel_id=1, source_target_pairs={{0,8},{8,0},{1,9},{9,1},{2,10},{10,2},{3,11},{11,3},{4,12},{12,4},... | collective-permute-start | bytes 1769480 | tf_op jit(solution)/shard_map/ppermute | solution.py:75
  225.1 31.8 %collective-permute-start.28 = (bf16[384,768]{1,0:T(8,128)(2,1)}, bf16[384,768]{1,0:T(8,128)(2,1)}, u32[]{:S(2)}, u32[]{:S(2)}) collective-permute-start(bf16[384,768]{1,0:T(8,128)(2,1)} %collective-permute-done.27), channel_id=1, source_target_pairs={{0,2},{2,4},{4,6},{6,7},{7,5},{5,3},{3,1},{1,0},{8,10},{10,12},{12... | collective-permute-start | bytes 1769480 | tf_op jit(solution)/shard_map/ppermute | solution.py:43
  236.5 33.0 %collective-permute-start.61 = (bf16[384,768]{1,0:T(8,128)(2,1)}, bf16[384,768]{1,0:T(8,128)(2,1)}, u32[]{:S(2)}, u32[]{:S(2)}) collective-permute-start(bf16[384,768]{1,0:T(8,128)(2,1)} %collective-permute-done.60), channel_id=1, source_target_pairs={{0,2},{2,4},{4,6},{6,7},{7,5},{5,3},{3,1},{1,0},{8,10},{10,12},{12... | collective-permute-start | bytes 1769480 | tf_op jit(solution)/shard_map/ppermute | solution.py:43
  242.8 33.6 %collective-permute-start.57 = (bf16[384,768]{1,0:T(8,128)(2,1)}, bf16[384,768]{1,0:T(8,128)(2,1)S(1)}, u32[]{:S(2)}, u32[]{:S(2)}) collective-permute-start(bf16[384,768]{1,0:T(8,128)(2,1)} %collective-permute-done.55), channel_id=1, source_target_pairs={{2,0},{4,2},{6,4},{7,6},{5,7},{3,5},{1,3},{0,1},{10,8},{12,10},{14... | collective-permute-start | bytes 1769480 | tf_op jit(solution)/shard_map/ppermute | solution.py:44
  256.8 67.1 %collective-permute-start.34 = (bf16[384,768]{1,0:T(8,128)(2,1)}, bf16[384,768]{1,0:T(8,128)(2,1)}, u32[]{:S(2)}, u32[]{:S(2)}) collective-permute-start(bf16[384,768]{1,0:T(8,128)(2,1)} %collective-permute-done.26), channel_id=1, source_target_pairs={{0,8},{8,0},{1,9},{9,1},{2,10},{10,2},{3,11},{11,3},{4,12},{12,4},... | collective-permute-start | bytes 1769480 | tf_op jit(solution)/shard_map/ppermute | solution.py:75
  281.6 88.5 %collective-permute-start.67 = (bf16[384,768]{1,0:T(8,128)(2,1)}, bf16[384,768]{1,0:T(8,128)(2,1)}, u32[]{:S(2)}, u32[]{:S(2)}) collective-permute-start(bf16[384,768]{1,0:T(8,128)(2,1)} %collective-permute-done.59), channel_id=1, source_target_pairs={{0,8},{8,0},{1,9},{9,1},{2,10},{10,2},{3,11},{11,3},{4,12},{12,4},... | collective-permute-start | bytes 1769480 | tf_op jit(solution)/shard_map/ppermute | solution.py:75
  281.7 38.0 %collective-permute-start.33 = (bf16[384,768]{1,0:T(8,128)(2,1)}, bf16[384,768]{1,0:T(8,128)(2,1)}, u32[]{:S(2)}, u32[]{:S(2)}) collective-permute-start(bf16[384,768]{1,0:T(8,128)(2,1)} %collective-permute-done.27), channel_id=1, source_target_pairs={{0,8},{8,0},{1,9},{9,1},{2,10},{10,2},{3,11},{11,3},{4,12},{12,4},... | collective-permute-start | bytes 1769480 | tf_op jit(solution)/shard_map/ppermute | solution.py:75
  311.4 54.9 %collective-permute-start.66 = (bf16[384,768]{1,0:T(8,128)(2,1)}, bf16[384,768]{1,0:T(8,128)(2,1)}, u32[]{:S(2)}, u32[]{:S(2)}) collective-permute-start(bf16[384,768]{1,0:T(8,128)(2,1)} %collective-permute-done.60), channel_id=1, source_target_pairs={{0,8},{8,0},{1,9},{9,1},{2,10},{10,2},{3,11},{11,3},{4,12},{12,4},... | collective-permute-start | bytes 1769480 | tf_op jit(solution)/shard_map/ppermute | solution.py:75
  315.7 46.7 %collective-permute-start.65 = (bf16[384,768]{1,0:T(8,128)(2,1)}, bf16[384,768]{1,0:T(8,128)(2,1)}, u32[]{:S(2)}, u32[]{:S(2)}) collective-permute-start(bf16[384,768]{1,0:T(8,128)(2,1)} %collective-permute-done.61), channel_id=1, source_target_pairs={{0,8},{8,0},{1,9},{9,1},{2,10},{10,2},{3,11},{11,3},{4,12},{12,4},... | collective-permute-start | bytes 1769480 | tf_op jit(solution)/shard_map/ppermute | solution.py:75
  408.8 160.1 %collective-permute-start.35 = (bf16[128,768]{1,0:T(8,128)(2,1)S(1)}, bf16[128,768]{1,0:T(8,128)(2,1)}, u32[]{:S(2)}, u32[]{:S(2)}) collective-permute-start(bf16[128,768]{1,0:T(8,128)(2,1)S(1)} %get-tuple-element.266), channel_id=1, source_target_pairs={{8,4},{4,8},{9,5},{5,9},{10,6},{6,10},{11,7},{7,11},{24,20},{20,24... | collective-permute-start | bytes 589832 | tf_op jit(solution)/shard_map/ppermute | solution.py:340
  445.3 123.6 %collective-permute-start.68 = (bf16[128,768]{1,0:T(8,128)(2,1)}, bf16[128,768]{1,0:T(8,128)(2,1)}, u32[]{:S(2)}, u32[]{:S(2)}) collective-permute-start(bf16[128,768]{1,0:T(8,128)(2,1)} %fusion.61), channel_id=1, source_target_pairs={{8,4},{4,8},{9,5},{5,9},{10,6},{6,10},{11,7},{7,11},{24,20},{20,24... | collective-permute-start | bytes 589832 | tf_op jit(solution)/shard_map/ppermute | solution.py:340
  491.0 203.5 %collective-permute-start.103 = (bf16[8,384,768]{2,1,0:T(8,128)(2,1)}, bf16[8,384,768]{2,1,0:T(8,128)(2,1)}, u32[]{:S(2)}, u32[]{:S(2)}) collective-permute-start(bf16[8,384,768]{2,1,0:T(8,128)(2,1)} %broadcast_select_fusion), channel_id=1, source_target_pairs={{0,8},{8,0},{1,9},{9,1},{2,10},{10,2},{3,11},{11,3},{4,12},{12,4},... | collective-permute-start | bytes 14155784 | tf_op jit(solution)/shard_map/ppermute | solution.py:75
  585.9 59.5 %collective-permute-start.69 = (bf16[128,768]{1,0:T(8,128)(2,1)}, bf16[128,768]{1,0:T(8,128)(2,1)}, u32[]{:S(2)}, u32[]{:S(2)}) collective-permute-start(bf16[128,768]{1,0:T(8,128)(2,1)} %get-tuple-element.233), channel_id=1, source_target_pairs={{0,16},{16,0},{1,17},{17,1},{2,18},{18,2},{3,19},{19,3},{4,20},{20... | collective-permute-start | bytes 589832 | tf_op jit(solution)/shard_map/ppermute | solution.py:75
  606.9 69.3 %collective-permute-start.83 = (bf16[8,208,768]{2,1,0:T(8,128)(2,1)}, bf16[8,208,768]{2,1,0:T(8,128)(2,1)}, u32[]{:S(2)}, u32[]{:S(2)}) collective-permute-start(bf16[8,208,768]{2,1,0:T(8,128)(2,1)} %broadcast_select_fusion.2), channel_id=1, source_target_pairs={{0,8},{8,0},{1,9},{9,1},{2,10},{10,2},{3,11},{11,3},{4,12},{12,4},... | collective-permute-start | bytes 7667720 | tf_op jit(solution)/shard_map/ppermute | solution.py:75
  643.9 83.8 %collective-permute-start.94 = (bf16[8,384,768]{2,1,0:T(8,128)(2,1)}, bf16[8,384,768]{2,1,0:T(8,128)(2,1)}, u32[]{:S(2)}, u32[]{:S(2)}) collective-permute-start(bf16[8,384,768]{2,1,0:T(8,128)(2,1)} %broadcast_select_fusion.1), channel_id=1, source_target_pairs={{0,8},{8,0},{1,9},{9,1},{2,10},{10,2},{3,11},{11,3},{4,12},{12,4},... | collective-permute-start | bytes 14155784 | tf_op jit(solution)/shard_map/ppermute | solution.py:75
  680.4 30.3 %collective-permute-start.74 = (bf16[8,208,768]{2,1,0:T(8,128)(2,1)S(1)}, bf16[8,208,768]{2,1,0:T(8,128)(2,1)S(1)}, u32[]{:S(2)}, u32[]{:S(2)}) collective-permute-start(bf16[8,208,768]{2,1,0:T(8,128)(2,1)S(1)} %broadcast_select_fusion.3), channel_id=1, source_target_pairs={{0,8},{8,0},{1,9},{9,1},{2,10},{10,2},{3,11},{11,3},{4,12},{12,4},... | collective-permute-start | bytes 7667720 | tf_op jit(solution)/shard_map/ppermute | solution.py:75
  704.4 29.8 %collective-permute-start.90 = (bf16[208,768]{1,0:T(8,128)(2,1)S(1)}, bf16[208,768]{1,0:T(8,128)(2,1)S(1)}, u32[]{:S(2)}, u32[]{:S(2)}) collective-permute-start(bf16[208,768]{1,0:T(8,128)(2,1)S(1)} %get-tuple-element.113), channel_id=1, source_target_pairs={{2,0},{4,2},{6,4},{7,6},{5,7},{3,5},{1,3},{0,1},{10,8},{12,10},{14... | collective-permute-start | bytes 958472 | tf_op jit(solution)/shard_map/ppermute | solution.py:66
  708.2 61.6 %collective-permute-start.87 = (bf16[208,768]{1,0:T(8,128)(2,1)S(1)}, bf16[208,768]{1,0:T(8,128)(2,1)S(1)}, u32[]{:S(2)}, u32[]{:S(2)}) collective-permute-start(bf16[208,768]{1,0:T(8,128)(2,1)S(1)} %get-tuple-element.112), channel_id=1, source_target_pairs={{0,2},{2,4},{4,6},{6,7},{7,5},{5,3},{3,1},{1,0},{8,10},{10,12},{12... | collective-permute-start | bytes 958472 | tf_op jit(solution)/shard_map/ppermute | solution.py:65
  737.5 33.9 %collective-permute-start.109 = (bf16[384,768]{1,0:T(8,128)(2,1)S(1)}, bf16[384,768]{1,0:T(8,128)(2,1)S(1)}, u32[]{:S(2)}, u32[]{:S(2)}) collective-permute-start(bf16[384,768]{1,0:T(8,128)(2,1)S(1)} %pad_maximum_fusion.15), channel_id=1, source_target_pairs={{2,0},{4,2},{6,4},{7,6},{5,7},{3,5},{1,3},{0,1},{10,8},{12,10},{14... | collective-permute-start | bytes 1769480 | tf_op jit(solution)/shard_map/ppermute | solution.py:66
  (233 other events, 3682.2 us)

commit v2 on v1

--- a/solution.py
+++ b/solution.py
@@ -1,9 +1,12 @@
 import math
+from types import SimpleNamespace as Bag
 
 import jax
 import jax.numpy as jnp
 import numpy as np
 from jax import lax
+from jax.experimental import pallas as pl
+from jax.experimental.pallas import tpu as pltpu
 from jax.sharding import PartitionSpec as P
 
 HEADS = 12
@@ -11,6 +14,7 @@
 EPSILON = 1e-05
 SCALING = 0.125
 FLOOR = -1e30
+SECTION, REPLICA, SHARD = "section", "replica", "shard"
 LOW = jnp.bfloat16
 F32 = jnp.float32
 
@@ -34,14 +38,14 @@
         if step == count // 2:
             got[step] = jnp.concatenate(
                 [
-                    lax.ppermute(from_left[:cut], "shard", right),
-                    lax.ppermute(from_right[cut:], "shard", left),
+                    lax.ppermute(from_left[:cut], SHARD, right),
+                    lax.ppermute(from_right[cut:], SHARD, left),
                 ],
                 axis=0,
             )
         else:
-            from_left = lax.ppermute(from_left, "shard", right)
-            from_right = lax.ppermute(from_right, "shard", left)
+            from_left = lax.ppermute(from_left, SHARD, right)
+            from_right = lax.ppermute(from_right, SHARD, left)
             got[count - step] = from_left
             got[step] = from_right
     return [got[k] for k in range(count)]
@@ -52,8 +56,8 @@
     cut = rows // 32 * 16
     half = count // 2
     far = piece(half)
-    to_right = lax.ppermute(far[:cut], "shard", right)
-    to_left = lax.ppermute(far[cut:], "shard", left)
+    to_right = lax.ppermute(far[:cut], SHARD, right)
+    to_left = lax.ppermute(far[cut:], SHARD, left)
     for distance in range(half - 1, 0, -1):
         first, second = piece(distance), piece(count - distance)
         if distance == half - 1:
@@ -62,8 +66,8 @@
         else:
             first = add_low(first, to_right)
             second = add_low(second, to_left)
-        to_right = lax.ppermute(first, "shard", right)
-        to_left = lax.ppermute(second, "shard", left)
+        to_right = lax.ppermute(first, SHARD, right)
+        to_left = lax.ppermute(second, SHARD, left)
     return piece(0).astype(F32) + to_right.astype(F32) + to_left.astype(F32)
 
 
@@ -91,11 +95,11 @@
 
 
 def dot_t(a, b):
-    return jnp.einsum("tc,dc->td", a, b, preferred_element_type=F32)
+    return lax.dot_general(a, b, (((1,), (1,)), ((), ())), preferred_element_type=F32)
 
 
 def dot_rows(a, b):
-    return jnp.einsum("ta,tb->ab", a, b, preferred_element_type=F32)
+    return lax.dot_general(a, b, (((0,), (0,)), ((), ())), preferred_element_type=F32)
 
 
 class Plan:
@@ -117,7 +121,7 @@
 
     def exchange(self, blocks):
         return lax.all_to_all(
-            blocks, ("replica", "shard"), 0, 0, tiled=True, axis_index_groups=self.groups
+            blocks, (REPLICA, SHARD), 0, 0, tiled=True, axis_index_groups=self.groups
         )
 
     def pack_units(self, heads):
@@ -170,6 +174,14 @@
         return jnp.concatenate(cols, axis=1)
 
 
+def over(a, b, dim_a, dim_b):
+    return lax.dot_general(a, b, (((dim_a,), (dim_b,)), ((), ())), preferred_element_type=F32)
+
+
+def over_units(a, b):
+    return lax.dot_general(a, b, (((0, 1), (0, 1)), ((), ())), preferred_element_type=F32)
+
+
 def widen(units, slot, slots):
     wide = jnp.concatenate([units] * slots, axis=2)
     lane_slot = jnp.arange(slots * HEAD, dtype=jnp.int32) // HEAD
@@ -183,38 +195,38 @@
 
 
 def attend_forward(queries, keys, values, query_pos, key_pos):
-    scores = jnp.einsum("uid,jd->uij", queries, keys, preferred_element_type=F32) * SCALING
+    scores = over(queries, keys, 2, 1) * SCALING
     visible = key_pos[None, None, :] <= query_pos[:, :, None]
     scores = jnp.where(visible, scores, FLOOR)
     highest = jnp.max(scores, axis=-1, keepdims=True)
     terms = jnp.exp(scores - highest)
     total = jnp.sum(terms, axis=-1, keepdims=True)
     weights = (terms / total).astype(LOW)
-    attended = jnp.einsum("uij,jd->uid", weights, values, preferred_element_type=F32)
+    attended = over(weights, values, 2, 0)
     return attended, highest + jnp.log(total)
 
 
 def attend_backward(queries, keys, values, query_pos, key_pos, log_total, grad, row_dots):
-    scores = jnp.einsum("uid,jd->uij", queries, keys, preferred_element_type=F32) * SCALING
+    scores = over(queries, keys, 2, 1) * SCALING
     visible = key_pos[None, None, :] <= query_pos[:, :, None]
     weights = jnp.where(visible, jnp.exp(scores - log_total), 0.0)
-    grad_weights = jnp.einsum("uid,jd->uij", grad, values, preferred_element_type=F32)
+    grad_weights = over(grad, values, 2, 1)
     grad_scores = (weights * (grad_weights - row_dots)).astype(LOW)
     grad_queries = (
-        jnp.einsum("uij,jd->uid", grad_scores, keys, preferred_element_type=F32) * SCALING
+        over(grad_scores, keys, 2, 0) * SCALING
     )
     grad_keys = (
-        jnp.einsum("uij,uid->jd", grad_scores, queries, preferred_element_type=F32) * SCALING
-    )
-    grad_values = jnp.einsum("uij,uid->jd", weights.astype(LOW), grad, preferred_element_type=F32)
+        over_units(grad_scores, queries) * SCALING
+    )
+    grad_values = over_units(weights.astype(LOW), grad)
     return grad_queries, grad_keys, grad_values
 
 
 def layer_forward(inputs, weights, plan, place):
-    normed = normalize(inputs, weights["gains"][0], weights["offsets"][0]).astype(LOW)
-    queries = (dot(normed, weights["q"]) + weights["q_bias"]).astype(LOW)
-    keys = dot(normed, weights["k"]).astype(LOW)
-    values = (dot(normed, weights["v"]) + weights["v_bias"]).astype(LOW)
+    normed = normalize(inputs, weights.gains[0], weights.offsets[0]).astype(LOW)
+    queries = (dot(normed, weights.q) + weights.q_bias).astype(LOW)
+    keys = dot(normed, weights.k).astype(LOW)
+    values = (dot(normed, weights.v) + weights.v_bias).astype(LOW)
     segment = inputs.shape[0]
     width = plan.slots * HEAD
     sent = jnp.concatenate(
@@ -232,19 +244,19 @@
     all_keys = arrived[:, :segment].reshape(length, width)
     all_values = arrived[:, segment : 2 * segment].reshape(length, width)
     units = plan.gather_units(arrived[:, 2 * segment :].reshape(plan.count, -1, 2 * HEAD))
-    units = widen(units, place["slot"], plan.slots)
+    units = widen(units, place.slot, plan.slots)
     attended, log_total = attend_forward(
-        units, all_keys, all_values, place["query_pos"], place["key_pos"]
-    )
-    attended = narrow(attended, place["slot"], plan.slots)
+        units, all_keys, all_values, place.query_pos, place.key_pos
+    )
+    attended = narrow(attended, place.slot, plan.slots)
     returned = plan.exchange(plan.scatter_units(attended.astype(LOW)))
     attended_low = plan.unpack_units(returned)
-    middle = inputs + dot(attended_low, weights["o"]) + weights["out_bias"]
-    normed_two = normalize(middle, weights["gains"][1], weights["offsets"][1]).astype(LOW)
-    hidden = dot(normed_two, weights["fc"]) + weights["fc_bias"]
+    middle = inputs + dot(attended_low, weights.o) + weights.out_bias
+    normed_two = normalize(middle, weights.gains[1], weights.offsets[1]).astype(LOW)
+    hidden = dot(normed_two, weights.fc) + weights.fc_bias
     active = gelu_tanh(hidden).astype(LOW)
-    output = middle + dot(active, weights["proj"]) + weights["proj_bias"]
-    saved = dict(
+    output = middle + dot(active, weights.proj) + weights.proj_bias
+    saved = Bag(
         inputs=inputs, normed=normed, units=units, keys=all_keys, values=all_values,
         attended=attended, log_total=log_total, attended_low=attended_low, middle=middle,
         normed_two=normed_two, hidden=hidden, active=active,
@@ -255,29 +267,29 @@
 def layer_backward(arriving, saved, weights, plan, place):
     segment, model_width = arriving.shape
     grad_branch = arriving.astype(LOW)
-    grad_active = dot_t(grad_branch, weights["proj"])
-    grad_hidden = jax.vjp(gelu_tanh, saved["hidden"])[1](grad_active)[0].astype(LOW)
-    grad_normed_two = dot_t(grad_hidden, weights["fc"])
+    grad_active = dot_t(grad_branch, weights.proj)
+    grad_hidden = jax.vjp(gelu_tanh, saved.hidden)[1](grad_active)[0].astype(LOW)
+    grad_normed_two = dot_t(grad_hidden, weights.fc)
     grad_middle_norm, gain_two, offset_two = jax.vjp(
-        normalize, saved["middle"], weights["gains"][1], weights["offsets"][1]
+        normalize, saved.middle, weights.gains[1], weights.offsets[1]
     )[1](grad_normed_two)
-    grads = dict(
-        proj=dot_rows(saved["active"], grad_branch),
+    grads = Bag(
+        proj=dot_rows(saved.active, grad_branch),
         proj_bias=jnp.sum(grad_branch.astype(F32), axis=0),
-        fc=dot_rows(saved["normed_two"], grad_hidden),
+        fc=dot_rows(saved.normed_two, grad_hidden),
         fc_bias=jnp.sum(grad_hidden.astype(F32), axis=0),
     )
     grad_middle = arriving + grad_middle_norm
     grad_out = grad_middle.astype(LOW)
-    grad_attended = dot_t(grad_out, weights["o"]).astype(LOW)
+    grad_attended = dot_t(grad_out, weights.o).astype(LOW)
     arrived = plan.exchange(plan.pack_units(grad_attended.reshape(segment, HEADS, HEAD)))
     grad_units = plan.gather_units(arrived)
-    row_dots = jnp.sum(grad_units.astype(F32) * saved["attended"], axis=-1, keepdims=True)
+    row_dots = jnp.sum(grad_units.astype(F32) * saved.attended, axis=-1, keepdims=True)
     grad_queries, grad_keys, grad_values = attend_backward(
-        saved["units"], saved["keys"], saved["values"], place["query_pos"], place["key_pos"],
-        saved["log_total"], widen(grad_units, place["slot"], plan.slots), row_dots,
-    )
-    grad_queries = narrow(grad_queries, place["slot"], plan.slots).astype(LOW)
+        saved.units, saved.keys, saved.values, place.query_pos, place.key_pos,
+        saved.log_total, widen(grad_units, place.slot, plan.slots), row_dots,
+    )
+    grad_queries = narrow(grad_queries, place.slot, plan.slots).astype(LOW)
     width = plan.slots * HEAD
     sent = jnp.concatenate(
         [
@@ -292,19 +304,20 @@
     grad_v = plan.sum_slots(returned[:, segment : 2 * segment]).astype(LOW)
     grad_q = plan.unpack_units(returned[:, 2 * segment :].reshape(plan.count, -1, 2 * HEAD))
     grad_normed = (
-        dot_t(grad_q, weights["q"]) + dot_t(grad_k, weights["k"]) + dot_t(grad_v, weights["v"])
+        dot_t(grad_q, weights.q) + dot_t(grad_k, weights.k) + dot_t(grad_v, weights.v)
     )
     grad_input_norm, gain_one, offset_one = jax.vjp(
-        normalize, saved["inputs"], weights["gains"][0], weights["offsets"][0]
+        normalize, saved.inputs, weights.gains[0], weights.offsets[0]
     )[1](grad_normed)
-    grads.update(
+    grads = Bag(
+        proj=grads.proj, proj_bias=grads.proj_bias, fc=grads.fc, fc_bias=grads.fc_bias,
         gains=jnp.stack([gain_one, gain_two]),
         offsets=jnp.stack([offset_one, offset_two]),
-        q=dot_rows(saved["normed"], grad_q),
-        k=dot_rows(saved["normed"], grad_k),
-        v=dot_rows(saved["normed"], grad_v),
+        q=dot_rows(saved.normed, grad_q),
+        k=dot_rows(saved.normed, grad_k),
+        v=dot_rows(saved.normed, grad_v),
         qv_bias=jnp.stack([jnp.sum(grad_q.astype(F32), axis=0), jnp.sum(grad_v.astype(F32), axis=0)]),
-        o=dot_rows(saved["attended_low"], grad_out),
+        o=dot_rows(saved.attended_low, grad_out),
         out_bias=jnp.sum(grad_out.astype(F32), axis=0),
     )
     return grad_middle + grad_input_norm, grads
@@ -314,10 +327,10 @@
     tokens, cotangent, group_order, norm_gains, norm_biases, w_qkv, qv_bias, w_out, out_bias,
     w_fc, fc_bias, w_proj, proj_bias,
 ):
-    count = lax.axis_size("shard")
-    section = lax.axis_index("section")
-    replica = lax.axis_index("replica")
-    shard = lax.axis_index("shard")
+    count = lax.axis_size(SHARD)
+    section = lax.axis_index(SECTION)
+    replica = lax.axis_index(REPLICA)
+    shard = lax.axis_index(SHARD)
     segment, model_width = tokens.shape[1], tokens.shape[2]
     rows = w_qkv.shape[1]
     half = count // 2
@@ -337,7 +350,7 @@
         crossing += [(count + s, s + half), (s + half, count + s)]
 
     def reshard(x):
-        moved = lax.ppermute(x, ("replica", "shard"), crossing)
+        moved = lax.ppermute(x, (REPLICA, SHARD), crossing)
         return jnp.where(keeps, x, moved)
 
     def pick(x):
@@ -364,7 +377,7 @@
             for u in range(plan.units)
         ]
     )
-    place = dict(
+    place = Bag(
         slot=unit_ids // plan.splits - (plan.units * seat) // plan.splits,
         query_pos=query_pos,
         key_pos=key_pos.reshape(-1),
@@ -390,14 +403,14 @@
 
     def gathered(sets):
         own = jnp.where(replica == 0, sets[0], sets[1])
-        other_layer = swap(own, "section")
+        other_layer = swap(own, SECTION)
         layers = []
         for layer in range(2):
             chunk = jnp.where(section == layer, own, other_layer)
             chunks = ring_gather(chunk, count)
             buffer = jnp.zeros((2, count) + chunk.shape, LOW)
             for offset in range(count):
-                twin = swap(chunks[offset], "replica")
+                twin = swap(chunks[offset], REPLICA)
                 at = owner(offset)
                 buffer = lax.dynamic_update_slice(buffer, chunks[offset][None, None], (replica, at, 0, 0))
                 buffer = lax.dynamic_update_slice(buffer, twin[None, None], (1 - replica, at, 0, 0))
@@ -417,7 +430,7 @@
         def row(i):
             return vec[:, i].reshape(-1)
 
-        return dict(
+        return Bag(
             q=block(a, 0, 0), k=block(a, 0, 1), v=block(a, 1, 0), o=block(a, 1, 1),
             fc=jnp.concatenate([block(f, 0, i) for i in range(4)], axis=1),
             proj=f[1].reshape(count * 4 * rows, model_width),
@@ -444,7 +457,7 @@
     def scattered(sets):
         own = jnp.where(replica == 0, sets[0], sets[1])
         other = jnp.where(replica == 0, sets[1], sets[0])
-        paired = add_low(own, swap(other, "replica"))
+        paired = add_low(own, swap(other, REPLICA))
         return ring_scatter(
             lambda k: lax.dynamic_index_in_dim(paired, owner(k), 0, keepdims=False),
             paired.shape[1], count,
@@ -457,11 +470,11 @@
         arriving = grad_input.astype(LOW).astype(F32)
         vec = jnp.concatenate(
             [
-                grads["gains"], grads["offsets"], grads["qv_bias"], grads["out_bias"][None],
+                grads.gains, grads.offsets, grads.qv_bias, grads.out_bias[None],
             ], axis=0,
         ).reshape(7, count, rows).transpose(1, 0, 2)
         vec = jnp.concatenate(
-            [vec, grads["fc_bias"].reshape(count, 4, rows), grads["proj_bias"].reshape(count, 1, rows)],
+            [vec, grads.fc_bias.reshape(count, 4, rows), grads.proj_bias.reshape(count, 1, rows)],
             axis=1,
         ).astype(LOW).reshape(count, 12 * rows)
         vec = jnp.concatenate(
@@ -470,24 +483,24 @@
         scattered_ffn[layer] = scattered(
             (
                 jnp.concatenate(
-                    [blocks_of(grads["fc"][:, i * model_width : (i + 1) * model_width], model_width) for i in range(4)],
+                    [blocks_of(grads.fc[:, i * model_width : (i + 1) * model_width], model_width) for i in range(4)],
                     axis=1,
                 ),
-                blocks_of(grads["proj"], model_width),
+                blocks_of(grads.proj, model_width),
             )
         )
         scattered_attn[layer] = scattered(
             (
-                jnp.concatenate([blocks_of(grads["q"], model_width), blocks_of(grads["k"], model_width), vec], axis=1),
-                jnp.concatenate([blocks_of(grads["v"], model_width), blocks_of(grads["o"], model_width), vec], axis=1),
+                jnp.concatenate([blocks_of(grads.q, model_width), blocks_of(grads.k, model_width), vec], axis=1),
+                jnp.concatenate([blocks_of(grads.v, model_width), blocks_of(grads.o, model_width), vec], axis=1),
             )
         )
 
     def finished(parts):
         own = jnp.where(section == 0, parts[0], parts[1])
         other = jnp.where(section == 0, parts[1], parts[0]).astype(LOW)
-        total = (own + swap(other, "section").astype(F32)).astype(LOW)
-        twin = swap(total, "replica")
+        total = (own + swap(other, SECTION).astype(F32)).astype(LOW)
+        twin = swap(total, REPLICA)
         return (
             jnp.where(replica == 0, total, twin).astype(F32),
             jnp.where(replica == 0, twin, total).astype(F32),
@@ -507,7 +520,7 @@
         low = [reshard(v.astype(LOW)) for v in per_layer]
         own = jnp.where(section == 0, low[0], low[1])
         other = jnp.where(section == 0, low[1], low[0])
-        got = swap(other, "section")
+        got = swap(other, SECTION)
         return jnp.stack([jnp.where(section == 0, own, got), jnp.where(section == 0, got, own)])[None]
 
     acts = by_owner(outputs)
@@ -528,36 +541,1113 @@
     )
 
 
+ANY = pl.BlockSpec(memory_space=pl.ANY)
+VMEM = pl.BlockSpec(memory_space=pltpu.VMEM)
+SMEM = pl.BlockSpec(memory_space=pltpu.SMEM)
+PAIR = 2 * HEAD
+VMEM_LIMIT = 60 * 2**20
+MEMORY_RATE = 3.69e6
+
+
+def mm(a, b):
+    return lax.dot_general(a, b, (((1,), (0,)), ((), ())), preferred_element_type=F32)
+
+
+def mm_nt(a, b):
+    return lax.dot_general(a, b, (((1,), (1,)), ((), ())), preferred_element_type=F32)
+
+
+def mm_tn(a, b):
+    return lax.dot_general(a, b, (((0,), (0,)), ((), ())), preferred_element_type=F32)
+
+
+def call(body, micros, operands, specs, outs, scratch, saves=(), keep=True):
+    outs = list(outs) + (list(saves) if keep else [])
+    spare = [] if keep else [pltpu.VMEM(shape, kind) for shape, kind, _ in saves]
+    return pl.pallas_call(
+        body,
+        in_specs=specs,
+        out_specs=[VMEM if space is None else ANY for _, _, space in outs],
+        out_shape=[jax.ShapeDtypeStruct(shape, kind) for shape, kind, _ in outs],
+        scratch_shapes=spare + scratch,
+        compiler_params=pltpu.CompilerParams(vmem_limit_bytes=VMEM_LIMIT),
+        cost_estimate=pl.CostEstimate(
+            flops=0, bytes_accessed=int(micros * MEMORY_RATE), transcendentals=0
+        ),
+    )(*operands)
+
+
+SEATS = 4
+
+
+def low_lanes(shape):
+    return lax.broadcasted_iota(jnp.int32, shape, len(shape) - 1) % PAIR < HEAD
+
+
+def turn(tile):
+    return pltpu.roll(tile, HEAD, 1)
+
+
+def tiles_of(values, seat):
+    at = 3 * seat // 2
+    pair, single = (at, at + 1) if seat % 2 == 0 else (at + 1, at)
+    return [values[:, t * PAIR : (t + 1) * PAIR] for t in (pair, single)]
+
+
+def join(first, second, seat):
+    low = low_lanes(first.shape)
+    if seat % 2 == 0:
+        return jnp.where(low, first, turn(second))
+    return jnp.where(low, turn(first), second)
+
+
+def fold(tile, seat):
+    half = tile.shape[0] // 2
+    return join(tile[:half], tile[half:], seat)
+
+
+def split(tile, seat):
+    low = low_lanes(tile.shape)
+    turned = turn(tile)
+    if seat % 2 == 0:
+        return jnp.where(low, tile, 0.0), jnp.where(low, turned, 0.0)
+    return jnp.where(low, 0.0, turned), jnp.where(low, 0.0, tile)
+
+
+def unfold(tile, seat):
+    return jnp.concatenate(split(tile, seat), axis=0)
+
+
+def whole_rows(pairs, singles):
+    tiles = []
+    for even in range(0, SEATS, 2):
+        tiles += [pairs[even], singles[even] + singles[even + 1], pairs[even + 1]]
+    return jnp.concatenate(tiles, axis=1)
+
+
+def start_all(copies):
+    for copy in copies:
+        copy.start()
+    return copies
+
+
+def wait_all(copies):
+    for copy in copies:
+        copy.wait()
+
+
+def to_seats(scratch, outs, idx, count, sems):
+    return start_all(
+        [
+            pltpu.make_async_copy(scratch.at[idx[count + 2 + k]], outs[k], sems.at[k])
+            for k in range(SEATS)
+        ]
+    )
+
+
+def from_seats(ins, scratch, idx, count, sems):
+    return start_all(
+        [
+            pltpu.make_async_copy(ins[k], scratch.at[idx[count + 2 + k]], sems.at[k])
+            for k in range(SEATS)
+        ]
+    )
+
+
+def in_order(refs, scratch, at, sems, outward):
+    copies = []
+    for k in range(SEATS):
+        for p in range(2):
+            ends = refs[k].at[p], scratch.at[at[2 * k + p]]
+            if outward:
+                ends = ends[::-1]
+            copies.append(pltpu.make_async_copy(*ends, sems.at[2 * k + p]))
+    return start_all(copies)
+
+
+def block_rows(segment):
+    return 4 * segment + segment // 2
+
+
+class Loader:
+    def __init__(self, sems):
+        self.sems = sems
+        self.used = 0
+        self.waits = {}
+
+    def load(self, idx, count, own, twin, targets):
+        slots = {}
+        for which in (0, 1):
+            for at, (offset, rows, ref, key) in enumerate(targets[which]):
+                for k in range(count):
+                    slots[which, at, k] = self.used
+                    self.waits.setdefault(key, []).append((ref, self.used))
+                    self.used += 1
+        for rep in (0, 1):
+            @pl.when(idx[count] == rep)
+            def _():
+                for which in (0, 1):
+                    chunks = own if which == rep else twin
+                    for at, (offset, rows, ref, key) in enumerate(targets[which]):
+                        for k in range(count):
+                            if len(chunks) == 1:
+                                chunk, place = chunks[0].at[k], k
+                            else:
+                                chunk, place = chunks[k], idx[k]
+                            pltpu.make_async_copy(
+                                chunk.at[pl.ds(offset, rows)], ref.at[place],
+                                self.sems.at[slots[which, at, k]],
+                            ).start()
+
+    def wait(self, key):
+        for ref, slot in self.waits[key]:
+            pltpu.make_async_copy(ref.at[0], ref.at[0], self.sems.at[slot]).wait()
+
+
+def flat(ref):
+    return ref[...].reshape(-1, ref.shape[-1])
+
+
+def centre(values):
+    average = jnp.mean(values, axis=-1, keepdims=True)
+    centred = values - average
+    scale = lax.rsqrt(jnp.mean(centred * centred, axis=-1, keepdims=True) + EPSILON)
+    return centred * scale, scale
+
+
+def centre_back(grad, hat, scale):
+    return scale * (
+        grad
+        - jnp.mean(grad, axis=-1, keepdims=True)
+        - hat * jnp.mean(grad * hat, axis=-1, keepdims=True)
+    )
+
+
+GELU_A, GELU_B = math.sqrt(2 / math.pi), 0.044715
+
+
+NOTE = 16
+
+
+def note_rows(small, width):
+    rows = small.shape[1]
+    hidden = jnp.pad(small[7:11].reshape(1, 4 * rows), ((0, 0), (0, width - 4 * rows)))
+    others = jnp.concatenate([small[:7], small[11:]], axis=0)
+    others = jnp.pad(others, ((0, NOTE - 9), (0, width - rows)))
+    return jnp.concatenate([others, hidden], axis=0)
+
+
+def read_notes(notes, count, width):
+    rows = width // count
+    total = None
+    hidden = []
+    for s in range(count):
+        note = notes[s].astype(F32)
+        moved = pltpu.roll(note, s * rows, 1) if s else note
+        total = moved if total is None else total + moved
+        at = (4 * rows * s) % width
+        hidden.append(pltpu.roll(note[8:], at, 1)[NOTE - 9 :] if at else note[8:][NOTE - 9 :])
+    per = width // (4 * rows)
+    lines = [sum(hidden[b * per + i] for i in range(per)) for b in range(4)]
+    return [total[:8]] + lines
+
+
+def project_kernel(count, segment, inputs, hopped, attn, idx, keep):
+    width = inputs[0].shape[1]
+    rows = width // count
+    given = [] if hopped is None else [hopped]
+    tall = block_rows(segment)
+
+    def body(idx, first, second, *rest):
+        arrived, rest = rest[: len(given)], rest[len(given) :]
+        chunks, rest = rest[: 2 * count], rest[2 * count :]
+        outs, rest = rest[:SEATS], rest[SEATS:]
+        vec, chosen, normed, blocks, wq, wk, wv, notes, sems, out_sems = rest
+        loader = Loader(sems)
+        loader.load(
+            idx, count, chunks[:count], chunks[count:],
+            [
+                [(0, rows, wq, 0), (rows, rows, wk, 1), (2 * rows, NOTE, notes, 3)],
+                [(0, rows, wv, 2)],
+            ],
+        )
+        values = jnp.concatenate([first[:segment], second[:segment]], axis=0).astype(F32)
+        if given:
+            values = jnp.where(idx[count + 1] == 0, values, arrived[0][...].astype(F32))
+        chosen[...] = values.astype(LOW)
+        hat, _ = centre(values)
+        loader.wait(3)
+        lines = read_notes([notes[s] for s in range(count)], count, width)
+        vec[0:8] = lines[0]
+        for b in range(4):
+            vec[8 + b : 9 + b] = lines[1 + b]
+        low = (hat * vec[0:1] + vec[2:3]).astype(LOW)
+        normed[...] = low
+        loader.wait(0)
+        queries = mm(low, flat(wq)) + vec[4:5]
+        loader.wait(1)
+        keys = mm(low, flat(wk))
+        loader.wait(2)
+        values = mm(low, flat(wv)) + vec[5:6]
+        for d in range(SEATS):
+            (qp, qs), (kp, ks), (vp, vs) = [tiles_of(x, d) for x in (queries, keys, values)]
+            both = join(qs, ks, d)
+            for p in range(2):
+                span = slice(p * segment, (p + 1) * segment)
+                for at, tile in enumerate((qp, kp, vp, both)):
+                    blocks[d, p, at * segment : (at + 1) * segment] = tile[span].astype(LOW)
+                blocks[d, p, 4 * segment :] = fold(vs[span], d).astype(LOW)
+        wait_all(to_seats(blocks, outs, idx, count, out_sems))
+
+    weight = pltpu.VMEM((count, rows, width), LOW)
+    return call(
+        body, 7, [idx, *inputs, *given, *attn[0], *attn[1]],
+        [SMEM, VMEM, VMEM] + [VMEM] * len(given) + [ANY] * (2 * count),
+        [((2, tall, PAIR), LOW, True)] * SEATS
+        + [((12, width), F32, None), ((2 * segment, width), LOW, None)],
+        [
+            pltpu.VMEM((SEATS, 2, tall, PAIR), LOW), weight, weight, weight,
+            pltpu.VMEM((count, NOTE, width), LOW), pltpu.SemaphoreType.DMA((4 * count,)),
+            pltpu.SemaphoreType.DMA((SEATS,)),
+        ],
+        [((2 * segment, width), LOW, None)], keep,
+    )
+
+
+def read_heads(blocks, segment):
+    def joined(at):
+        return jnp.concatenate(
+            [blocks[i, at * segment : (at + 1) * segment] for i in range(blocks.shape[0])], axis=0
+        )
+
+    third = joined(3).astype(F32)
+    low = low_lanes(third.shape)
+    values = [unfold(blocks[i, 4 * segment :].astype(F32), 0) for i in range(blocks.shape[0])]
+    return (
+        (joined(0), joined(1), joined(2)),
+        (
+            jnp.where(low, third, 0.0).astype(LOW), turn(third).astype(LOW),
+            jnp.concatenate(values, axis=0).astype(LOW),
+        ),
+    )
+
+
+def stacked(rows):
+    low = low_lanes(rows.shape)
+    zero = jnp.zeros_like(rows)
+    return jnp.concatenate([jnp.where(low, rows, zero), jnp.where(low, zero, rows)], axis=0)
+
+
+def unstacked(rows):
+    half = rows.shape[0] // 2
+    return jnp.where(low_lanes((half, PAIR)), rows[:half], rows[half:])
+
+
+def earlier(rows, step):
+    row = lax.broadcasted_iota(jnp.int32, (rows, step), 0) % step
+    return lax.broadcasted_iota(jnp.int32, (rows, step), 1) <= row
+
+
+def attend_kernel(count, segment, arrived, at, keep):
+    length, step = count * segment, 2 * segment
+    tall = block_rows(segment)
+    short = segment + segment // 2
+
+    def body(at, *rest):
+        ins, outs, rest = rest[:SEATS], rest[SEATS : 2 * SEATS], rest[2 * SEATS :]
+        attended, total, blocks, backs, sems, out_sems = rest
+        wait_all(in_order(ins, blocks, at, sems, False))
+        heads = read_heads(blocks, segment)
+        for i in range(length // step):
+            span = slice(i * step, (i + 1) * step)
+            logs = []
+            for g, (queries, keys, values) in enumerate(heads):
+                query = queries[span] * SCALING
+                if g == 0:
+                    query = stacked(query)
+                mask = earlier(query.shape[0], step)
+                near = jnp.where(mask, mm_nt(query, keys[span]), FLOOR)
+                highest = jnp.max(near, axis=-1, keepdims=True)
+                if i > 0:
+                    far = mm_nt(query, keys[: i * step])
+                    highest = jnp.maximum(highest, jnp.max(far, axis=-1, keepdims=True))
+                    far = jnp.exp(far - highest)
+                near = jnp.exp(near - highest)
+                denominator = jnp.sum(near, axis=-1, keepdims=True)
+                result = mm(near.astype(LOW), values[span])
+                if i > 0:
+                    denominator += jnp.sum(far, axis=-1, keepdims=True)
+                    result += mm(far.astype(LOW), values[: i * step])
+                result = result * (1.0 / denominator)
+                log = highest + jnp.log(denominator)
+                if g == 0:
+                    result = unstacked(result)
+                    logs += [log[:step], log[step:]]
+                else:
+                    logs.append(log)
+                attended[g, span] = result
+                for p in range(2):
+                    tile = result[p * segment : (p + 1) * segment]
+                    if g == 0:
+                        backs[2 * i + p, :segment] = tile.astype(LOW)
+                    else:
+                        backs[2 * i + p, segment:] = fold(tile, 0).astype(LOW)
+            lane = lax.broadcasted_iota(jnp.int32, (step, PAIR), 1)
+            total[span] = jnp.where(lane == 0, logs[0], jnp.where(lane == 1, logs[1], logs[2]))
+        wait_all(in_order(outs, backs, at, out_sems, True))
+
+    return call(
+        body, 9, [at, *arrived], [SMEM] + [ANY] * SEATS,
+        [((2, short, PAIR), LOW, True)] * SEATS,
+        [
+            pltpu.VMEM((count, tall, PAIR), LOW), pltpu.VMEM((count, short, PAIR), LOW),
+            pltpu.SemaphoreType.DMA((2 * SEATS,)), pltpu.SemaphoreType.DMA((2 * SEATS,)),
+        ],
+        [((2, length, PAIR), F32, None), ((length, PAIR), F32, None)], keep,
+    )
+
+
+def attend_back_kernel(count, segment, arrived, grads, attended, total, at, ties):
+    length, step = count * segment, 2 * segment
+    tall = block_rows(segment)
+    short = segment + segment // 2
+
+    def body(at, attended, total, *rest):
+        ins, grad_ins, rest = rest[:SEATS], rest[SEATS : 2 * SEATS], rest[2 * SEATS + len(ties) :]
+        outs, rest = rest[:SEATS], rest[SEATS:]
+        blocks, grads, backs, of_keys, of_values, sems, grad_sems, out_sems = rest
+        first = in_order(ins, blocks, at, sems, False)
+        second = in_order(grad_ins, grads, at, grad_sems, False)
+        wait_all(first)
+        heads = read_heads(blocks, segment)
+        wait_all(second)
+        for i in reversed(range(length // step)):
+            span = slice(i * step, (i + 1) * step)
+            third = None
+            for g, (queries, keys, values) in enumerate(heads):
+                query = queries[span] * SCALING
+                if g == 0:
+                    grad = jnp.concatenate([grads[2 * i + p, :segment] for p in range(2)], axis=0)
+                    dots = grad.astype(F32) * attended[0, span]
+                    low = low_lanes(dots.shape)
+                    dots = jnp.concatenate([jnp.where(low, dots, 0.0), jnp.where(low, 0.0, dots)], axis=0)
+                    log = jnp.concatenate([total[span, 0:1], total[span, 1:2]], axis=0)
+                    query, grad = stacked(query), stacked(grad)
+                else:
+                    grad = jnp.concatenate(
+                        [unfold(grads[2 * i + p, segment:].astype(F32), 0) for p in range(2)], axis=0
+                    )
+                    dots = grad * attended[1, span]
+                    grad = grad.astype(LOW)
+                    log = total[span, 2:3]
+                dots = jnp.sum(dots, axis=-1, keepdims=True)
+                parts = [(span, True)] + ([(slice(0, i * step), False)] if i > 0 else [])
+                of_queries = None
+                for keyed, near in parts:
+                    weights = jnp.exp(mm_nt(query, keys[keyed]) - log)
+                    if near:
+                        weights = jnp.where(earlier(query.shape[0], step), weights, 0.0)
+                    grad_scores = (weights * (mm_nt(grad, values[keyed]) - dots)).astype(LOW)
+                    term = mm(grad_scores, keys[keyed])
+                    of_queries = term if of_queries is None else of_queries + term
+                    key_term = mm_tn(grad_scores, query)
+                    value_term = mm_tn(weights.astype(LOW), grad)
+                    if i == length // step - 1:
+                        of_keys[g, keyed] = key_term
+                        of_values[g, keyed] = value_term
+                    else:
+                        of_keys[g, keyed] += key_term
+                        of_values[g, keyed] += value_term
+                of_queries = of_queries * SCALING
+                if g == 0:
+                    of_queries = unstacked(of_queries)
+                    for p in range(2):
+                        backs[2 * i + p, :segment] = of_queries[p * segment : (p + 1) * segment].astype(LOW)
+                else:
+                    third = of_queries
+            low = low_lanes((segment, PAIR))
+            for p in range(2):
+                own = slice(i * step + p * segment, i * step + (p + 1) * segment)
+                block = backs.at[2 * i + p]
+                block[segment : 2 * segment] = of_keys[0, own].astype(LOW)
+                block[2 * segment : 3 * segment] = of_values[0, own].astype(LOW)
+                block[3 * segment : 4 * segment] = join(
+                    third[p * segment : (p + 1) * segment], of_keys[1, own], 0
+                ).astype(LOW)
+                block[4 * segment :] = fold(of_values[1, own], 0).astype(LOW)
+        wait_all(in_order(outs, backs, at, out_sems, True))
+
+    return call(
+        body, 14, [at, attended, total, *arrived, *grads, *ties],
+        [SMEM, VMEM, VMEM] + [ANY] * (2 * SEATS + len(ties)),
+        [((2, tall, PAIR), LOW, True)] * SEATS,
+        [
+            pltpu.VMEM((count, tall, PAIR), LOW), pltpu.VMEM((count, short, PAIR), LOW),
+            pltpu.VMEM((count, tall, PAIR), LOW), pltpu.VMEM((2, length, PAIR), F32),
+            pltpu.VMEM((2, length, PAIR), F32), pltpu.SemaphoreType.DMA((2 * SEATS,)),
+            pltpu.SemaphoreType.DMA((2 * SEATS,)), pltpu.SemaphoreType.DMA((2 * SEATS,)),
+        ],
+    )
+
+
+def feed_kernel(count, segment, returned, inputs, vec, attn, ffn, idx, keep):
+    width = inputs.shape[1]
+    rows, tokens = width // count, 2 * segment
+    short = segment + segment // 2
+
+    def body(idx, x, vec, *rest):
+        back, rest = rest[:SEATS], rest[SEATS:]
+        chunks, rest = rest[: 4 * count], rest[4 * count :]
+        output, attended, middle, normed, slope, active, blocks, wo, wf, wp, sems, in_sems = rest
+        copies = from_seats(back, blocks, idx, count, in_sems)
+        loader = Loader(sems)
+        loader.load(idx, count, chunks[:count], chunks[count : 2 * count], [[], [(rows, rows, wo, 5)]])
+        loader.load(
+            idx, count, chunks[2 * count : 3 * count], chunks[3 * count :],
+            [[(b * rows, rows, wf.at[b], b) for b in range(4)], [(b * rows, rows, wp.at[:, b], 4) for b in range(4)]],
+        )
+        wait_all(copies)
+        low = read_returned(blocks, segment).astype(LOW)
+        attended[...] = low
+        loader.wait(5)
+        mid = x[...].astype(F32) + mm(low, flat(wo)) + vec[6:7]
+        middle[...] = mid
+        hat, _ = centre(mid)
+        low = (hat * vec[1:2] + vec[3:4]).astype(LOW)
+        normed[...] = low
+        for b in range(4):
+            loader.wait(b)
+            span = slice(b * width, (b + 1) * width)
+            u = mm(low, flat(wf.at[b])) + vec[8 + b : 9 + b]
+            square = u * u
+            t = jnp.tanh(u * (GELU_A + GELU_A * GELU_B * square))
+            half = 0.5 + 0.5 * t
+            active[:, span] = (u * half).astype(LOW)
+            if keep:
+                slope[:, span] = (
+                    half + u * (0.5 - 0.5 * t * t) * (GELU_A + 3.0 * GELU_A * GELU_B * square)
+                ).astype(LOW)
+        loader.wait(4)
+        output[...] = (mid + mm(active[...], flat(wp)) + vec[7:8]).astype(LOW)
+
+    return call(
+        body, 10, [idx, inputs, vec, *returned, *attn[0], *attn[1], *ffn[0], *ffn[1]],
+        [SMEM, VMEM, VMEM] + [ANY] * (SEATS + 4 * count),
+        [((tokens, width), LOW, None)],
+        [
+            pltpu.VMEM((SEATS, 2, short, PAIR), LOW), pltpu.VMEM((count, rows, width), LOW),
+            pltpu.VMEM((4, count, rows, width), LOW), pltpu.VMEM((count, 4, rows, width), LOW),
+            pltpu.SemaphoreType.DMA((9 * count,)), pltpu.SemaphoreType.DMA((SEATS,)),
+        ],
+        [
+            ((tokens, width), LOW, None), ((tokens, width), F32, None), ((tokens, width), LOW, None),
+            ((tokens, 4 * width), LOW, None), ((tokens, 4 * width), LOW, None),
+        ],
+        keep,
+    )
+
+
+def read_returned(blocks, segment):
+    pairs, singles = [], []
+    for d in range(SEATS):
+        pairs.append(jnp.concatenate([blocks[d, p, :segment].astype(F32) for p in range(2)], axis=0))
+        singles.append(
+            jnp.concatenate([unfold(blocks[d, p, segment:].astype(F32), d) for p in range(2)], axis=0)
+        )
+    return whole_rows(pairs, singles)
+
+
+def feed_back_kernel(count, segment, grads, hopped, saved, attn, ffn, idx, keep):
+    width = grads[0].shape[1]
+    rows, tokens = width // count, 2 * segment
+    short = segment + segment // 2
+    given = [] if hopped is None else [hopped]
+
+    def body(idx, first, second, middle, slope, active, normed, vec, *rest):
+        arrived, rest = rest[: len(given)], rest[len(given) :]
+        chunks, rest = rest[: 4 * count], rest[4 * count :]
+        outs, rest = rest[:SEATS], rest[SEATS:]
+        grad_middle, mine, theirs, sums, grad_out, blocks, wo, wf, wp, gh, sems, out_sems = rest
+        loader = Loader(sems)
+        loader.load(
+            idx, count, chunks[2 * count : 3 * count], chunks[3 * count :],
+            [[(b * rows, rows, wf.at[b], b) for b in range(4)], [(b * rows, rows, wp.at[:, b], 4) for b in range(4)]],
+        )
+        loader.load(idx, count, chunks[:count], chunks[count : 2 * count], [[], [(rows, rows, wo, 5)]])
+        branch = jnp.concatenate([first[...], second[...]], axis=0).astype(F32)
+        if given:
+            branch = jnp.where(idx[count + 1] == 1, branch, arrived[0][...].astype(F32))
+        wide, branch = branch, branch.astype(LOW)
+        loader.wait(4)
+        weight = flat(wp)
+        back = jnp.zeros((tokens, width), F32)
+        for b in range(4):
+            span = slice(b * width, (b + 1) * width)
+            ga = mm_nt(branch, weight[span])
+            low = (ga * slope[:, span].astype(F32)).astype(LOW)
+            gh[:, span] = low
+            if keep:
+                sums[3 + b : 4 + b] = jnp.sum(low.astype(F32), axis=0, keepdims=True)
+            loader.wait(b)
+            back += mm_nt(low, flat(wf.at[b]))
+        hat, scale = centre(middle[...])
+        total = wide + centre_back(back * vec[1:2], hat, scale)
+        grad_middle[...] = total
+        low = total.astype(LOW)
+        grad_out[...] = low
+        loader.wait(5)
+        values = mm_nt(low, flat(wo))
+        for d in range(SEATS):
+            pair, single = tiles_of(values, d)
+            for p in range(2):
+                part = slice(p * segment, (p + 1) * segment)
+                blocks[d, p, :segment] = pair[part].astype(LOW)
+                blocks[d, p, segment:] = fold(single[part], d).astype(LOW)
+        copies = to_seats(blocks, outs, idx, count, out_sems)
+        if keep:
+            sums[0:1] = jnp.sum(back * hat, axis=0, keepdims=True)
+            sums[1:2] = jnp.sum(back, axis=0, keepdims=True)
+            sums[2:3] = jnp.sum(low.astype(F32), axis=0, keepdims=True)
+            sums[7:8] = jnp.sum(wide, axis=0, keepdims=True)
+
+            @pl.when(idx[count] == 0)
+            def _():
+                mine[:, :width] = normed[...]
+                mine[:, width:] = gh[...]
+                theirs[:, :width] = branch
+                theirs[:, width:] = active[...]
+
+            @pl.when(idx[count] == 1)
+            def _():
+                mine[:, :width] = branch
+                mine[:, width:] = active[...]
+                theirs[:, :width] = normed[...]
+                theirs[:, width:] = gh[...]
+
+        wait_all(copies)
+
+    return call(
+        body, 14,
+        [
+            idx, *grads, saved.middle, saved.slope, saved.active, saved.normed_two, saved.vec,
+            *given, *attn[0], *attn[1], *ffn[0], *ffn[1],
+        ],
+        [SMEM] + [VMEM] * (7 + len(given)) + [ANY] * (4 * count),
+        [((2, short, PAIR), LOW, True)] * SEATS + [((tokens, width), F32, None)],
+        [
+            pltpu.VMEM((SEATS, 2, short, PAIR), LOW), pltpu.VMEM((count, rows, width), LOW),
+            pltpu.VMEM((4, count, rows, width), LOW), pltpu.VMEM((count, 4, rows, width), LOW),
+            pltpu.VMEM((tokens, 4 * width), LOW), pltpu.SemaphoreType.DMA((9 * count,)),
+            pltpu.SemaphoreType.DMA((SEATS,)),
+        ],
+        [
+            ((tokens, 5 * width), LOW, None), ((tokens, 5 * width), LOW, None), ((8, width), F32, None),
+            ((tokens, width), LOW, None),
+        ],
+        keep,
+    )
+
+
+def project_back_kernel(count, segment, returned, grad_middle, grad_out, saved, attn, idx, keep):
+    tokens, width = grad_middle.shape
+    rows = width // count
+    tall = block_rows(segment)
+    kept = [grad_out, saved.normed, saved.attended_low] if keep else []
+
+    def body(idx, grad_middle, x, vec, *rest):
+        held, rest = rest[: len(kept)], rest[len(kept) :]
+        back, rest = rest[:SEATS], rest[SEATS:]
+        chunks, rest = rest[: 2 * count], rest[2 * count :]
+        grad_low, grad_in, mine, theirs, sums, blocks, wq, wk, wv, sems, in_sems = rest
+        copies = from_seats(back, blocks, idx, count, in_sems)
+        loader = Loader(sems)
+        loader.load(
+            idx, count, chunks[:count], chunks[count:],
+            [[(0, rows, wq, 0), (rows, rows, wk, 1)], [(0, rows, wv, 2)]],
+        )
+        hat, scale = centre(x[...].astype(F32))
+        wait_all(copies)
+        pairs, singles = [[], [], []], [[], [], []]
+        for d in range(SEATS):
+            for at in range(3):
+                pairs[at].append(
+                    jnp.concatenate(
+                        [blocks[d, p, at * segment : (at + 1) * segment].astype(F32) for p in range(2)], axis=0
+                    )
+                )
+            both = [split(blocks[d, p, 3 * segment : 4 * segment].astype(F32), d) for p in range(2)]
+            for at in range(2):
+                singles[at].append(jnp.concatenate([b[at] for b in both], axis=0))
+            singles[2].append(
+                jnp.concatenate([unfold(blocks[d, p, 4 * segment :].astype(F32), d) for p in range(2)], axis=0)
+            )
+        gq, gk, gv = [whole_rows(a, b).astype(LOW) for a, b in zip(pairs, singles)]
+        loader.wait(0)
+        total = mm_nt(gq, flat(wq))
+        loader.wait(1)
+        total += mm_nt(gk, flat(wk))
+        loader.wait(2)
+        total += mm_nt(gv, flat(wv))
+        result = grad_middle[...] + centre_back(total * vec[0:1], hat, scale)
+        grad_low[...] = result.astype(LOW)
+        if not keep:
+            return
+        grad_in[...] = result
+        sums[0:1] = jnp.sum(total * hat, axis=0, keepdims=True)
+        sums[1:2] = jnp.sum(total, axis=0, keepdims=True)
+        sums[2:3] = jnp.sum(gq.astype(F32), axis=0, keepdims=True)
+        sums[3:4] = jnp.sum(gv.astype(F32), axis=0, keepdims=True)
+        sums[4:8] = jnp.zeros((4, width), F32)
+        grad_out, normed, attended = held
+
+        def fill(first, second):
+            first[:, :width] = normed[...]
+            first[:, width : 2 * width] = gq
+            first[:, 2 * width : 3 * width] = normed[...]
+            first[:, 3 * width :] = gk
+            second[:, :width] = normed[...]
+            second[:, width : 2 * width] = gv
+            second[:, 2 * width : 3 * width] = attended[...]
+            second[:, 3 * width :] = grad_out[...]
+
+        @pl.when(idx[count] == 0)
+        def _():
+            fill(mine, theirs)
+
+        @pl.when(idx[count] == 1)
+        def _():
+            fill(theirs, mine)
+
+    weight = pltpu.VMEM((count, rows, width), LOW)
+    return call(
+        body, 8, [idx, grad_middle, saved.inputs, saved.vec, *kept, *returned, *attn[0], *attn[1]],
+        [SMEM] + [VMEM] * (3 + len(kept)) + [ANY] * (SEATS + 2 * count),
+        [((tokens, width), LOW, None)],
+        [
+            pltpu.VMEM((SEATS, 2, tall, PAIR), LOW), weight, weight, weight,
+            pltpu.SemaphoreType.DMA((3 * count,)), pltpu.SemaphoreType.DMA((SEATS,)),
+        ],
+        [
+            ((tokens, width), F32, None), ((tokens, 4 * width), LOW, None),
+            ((tokens, 4 * width), LOW, None), ((8, width), F32, None),
+        ],
+        keep,
+    )
+
+
+def send_out(scratch, outs, idx, count, blocks, rows, base, sems, start):
+    for k in range(count):
+        for b in range(blocks):
+            if len(outs) == 1:
+                piece, place = outs[0].at[k], k
+            else:
+                piece, place = outs[k], idx[k]
+            copy = pltpu.make_async_copy(
+                scratch.at[pl.ds(pl.multiple_of(b * base + place * rows, 16), rows)],
+                piece.at[pl.ds(b * rows, rows)], sems.at[k * blocks + b],
+            )
+            copy.start() if start else copy.wait()
+
+
+def ffn_terms_kernel(count, parts, idx):
+    ties = []
+    width = parts[0].shape[1] // 5
+    rows = width // count
+
+    shape = (4 * rows, width)
+    pieces = [(shape, LOW, True)] * count
+
+    def body(idx, *rest):
+        given, rest = rest[: len(parts)], rest[len(parts) + len(ties) :]
+        outs, (scratch, sems) = rest[: len(pieces)], rest[len(pieces) :]
+        narrow = jnp.concatenate([part[:, :width] for part in given], axis=0)
+
+        def wide(b):
+            span = slice((1 + b) * width, (2 + b) * width)
+            return jnp.concatenate([part[:, span] for part in given], axis=0)
+
+        @pl.when(idx[count] == 0)
+        def _():
+            for b in range(4):
+                scratch[b * width : (b + 1) * width] = mm_tn(narrow, wide(b)).astype(LOW)
+            send_out(scratch, outs, idx, count, 4, rows, width, sems, True)
+            send_out(scratch, outs, idx, count, 4, rows, width, sems, False)
+
+        @pl.when(idx[count] == 1)
+        def _():
+            for b in range(4):
+                scratch[b * width : (b + 1) * width] = mm_tn(wide(b), narrow).astype(LOW)
+            send_out(scratch, outs, idx, count, 1, 4 * rows, 0, sems, True)
+            send_out(scratch, outs, idx, count, 1, 4 * rows, 0, sems, False)
+
+    return call(
+        body, 8, [idx, *parts, *ties], [SMEM] + [VMEM] * len(parts) + [ANY] * len(ties),
+        pieces,
+        [pltpu.VMEM((4 * width, width), LOW), pltpu.SemaphoreType.DMA((4 * count,))],
+    )
+
+
+def attn_terms_kernel(count, parts, sums_one, sums_two, idx):
+    ties = []
+    width = parts[0].shape[1] // 4
+    given = len(parts), len(sums_one)
+    rows = width // count
+
+    def body(idx, *rest):
+        parts, rest = rest[: given[0]], rest[given[0] :]
+        one = sum(ref[...] for ref in rest[: given[1]])
+        two = sum(ref[...] for ref in rest[given[1] : 2 * given[1]])
+        rest = rest[2 * given[1] + len(ties) :]
+        outs, (scratch, notes, sems) = rest[:count], rest[count:]
+
+        def both(b):
+            span = slice(b * width, (b + 1) * width)
+            return jnp.concatenate([part[:, span] for part in parts], axis=0)
+
+        flatly = jnp.concatenate(
+            [
+                one[0:1], two[0:1], one[1:2], two[1:2], one[2:3], one[3:4], two[2:3], two[7:8],
+                jnp.zeros((NOTE - 8, width), F32),
+            ],
+            axis=0,
+        )
+        lane = lax.broadcasted_iota(jnp.int32, (NOTE, width), 1)
+        line = lax.broadcasted_iota(jnp.int32, (NOTE, width), 0)
+        for s in range(count):
+            note = pltpu.roll(flatly, width - s * rows, 1) if s else flatly
+            start = 4 * rows * s
+            hidden = two[3 + start // width : 4 + start // width]
+            hidden = pltpu.roll(
+                jnp.broadcast_to(hidden, (8, width)), (width - start % width) % width, 1
+            )
+            hidden = jnp.concatenate([hidden, hidden], axis=0)
+            note = jnp.where(
+                (line < 8) & (lane < rows), note,
+                jnp.where((line == NOTE - 1) & (lane < 4 * rows), hidden, 0.0),
+            )
+            notes[s] = note.astype(LOW)
+        for b in range(2):
+            scratch[b * width : (b + 1) * width] = mm_tn(both(2 * b), both(2 * b + 1)).astype(LOW)
+        for start in (True, False):
+            send_out(scratch, outs, idx, count, 2, rows, width, sems, start)
+            for k in range(count):
+                copy = pltpu.make_async_copy(
+                    notes.at[idx[k]], outs[k].at[pl.ds(2 * rows, NOTE)], sems.at[2 * count + k]
+                )
+                copy.start() if start else copy.wait()
+
+    return call(
+        body, 5, [idx, *parts, *sums_one, *sums_two, *ties],
+        [SMEM] + [VMEM] * (given[0] + 2 * given[1]) + [ANY] * len(ties),
+        [((2 * rows + NOTE, width), LOW, True)] * count,
+        [
+            pltpu.VMEM((2 * width, width), LOW), pltpu.VMEM((count, NOTE, width), LOW),
+            pltpu.SemaphoreType.DMA((3 * count,)),
+        ],
+    )
+
+
+def hold(values, *after):
+    return lax.optimization_barrier((values, after))[0] if len(after) else values
+
+
+class GatherRing:
+    def __init__(self, chunk, count, rightward):
+        self.right, self.left = ring_pairs(count)
+        self.count, self.rightward, self.at = count, rightward, 0
+        self.last = (chunk, chunk)
+        self.own = {0: chunk}
+        self.twin = {0: swap(chunk, REPLICA)}
+
+    def keep(self, k, chunk):
+        self.own[k], self.twin[k] = chunk, swap(chunk, REPLICA)
+
+    def step(self, *after):
+        self.at += 1
+        near, far = hold(self.last, *after)
+        if self.at < self.count // 2:
+            near = lax.ppermute(near, SHARD, self.right)
+            far = lax.ppermute(far, SHARD, self.left)
+            self.keep(self.count - self.at, near)
+            self.keep(self.at, far)
+            self.last = (near, far)
+        else:
+            if self.rightward:
+                last = lax.ppermute(near, SHARD, self.right)
+            else:
+                last = lax.ppermute(far, SHARD, self.left)
+            self.keep(self.at, last)
+            self.last = (last,)
+
+    def lists(self):
+        return [[side[k] for k in range(self.count)] for side in (self.own, self.twin)]
+
+
+class ScatterRing:
+    def __init__(self, pieces, count, rightward):
+        self.right, self.left = ring_pairs(count)
+        self.pieces, self.count, self.rightward = pieces, count, rightward
+        self.at = count // 2
+        self.last = None
+
+    def step(self, *after):
+        pieces, half = self.pieces, self.count // 2
+        if self.at == half:
+            far = hold(pieces[half], *after)
+            if self.rightward:
+                self.last = (lax.ppermute(far, SHARD, self.right), None)
+            else:
+                self.last = (None, lax.ppermute(far, SHARD, self.left))
+        else:
+            sides = []
+            for piece, term in zip((pieces[self.at], pieces[self.count - self.at]), self.last):
+                sides.append(piece if term is None else add_low(piece, term))
+            first, second = hold(tuple(sides), *after)
+            self.last = (
+                lax.ppermute(first, SHARD, self.right), lax.ppermute(second, SHARD, self.left)
+            )
+        self.at -= 1
+
+    def total(self):
+        return self.pieces[0].astype(F32) + self.last[0].astype(F32) + self.last[1].astype(F32)
+
+
+def fast_device(
+    tokens, cotangent, group_order, norm_gains, norm_biases, w_qkv, qv_bias, w_out, out_bias,
+    w_fc, fc_bias, w_proj, proj_bias,
+):
+    count = lax.axis_size(SHARD)
+    section = lax.axis_index(SECTION)
+    replica = lax.axis_index(REPLICA)
+    shard = lax.axis_index(SHARD)
+    segment, width = tokens.shape[1], tokens.shape[2]
+    rows = w_qkv.shape[1]
+    half = count // 2
+    order = ring_order(count)
+    position = jnp.asarray(np.argsort(np.array(order)), jnp.int32)[shard]
+    around = lax.rem(position + jnp.arange(count, dtype=jnp.int32), count)
+    seat = 2 * replica + lax.rem(shard, 2)
+    others = seat ^ jnp.arange(SEATS, dtype=jnp.int32)
+    idx = jnp.concatenate(
+        [jnp.asarray(order, jnp.int32)[around], jnp.stack([replica, section]).astype(jnp.int32), others]
+    )
+
+    ways = [
+        [
+            (r * count + 2 * z + y, (z // 2) * count + 2 * (2 * r + (z + j) % 2) + y)
+            for r in range(2) for z in range(half) for y in range(2)
+        ]
+        for j in range(2)
+    ]
+    odd = lax.rem(shard // 2, 2)
+
+    def gather_in(x, j, *more):
+        own = lax.dynamic_index_in_dim(x, lax.rem(odd + j, 2), 0, keepdims=False)
+        own = jnp.concatenate([own, *more], axis=0) if more else own
+        return lax.ppermute(own, (REPLICA, SHARD), ways[j])
+
+    def give_back(x):
+        parts = [
+            lax.ppermute(
+                x[j * segment : (j + 1) * segment], (REPLICA, SHARD), [(b, a) for a, b in ways[j]]
+            )
+            for j in range(2)
+        ]
+        return jnp.stack([jnp.where(odd == 0, *parts), jnp.where(odd == 0, *parts[::-1])])[None]
+
+    def exchange(parts):
+        diagonal = [(r * count + s, (1 - r) * count + (s ^ 1)) for r in range(2) for s in range(count)]
+        return [
+            parts[0],
+            lax.ppermute(parts[1], SHARD, [(s, s ^ 1) for s in range(count)]),
+            swap(parts[2], REPLICA),
+            lax.ppermute(parts[3], (REPLICA, SHARD), diagonal),
+        ]
+
+    small = jnp.concatenate(
+        [norm_gains[0], norm_biases[0], qv_bias[0], out_bias, fc_bias.reshape(4, rows), proj_bias],
+        axis=0,
+    )
+    qkv = w_qkv[0]
+    attn_own = jnp.concatenate(
+        [
+            jnp.where(replica == 0, qkv[:, :width], qkv[:, 2 * width :]),
+            jnp.where(replica == 0, qkv[:, width : 2 * width], w_out[0]),
+            note_rows(small, width),
+        ],
+        axis=0,
+    )
+    fc_blocks = jnp.concatenate([w_fc[0][:, b * width : (b + 1) * width] for b in range(4)], axis=0)
+    ffn_own = jnp.where(replica == 0, fc_blocks, w_proj[0])
+
+    attn_ring = GatherRing(attn_own, count, True)
+    attn_ring.step()
+    order_row = lax.dynamic_index_in_dim(group_order, odd, 0).astype(LOW)
+    order_rows = jnp.pad(order_row, ((0, NOTE - 1), (0, width - count)))
+    packed = [gather_in(tokens, 0, order_rows), gather_in(tokens, 1)]
+    blocks_at = packed[0][segment, :count].astype(jnp.int32)
+    pair = shard // 2
+    slot = lax.rem(pair + jnp.arange(2, dtype=jnp.int32), 2)
+    which = (4 * (others // 2) + others % 2)[:, None] + 2 * slot[None, :]
+    at = jnp.sum(
+        jnp.where(
+            which.reshape(-1, 1) == jnp.arange(count, dtype=jnp.int32)[None, :], blocks_at[None, :], 0
+        ),
+        axis=1,
+    )
+    attn_ring.step()
+    attn_ring.step()
+    ffn_ring = GatherRing(hold(ffn_own, attn_ring.last), count, False)
+    ffn_ring.step()
+    attn_ring.step()
+    attn = attn_ring.lists()
+
+    def forward(hopped, keep, before):
+        *sent, vec, inputs = project_kernel(count, segment, packed, hopped, attn, idx, keep)[: SEATS + 2 + keep]
+        normed = None
+        if keep:
+            vec, inputs, normed = sent.pop(), vec, inputs
+        sent = before[0](sent)
+        arrived = exchange(sent)
+        back = attend_kernel(count, segment, before[1](arrived), at, keep)
+        back, kept = back[:SEATS], back[SEATS:]
+        returned = exchange(before[2](back))
+        fed = feed_kernel(
+            count, segment, before[3](returned), inputs, vec, attn, ffn_ring.lists(), idx, keep
+        )
+        state = Bag(vec=vec, inputs=inputs, normed=normed, arrived=arrived, output=fed[0])
+        if keep:
+            state.attended, state.total = kept
+            state.attended_low, state.middle, state.normed_two, state.slope, state.active = fed[1:]
+        return state
+
+    def ring_sent(sent):
+        sent = hold(sent, ffn_ring.last)
+        ffn_ring.step(sent[1])
+        return sent
+
+    def ring_arrived(arrived):
+        return arrived
+
+    def ring_back(back):
+        ffn_ring.step(back[0])
+        return back
+
+    def ring_returned(returned):
+        ffn_ring.step(returned[1])
+        return returned
+
+    def same(values):
+        return values
+
+    first = forward(None, False, [ring_sent, ring_arrived, ring_back, ring_returned])
+    ffn = ffn_ring.lists()
+
+    def hop(values, backward):
+        return lax.ppermute(values, SECTION, [(1, 0)] if backward else [(0, 1)])
+
+    upstream = [gather_in(hold(cotangent, first.output), j) for j in range(2)]
+    state = forward(
+        hop(first.output, False), True, [same, lambda arrived: hold(arrived, upstream), same, same]
+    )
+    acts = give_back(state.output)
+
+    def backward(hopped, keep, ties, terms, between):
+        out = feed_back_kernel(count, segment, upstream, hopped, state, attn, ffn, idx, keep)
+        sent, grad_middle, kept = out[:SEATS], out[SEATS], out[SEATS + 1 :]
+        arrived = exchange(sent)
+        if keep:
+            ties = ties + terms(kept)
+        back = attend_back_kernel(
+            count, segment, state.arrived, arrived, state.attended, state.total, at, ties
+        )
+        returned = exchange(between[0](back))
+        low, *last = project_back_kernel(
+            count, segment, between[1](returned), grad_middle, kept[3] if keep else None, state, attn,
+            idx, keep,
+        )
+        return low, kept, last
+
+    early, _, _ = backward(None, False, [acts], None, [same, same])
+    rings = []
+
+    def ffn_terms(kept):
+        terms = ffn_terms_kernel(count, [kept[0], swap(kept[1], REPLICA)], idx)
+        rings.append(ScatterRing(terms, count, False))
+        rings[0].step()
+        return [terms[0]]
+
+    def ring_step(values):
+        rings[0].step(values[1])
+        return values
+
+    low, kept, last = backward(hop(early, True), True, [], ffn_terms, [ring_step, ring_step])
+    rings[0].step(low)
+    terms = attn_terms_kernel(count, [last[1], swap(last[2], REPLICA)], [last[3]], [kept[2]], idx)
+    rings.append(ScatterRing(terms, count, True))
+    for _ in range(half):
+        rings[1].step()
+    in_grads = give_back(hold(last[0].astype(LOW), low)).astype(F32)
+
+    def finished(ring):
+        total = ring.total().astype(LOW)
+        twin = swap(total, REPLICA)
+        return (
+            jnp.where(replica == 0, total, twin).astype(F32),
+            jnp.where(replica == 0, twin, total).astype(F32),
+        )
+
+    ffn_total, attn_total = finished(rings[0]), finished(rings[1])
+    fc_grad = jnp.concatenate([ffn_total[0][b * rows : (b + 1) * rows] for b in range(4)], axis=1)
+    qkv_grad = jnp.concatenate(
+        [attn_total[0][:rows], attn_total[0][rows : 2 * rows], attn_total[1][:rows]], axis=1
+    )
+    note = attn_total[0][2 * rows :] + attn_total[1][2 * rows :]
+    vec = note[:8, :rows]
+    return (
+        acts, in_grads, vec[0:2][None], vec[2:4][None], qkv_grad[None], vec[4:6][None],
+        attn_total[1][rows : 2 * rows][None], vec[6][None], fc_grad[None],
+        note[NOTE - 1, : 4 * rows][None], ffn_total[1][None], vec[7][None],
+    )
+
+
+def on_each(tokens, *others):
+    count = lax.axis_size(SHARD)
+    tiles = (tokens.shape[2] // count) % 32 == 0 and tokens.shape[1] % 64 == 0
+    seats = count == 2 * SEATS and tokens.shape[0] == 2 and HEADS == 3 * SEATS
+    return (fast_device if tiles and seats else on_device)(tokens, *others)
+
+
 def solution(mesh):
     in_specs = (
-        P("replica", "shard", None),
-        P("replica", "shard", None),
-        P("replica", None),
-        P("section", None, "shard"),
-        P("section", None, "shard"),
-        P("section", "shard", None),
-        P("section", None, "shard"),
-        P("section", "shard", None),
-        P("section", "shard"),
-        P("section", "shard", None),
-        P("section", "shard"),
-        P("section", "shard", None),
-        P("section", "shard"),
+        P(REPLICA, SHARD, None),
+        P(REPLICA, SHARD, None),
+        P(REPLICA, None),
+        P(SECTION, None, SHARD),
+        P(SECTION, None, SHARD),
+        P(SECTION, SHARD, None),
+        P(SECTION, None, SHARD),
+        P(SECTION, SHARD, None),
+        P(SECTION, SHARD),
+        P(SECTION, SHARD, None),
+        P(SECTION, SHARD),
+        P(SECTION, SHARD, None),
+        P(SECTION, SHARD),
     )
     out_specs = (
-        P("section", "replica", "shard", None),
-        P("section", "replica", "shard", None),
-        P("section", None, "shard"),
-        P("section", None, "shard"),
-        P("section", "shard", None),
-        P("section", None, "shard"),
-        P("section", "shard", None),
-        P("section", "shard"),
-        P("section", "shard", None),
-        P("section", "shard"),
-        P("section", "shard", None),
-        P("section", "shard"),
+        P(SECTION, REPLICA, SHARD, None),
+        P(SECTION, REPLICA, SHARD, None),
+        P(SECTION, None, SHARD),
+        P(SECTION, None, SHARD),
+        P(SECTION, SHARD, None),
+        P(SECTION, None, SHARD),
+        P(SECTION, SHARD, None),
+        P(SECTION, SHARD),
+        P(SECTION, SHARD, None),
+        P(SECTION, SHARD),
+        P(SECTION, SHARD, None),
+        P(SECTION, SHARD),
     )
     return jax.shard_map(
-        on_device, mesh=mesh, in_specs=in_specs, out_specs=out_specs, check_vma=False
-    )
+        on_each, mesh=mesh, in_specs=in_specs, out_specs=out_specs, check_vma=False
+    )

time: 887 us -> 455 us (0.51)
  local copies, waits for them, and re-layouts: 276 us -> 20.4 us
  Pallas kernels: 0 us -> 125 us
  matrix products: 112 us -> 0 us
  other arithmetic: 89.9 us -> 13.2 us
  starting transfers between devices: 147 us -> 72 us
  between operations: 32.5 us -> 1.94 us
    pallas_call x0 -> x14, Pallas kernels: none -> 125 us  [call(): pl.pallas_call(body, in_specs=specs, out_specs=[VMEM if space is None els...]
    dot_general x48 -> x0, matrix products: 112 us -> none  [the longest x12 30 us: dot_rows(): return jnp.einsum('ta,tb->ab', a, b, preferred_element_type=F32)]
    dynamic_update_slice x61 -> x0, local copies, waits for them, and re-layouts: 77 us -> none  [the longest x32 42.4 us: gathered(): lax.dynamic_update_slice(buffer, twin[None, None], (1 - replica, at, 0, 0))]
    unnamed x428 -> x170, local copies, waits for them, and re-layouts: 68.5 us -> 12.8 us
    slice x56 -> x7, local copies, waits for them, and re-layouts: 56.8 us -> 4.19 us  [the longest x2 1.83 us: give_back(): x[j * segment:(j + 1) * segment]]
    all_to_all x8 -> x0, starting transfers between devices: 36.9 us -> none  [exchange(): lax.all_to_all(blocks, ('replica', 'shard'), 0, 0, tiled=True, axis_index...]
    reshape x36 -> x0, local copies, waits for them, and re-layouts: 33.6 us -> none  [the longest x8 8.99 us: scatter_units(): values.reshape(self.units, self.count, self.part, HEAD)]
    ppermute x70 -> x54, starting transfers between devices: 87 us -> 55.1 us  [the longest x6 9.86 us: step(): near = lax.ppermute(near, SHARD, self.right)]
  transfers between devices with their start and end apart: 122 -> 82, of which waited for: 45 -> 39; matrix products, arithmetic and copies ran while one was open for 50% -> 3% of each run, Pallas kernels for 0% -> 11%
where the time goes in v2:
time: 455 us; the launch traced here: 446 us
  waiting for transfers between devices  214 us (47%)
  Pallas kernels  125 us (27%)
  starting transfers between devices  72 us (16%)
  local copies, waits for them, and re-layouts  20.4 us (4%)
  other arithmetic  13.2 us (3%)
    pallas_call x14, Pallas kernels, call(): pl.pallas_call(body, in_specs=specs, out_specs=[VMEM if space is None els...  125 us
    ppermute x8, waiting for transfers between devices, exchange(): lax.ppermute(parts[3], (REPLICA, SHARD), diagonal)  68.2 us
    ppermute x8, waiting for transfers between devices, exchange(): lax.ppermute(parts[1], SHARD, [(s, s ^ 1) for s in range(count)])  47.4 us
    ppermute x2, waiting for transfers between devices, hop(): return lax.ppermute(values, SECTION, [(1, 0)] if backward else [(0, 1)])  21.4 us
    ppermute x6, waiting for transfers between devices, step(): lax.ppermute(first, SHARD, self.right)  21.2 us
    ppermute x28, starting transfers between devices, swap(): return lax.ppermute(x, axis, [(0, 1), (1, 0)])  16.9 us
    ppermute x6, waiting for transfers between devices, step(): lax.ppermute(second, SHARD, self.left)  15 us
    unnamed x170, local copies, waits for them, and re-layouts  12.8 us
  transfers between devices with their start and end apart: 82, of which 39 were waited for; matrix products, arithmetic and copies ran while one was open for 3% of the time, Pallas kernels for 11%

profile of v2, /device:TPU:0, one launch (start us, length us, event | category | flops | bytes accessed | tf_op | source)
XLA Modules:
  0.0 446.4 jit_solution(17171039538048700257)
XLA Ops:
  6.5 7.4 %collective-permute-done.5.rest_7_.rest_11_.rest_8_.rest_14_ = bf16[208,768]{1,0:T(8,128)(2,1)S(1)} collective-permute-done((bf16[208,768]{1,0:T(8,128)(2,1)S(1)}, bf16[208,768]{1,0:T(8,128)(2,1)S(1)}, u32[]{:S(2)}, u32[]{:S(2)}) %collective-permute-start.5) | collective-permute-done | bytes 319520 | tf_op jit(solution)/shard_map/ppermute | solution.py:1369
  24.7 4.6 %collective-permute-done.1.second = bf16[128,768]{1,0:T(8,128)(2,1)S(1)} collective-permute-done((bf16[128,768]{1,0:T(8,128)(2,1)S(1)}, bf16[128,768]{1,0:T(8,128)(2,1)S(1)}, u32[]{:S(2)}, u32[]{:S(2)}) %collective-permute-start.1) | collective-permute-done | bytes 196640 | tf_op jit(solution)/shard_map/ppermute | solution.py:1447
  29.2 6.6 %collective-permute-start.16 = (bf16[208,768]{1,0:T(8,128)(2,1)S(1)}, bf16[208,768]{1,0:T(8,128)(2,1)S(1)}, u32[]{:S(2)}, u32[]{:S(2)}) collective-permute-start(bf16[208,768]{1,0:T(8,128)(2,1)S(1)} %collective-permute-done.5.rest_7_.rest_11_.rest_8_.rest_14_), channel_id=1, source_target_pairs={{0,8},{8,0},{1,9},{9,1},{2,10},{10,2},{3,11},{11,3},{4,12},{12,4},... | collective-permute-start | bytes 958472 | tf_op jit(solution)/shard_map/ppermute | solution.py:79
  51.9 6.7 %shard_map.238 = (bf16[2,576,128]{2,1,0:T(8,128)(2,1)}, bf16[2,576,128]{2,1,0:T(8,128)(2,1)}, bf16[2,576,128]{2,1,0:T(8,128)(2,1)}, bf16[2,576,128]{2,1,0:T(8,12...) custom-call(s32[14]{0:T(128)} %pad_add_fusion.idx, bf16[144,768]{1,0:T(8,128)(2,1)} %collective-permute-done.first, ...), custom_call_target="tpu_custom_call" | custom-call | bytes 25830000 | tf_op jit(solution)/shard_map/pallas_call | solution.py:567
  66.4 22.2 %collective-permute-done.21.rest_3_ = bf16[2,576,128]{2,1,0:T(8,128)(2,1)S(1)} collective-permute-done((bf16[2,576,128]{2,1,0:T(8,128)(2,1)}, bf16[2,576,128]{2,1,0:T(8,128)(2,1)S(1)}, u32[]{:S(2)}, u32[]{:S(2)}) %collective-permute-start.21) | collective-permute-done | bytes 294944 | tf_op jit(solution)/shard_map/ppermute | solution.py:1464
  90.1 6.3 %shard_map.239 = (bf16[2,192,128]{2,1,0:T(8,128)(2,1)}, bf16[2,192,128]{2,1,0:T(8,128)(2,1)}, bf16[2,192,128]{2,1,0:T(8,128)(2,1)}, bf16[2,192,128]{2,1,0:T(8,128)(2,1)}) custom-call(s32[8]{0:T(128)} %select_reduce_fusion.at, bf16[2,576,128]{2,1,0:T(8,128)(2,1)} %get-tuple-element.113.rest_0_, bf16[2,576,128]{2,1,0:T(8,128)(2,1)} %copy-done.61, ...), custom_call_target="tpu_custom_call" | custom-call | bytes 33210000 | tf_op jit(solution)/shard_map/pallas_call | solution.py:567
  99.8 15.3 %collective-permute-done.22.rest_1_ = bf16[2,192,128]{2,1,0:T(8,128)(2,1)S(1)} collective-permute-done((bf16[2,192,128]{2,1,0:T(8,128)(2,1)}, bf16[2,192,128]{2,1,0:T(8,128)(2,1)S(1)}, u32[]{:S(2)}, u32[]{:S(2)}) %collective-permute-start.22) | collective-permute-done | bytes 98336 | tf_op jit(solution)/shard_map/ppermute | solution.py:1462
  117.6 13.3 %collective-permute-done.24.rest_3_ = bf16[2,192,128]{2,1,0:T(8,128)(2,1)S(1)} collective-permute-done((bf16[2,192,128]{2,1,0:T(8,128)(2,1)}, bf16[2,192,128]{2,1,0:T(8,128)(2,1)S(1)}, u32[]{:S(2)}, u32[]{:S(2)}) %collective-permute-start.24) | collective-permute-done | bytes 98336 | tf_op jit(solution)/shard_map/ppermute | solution.py:1464
  136.4 9.3 %shard_map.240 = bf16[256,768]{1,0:T(8,128)(2,1)} custom-call(s32[14]{0:T(128)} %pad_add_fusion.idx, bf16[256,768]{1,0:T(8,128)(2,1)} %get-tuple-element.106.x, f32[12,768]{1,0:T(8,128)} %get-tuple-element.107.vec, bf16[2,192,128]{2,1,0:T(8,128)(2,1)} %get-tuple-element.117.rest_0_, bf16[2,192,128]{2,1,0:T(8,128)(2,1)} %copy-done.64, ...), custom_call_target="tpu_custom_call" | custom-call | bytes 36900000 | tf_op jit(solution)/shard_map/pallas_call | solution.py:567
  149.3 8.9 %collective-permute-done.38.rest_0_ = bf16[256,768]{1,0:T(8,128)(2,1)S(1)} collective-permute-done((bf16[256,768]{1,0:T(8,128)(2,1)}, bf16[256,768]{1,0:T(8,128)(2,1)S(1)}, u32[]{:S(2)}, u32[]{:S(2)}) %collective-permute-start.38) | collective-permute-done | bytes 393248 | tf_op jit(solution)/shard_map/ppermute | solution.py:1547
  158.9 7.1 %shard_map.241 = (bf16[2,576,128]{2,1,0:T(8,128)(2,1)}, bf16[2,576,128]{2,1,0:T(8,128)(2,1)}, bf16[2,576,128]{2,1,0:T(8,128)(2,1)}, bf16[2,576,128]{2,1,0:T(8,12...) custom-call(s32[14]{0:T(128)} %pad_add_fusion.idx, ...), custom_call_target="tpu_custom_call" | custom-call | bytes 25830000 | tf_op jit(solution)/shard_map/pallas_call | solution.py:567
  169.1 7.1 %collective-permute-done.43.second = bf16[128,768]{1,0:T(8,128)(2,1)S(1)} collective-permute-done((bf16[128,768]{1,0:T(8,128)(2,1)S(1)}, bf16[128,768]{1,0:T(8,128)(2,1)S(1)}, u32[]{:S(2)}, u32[]{:S(2)}) %collective-permute-start.43) | collective-permute-done | bytes 196640 | tf_op jit(solution)/shard_map/ppermute | solution.py:1447
  176.3 4.2 collective-permute-done.41.rest_3_
  181.2 7.5 %shard_map.242 = (bf16[2,192,128]{2,1,0:T(8,128)(2,1)}, bf16[2,192,128]{2,1,0:T(8,128)(2,1)}, bf16[2,192,128]{2,1,0:T(8,128)(2,1)}, bf16[2,192,128]{2,1,0:T(8,12...) custom-call(s32[8]{0:T(128)} %select_reduce_fusion.at, bf16[2,576,128]{2,1,0:T(8,128)(2,1)} %get-tuple-element.133.rest_0_, ...), custom_call_target="tpu_custom_call" | custom-call | bytes 33210000 | tf_op jit(solution)/shard_map/pallas_call | solution.py:567
  196.7 9.9 %shard_map.243 = (bf16[256,768]{1,0:T(8,128)(2,1)}, bf16[256,768]{1,0:T(8,128)(2,1)}, f32[256,768]{1,0:T(8,128)}, bf16[256,768]{1,0:T(8,128)(2,1)}, bf16[256,307...) custom-call(s32[14]{0:T(128)} %pad_add_fusion.idx, bf16[256,768]{1,0:T(8,128)(2,1)} %get-tuple-element.126.x, ...), custom_call_target="tpu_custom_call" | custom-call | bytes 36900000 | tf_op jit(solution)/shard_map/pallas_call | solution.py:567
  208.5 13.6 %shard_map.244 = (bf16[2,192,128]{2,1,0:T(8,128)(2,1)}, bf16[2,192,128]{2,1,0:T(8,128)(2,1)}, bf16[2,192,128]{2,1,0:T(8,128)(2,1)}, bf16[2,192,128]{2,1,0:T(8,128)(2,1)}, f32[256,768]{1,0:T(8,128)}) custom-call(s32[14]{0:T(128)} %pad_add_fusion.idx, bf16[128,768]{1,0:T(8,128)(2,1)} %copy-done.36, bf16[128,768]{1,0:T(8,128)(2,1)} %copy-done.35, ...), custom_call_target="tpu_custom_call" | custom-call | bytes 51660000 | tf_op jit(solution)/shard_map/pallas_call | solution.py:567
  231.2 11.6 %shard_map.245 = (bf16[2,576,128]{2,1,0:T(8,128)(2,1)}, bf16[2,576,128]{2,1,0:T(8,128)(2,1)}, bf16[2,576,128]{2,1,0:T(8,128)(2,1)}, bf16[2,576,128]{2,1,0:T(8,128)(2,1)}) custom-call(s32[8]{0:T(128)} %select_reduce_fusion.at, f32[2,1024,128]{2,1,0:T(8,128)} %get-tuple-element.147.attended, f32[1024,128]{1,0:T(8,128)} %get-tuple-element.148.total, ...), custom_call_target="tpu_custom_call" | custom-call | bytes 51660000 | tf_op jit(solution)/shard_map/pallas_call | solution.py:567
  245.1 7.9 %collective-permute-done.52.rest_1_ = bf16[2,576,128]{2,1,0:T(8,128)(2,1)S(1)} collective-permute-done((bf16[2,576,128]{2,1,0:T(8,128)(2,1)}, bf16[2,576,128]{2,1,0:T(8,128)(2,1)S(1)}, u32[]{:S(2)}, u32[]{:S(2)}) %collective-permute-start.52) | collective-permute-done | bytes 294944 | tf_op jit(solution)/shard_map/ppermute | solution.py:1462
  253.0 4.6 %collective-permute-done.54.rest_3_ = bf16[2,576,128]{2,1,0:T(8,128)(2,1)S(1)} collective-permute-done((bf16[2,576,128]{2,1,0:T(8,128)(2,1)}, bf16[2,576,128]{2,1,0:T(8,128)(2,1)S(1)}, u32[]{:S(2)}, u32[]{:S(2)}) %collective-permute-start.54) | collective-permute-done | bytes 294944 | tf_op jit(solution)/shard_map/ppermute | solution.py:1464
  258.3 5.7 %shard_map.246 = bf16[256,768]{1,0:T(8,128)(2,1)} custom-call(s32[14]{0:T(128)} %pad_add_fusion.idx, f32[256,768]{1,0:T(8,128)} %get-tuple-element.146.grad_middle, bf16[256,768]{1,0:T(8,128)(2,1)} %get-tuple-element.126.x, f32[12,768]{1,0:T(8,128)} %get-tuple-element.127.vec, bf16[2,576,128]{2,1,0:T(8,128)(2,1)} %get-tuple-element.153.rest_0_, ...), custom_call_target="tpu_custom_call" | custom-call | bytes 29520000 | tf_op jit(solution)/shard_map/pallas_call | solution.py:567
  265.4 12.5 %collective-permute-done.55.rest_0_ = bf16[256,768]{1,0:T(8,128)(2,1)S(1)} collective-permute-done((bf16[256,768]{1,0:T(8,128)(2,1)}, bf16[256,768]{1,0:T(8,128)(2,1)S(1)}, u32[]{:S(2)}, u32[]{:S(2)}) %collective-permute-start.55) | collective-permute-done | bytes 393248 | tf_op jit(solution)/shard_map/ppermute | solution.py:1547
  278.6 15.2 %shard_map.247 = (bf16[2,192,128]{2,1,0:T(8,128)(2,1)}, bf16[2,192,128]{2,1,0:T(8,128)(2,1)}, bf16[2,192,128]{2,1,0:T(8,128)(2,1)}, bf16[2,192,128]{2,1,0:T(8,12...) custom-call(s32[14]{0:T(128)} %pad_add_fusion.idx, ...), custom_call_target="tpu_custom_call" | custom-call | bytes 51660000 | tf_op jit(solution)/shard_map/pallas_call | solution.py:567
  299.5 7.3 %shard_map.248 = (bf16[384,768]{1,0:T(8,128)(2,1)}, bf16[384,768]{1,0:T(8,128)(2,1)}, bf16[384,768]{1,0:T(8,128)(2,1)}, bf16[384,768]{1,0:T(8,128)(2,1)}, bf16[3...) custom-call(s32[14]{0:T(128)} %pad_add_fusion.idx, ...), custom_call_target="tpu_custom_call" | custom-call | bytes 29520000 | tf_op jit(solution)/shard_map/pallas_call | solution.py:567
  310.4 13.9 %collective-permute-done.56.rest_5_ = bf16[2,192,128]{2,1,0:T(8,128)(2,1)S(1)} collective-permute-done((bf16[2,192,128]{2,1,0:T(8,128)(2,1)S(1)}, bf16[2,192,128]{2,1,0:T(8,128)(2,1)S(1)}, u32[]{:S(2)}, u32[]{:S(2)}) %collective-permute-start.56) | collective-permute-done | bytes 98336 | tf_op jit(solution)/shard_map/ppermute | solution.py:1462
  326.2 11.7 %shard_map.249 = (bf16[2,576,128]{2,1,0:T(8,128)(2,1)}, bf16[2,576,128]{2,1,0:T(8,128)(2,1)}, bf16[2,576,128]{2,1,0:T(8,128)(2,1)}, bf16[2,576,128]{2,1,0:T(8,128)(2,1)}) custom-call(s32[8]{0:T(128)} %select_reduce_fusion.at, f32[2,1024,128]{2,1,0:T(8,128)} %get-tuple-element.147.attended, f32[1024,128]{1,0:T(8,128)} %get-tuple-element.148.total, ...), custom_call_target="tpu_custom_call" | custom-call | bytes 51660000 | tf_op jit(solution)/shard_map/pallas_call | solution.py:567
  342.9 17.2 %collective-permute-done.62.rest_6_ = bf16[2,576,128]{2,1,0:T(8,128)(2,1)S(1)} collective-permute-done((bf16[2,576,128]{2,1,0:T(8,128)(2,1)S(1)}, bf16[2,576,128]{2,1,0:T(8,128)(2,1)S(1)}, u32[]{:S(2)}, u32[]{:S(2)}) %collective-permute-start.62) | collective-permute-done | bytes 294944 | tf_op jit(solution)/shard_map/ppermute | solution.py:1464
  360.1 6.7 %collective-permute-done.60.rest_4_ = bf16[2,576,128]{2,1,0:T(8,128)(2,1)S(1)} collective-permute-done((bf16[2,576,128]{2,1,0:T(8,128)(2,1)S(1)}, bf16[2,576,128]{2,1,0:T(8,128)(2,1)S(1)}, u32[]{:S(2)}, u32[]{:S(2)}) %collective-permute-start.60) | collective-permute-done | bytes 294944 | tf_op jit(solution)/shard_map/ppermute | solution.py:1462
  367.5 7.8 %shard_map.250 = (bf16[256,768]{1,0:T(8,128)(2,1)}, f32[256,768]{1,0:T(8,128)}, bf16[256,3072]{1,0:T(8,128)(2,1)}, bf16[256,3072]{1,0:T(8,128)(2,1)}, f32[8,768]{1,0:T(8,128)}) custom-call(s32[14]{0:T(128)} %pad_add_fusion.idx, f32[256,768]{1,0:T(8,128)} %get-tuple-element.157.grad_middle, bf16[256,768]{1,0:T(8,128)(2,1)} %get-tuple-element.126.x, ...), custom_call_target="tpu_custom_call" | custom-call | bytes 29520000 | tf_op jit(solution)/shard_map/pallas_call | solution.py:567
  381.3 10.3 %collective-permute-done.77 = bf16[384,768]{1,0:T(8,128)(2,1)S(1)} collective-permute-done((bf16[384,768]{1,0:T(8,128)(2,1)S(1)}, bf16[384,768]{1,0:T(8,128)(2,1)S(1)}, u32[]{:S(2)}, u32[]{:S(2)}) %collective-permute-start.77) | collective-permute-done | bytes 589856 | tf_op jit(solution)/shard_map/ppermute | solution.py:1407
  392.9 5.0 %shard_map.251 = (bf16[208,768]{1,0:T(8,128)(2,1)}, bf16[208,768]{1,0:T(8,128)(2,1)}, bf16[208,768]{1,0:T(8,128)(2,1)}, bf16[208,768]{1,0:T(8,128)(2,1)}, bf16[2...) custom-call(s32[14]{0:T(128)} %pad_add_fusion.idx, ...), custom_call_target="tpu_custom_call" | custom-call | bytes 18450000 | tf_op jit(solution)/shard_map/pallas_call | solution.py:567
  403.3 5.4 %collective-permute-done.66 = bf16[208,768]{1,0:T(8,128)(2,1)S(1)} collective-permute-done((bf16[208,768]{1,0:T(8,128)(2,1)}, bf16[208,768]{1,0:T(8,128)(2,1)S(1)}, u32[]{:S(2)}, u32[]{:S(2)}) %collective-permute-start.66) | collective-permute-done | bytes 319520 | tf_op jit(solution)/shard_map/ppermute | solution.py:1398
  410.0 12.3 %collective-permute-done.70 = bf16[208,768]{1,0:T(8,128)(2,1)S(1)} collective-permute-done((bf16[208,768]{1,0:T(8,128)(2,1)S(1)}, bf16[208,768]{1,0:T(8,128)(2,1)S(1)}, u32[]{:S(2)}, u32[]{:S(2)}) %collective-permute-start.70) | collective-permute-done | bytes 319520 | tf_op jit(solution)/shard_map/ppermute | solution.py:1407
  (367 shorter events, 139.1 us)
Async XLA Ops:
  16.0 19.9 %collective-permute-start = (bf16[144,768]{1,0:T(8,128)(2,1)S(1)}, bf16[144,768]{1,0:T(8,128)(2,1)}, u32[]{:S(2)}, u32[]{:S(2)}) collective-permute-start(bf16[144,768]{1,0:T(8,128)(2,1)S(1)} %fusion.6), channel_id=1, source_target_pairs={{0,0},{1,1},{2,2},{3,3},{4,8},{5,9},{6,10},{7,11},{8,4},{9,5},{10,... | collective-permute-start | bytes 663560 | tf_op jit(solution)/shard_map/ppermute | solution.py:1447
  19.1 18.6 %collective-permute-start.9 = (bf16[208,768]{1,0:T(8,128)(2,1)S(1)}, bf16[208,768]{1,0:T(8,128)(2,1)S(1)}, u32[]{:S(2)}, u32[]{:S(2)}) collective-permute-start(bf16[208,768]{1,0:T(8,128)(2,1)S(1)} %fusion.5.rest_0_.rest_4_.rest_1_.rest_7_), channel_id=1, source_target_pairs={{0,8},{8,0},{1,9},{9,1},{2,10},{10,2},{3,11},{11,3},{4,12},{12,4},... | collective-permute-start | bytes 958472 | tf_op jit(solution)/shard_map/ppermute | solution.py:79
  42.2 16.3 %collective-permute-start.18 = (bf16[384,768]{1,0:T(8,128)(2,1)}, bf16[384,768]{1,0:T(8,128)(2,1)}, u32[]{:S(2)}, u32[]{:S(2)}) collective-permute-start(bf16[384,768]{1,0:T(8,128)(2,1)} %maximum_select_fusion.rest_20_.rest_16_.rest_17_), channel_id=1, source_target_pairs={{2,0},{4,2},{6,4},{7,6},{5,7},{3,5},{1,3},{0,1},{10,8},{12,10},{14... | collective-permute-start | bytes 1769480 | tf_op jit(solution)/shard_map/ppermute | solution.py:1370
  42.3 18.3 %collective-permute-start.17 = (bf16[384,768]{1,0:T(8,128)(2,1)}, bf16[384,768]{1,0:T(8,128)(2,1)}, u32[]{:S(2)}, u32[]{:S(2)}) collective-permute-start(bf16[384,768]{1,0:T(8,128)(2,1)} %maximum_select_fusion.rest_20_.rest_16_.rest_17_), channel_id=1, source_target_pairs={{0,2},{2,4},{4,6},{6,7},{7,5},{5,3},{3,1},{1,0},{8,10},{10,12},{12... | collective-permute-start | bytes 1769480 | tf_op jit(solution)/shard_map/ppermute | solution.py:1369
  60.6 35.8 %collective-permute-start.25 = (bf16[384,768]{1,0:T(8,128)(2,1)}, bf16[384,768]{1,0:T(8,128)(2,1)S(1)}, u32[]{:S(2)}, u32[]{:S(2)}) collective-permute-start(bf16[384,768]{1,0:T(8,128)(2,1)} %collective-permute-done.18.rest_21_.rest_17_.rest_18_), channel_id=1, source_target_pairs={{2,0},{4,2},{6,4},{7,6},{5,7},{3,5},{1,3},{0,1},{10,8},{12,10},{14... | collective-permute-start | bytes 1769480 | tf_op jit(solution)/shard_map/ppermute | solution.py:1370
  62.4 34.0 %collective-permute-start.26 = (bf16[384,768]{1,0:T(8,128)(2,1)}, bf16[384,768]{1,0:T(8,128)(2,1)S(1)}, u32[]{:S(2)}, u32[]{:S(2)}) collective-permute-start(bf16[384,768]{1,0:T(8,128)(2,1)} %collective-permute-done.17.rest_27_.rest_23_.rest_24_), channel_id=1, source_target_pairs={{0,2},{2,4},{4,6},{6,7},{7,5},{5,3},{3,1},{1,0},{8,10},{10,12},{12... | collective-permute-start | bytes 1769480 | tf_op jit(solution)/shard_map/ppermute | solution.py:1369
  62.8 25.8 %collective-permute-start.19 = (bf16[2,576,128]{2,1,0:T(8,128)(2,1)}, bf16[2,576,128]{2,1,0:T(8,128)(2,1)S(1)}, u32[]{:S(2)}, u32[]{:S(2)}) collective-permute-start(bf16[2,576,128]{2,1,0:T(8,128)(2,1)} %get-tuple-element.114), channel_id=1, source_target_pairs={{0,1},{1,0},{2,3},{3,2},{4,5},{5,4},{6,7},{7,6},{8,9},{9,8},{10,11... | collective-permute-start | bytes 884744 | tf_op jit(solution)/shard_map/ppermute | solution.py:1462
  64.6 24.0 %collective-permute-start.21 = (bf16[2,576,128]{2,1,0:T(8,128)(2,1)}, bf16[2,576,128]{2,1,0:T(8,128)(2,1)S(1)}, u32[]{:S(2)}, u32[]{:S(2)}) collective-permute-start(bf16[2,576,128]{2,1,0:T(8,128)(2,1)} %get-tuple-element.116), channel_id=1, source_target_pairs={{0,9},{1,8},{2,11},{3,10},{4,13},{5,12},{6,15},{7,14},{8,1},{9,0},... | collective-permute-start | bytes 884744 | tf_op jit(solution)/shard_map/ppermute | solution.py:1464
  96.4 18.7 %collective-permute-start.27 = (bf16[384,768]{1,0:T(8,128)(2,1)S(1)}, bf16[384,768]{1,0:T(8,128)(2,1)S(1)}, u32[]{:S(2)}, u32[]{:S(2)}) collective-permute-start(bf16[384,768]{1,0:T(8,128)(2,1)S(1)} %collective-permute-done.25.rest_22_.rest_18_.rest_19_), channel_id=1, source_target_pairs={{2,0},{4,2},{6,4},{7,6},{5,7},{3,5},{1,3},{0,1},{10,8},{12,10},{14... | collective-permute-start | bytes 1769480 | tf_op jit(solution)/shard_map/ppermute | solution.py:1370
  97.6 17.6 %collective-permute-start.28 = (bf16[384,768]{1,0:T(8,128)(2,1)S(1)}, bf16[384,768]{1,0:T(8,128)(2,1)S(1)}, u32[]{:S(2)}, u32[]{:S(2)}) collective-permute-start(bf16[384,768]{1,0:T(8,128)(2,1)S(1)} %collective-permute-done.26.rest_26_.rest_22_.rest_23_), channel_id=1, source_target_pairs={{0,2},{2,4},{4,6},{6,7},{7,5},{5,3},{3,1},{1,0},{8,10},{10,12},{12... | collective-permute-start | bytes 1769480 | tf_op jit(solution)/shard_map/ppermute | solution.py:1369
  98.5 17.3 %collective-permute-start.30 = (bf16[384,768]{1,0:T(8,128)(2,1)}, bf16[384,768]{1,0:T(8,128)(2,1)S(1)}, u32[]{:S(2)}, u32[]{:S(2)}) collective-permute-start(bf16[384,768]{1,0:T(8,128)(2,1)} %maximum_select_fusion.rest_20_.rest_16_.rest_17_), channel_id=1, source_target_pairs={{0,8},{8,0},{1,9},{9,1},{2,10},{10,2},{3,11},{11,3},{4,12},{12,4},... | collective-permute-start | bytes 1769480 | tf_op jit(solution)/shard_map/ppermute | solution.py:79
  99.2 15.9 %collective-permute-start.22 = (bf16[2,192,128]{2,1,0:T(8,128)(2,1)}, bf16[2,192,128]{2,1,0:T(8,128)(2,1)S(1)}, u32[]{:S(2)}, u32[]{:S(2)}) collective-permute-start(bf16[2,192,128]{2,1,0:T(8,128)(2,1)} %get-tuple-element.118), channel_id=1, source_target_pairs={{0,1},{1,0},{2,3},{3,2},{4,5},{5,4},{6,7},{7,6},{8,9},{9,8},{10,11... | collective-permute-start | bytes 294920 | tf_op jit(solution)/shard_map/ppermute | solution.py:1462
  99.6 31.4 %collective-permute-start.31 = (bf16[384,768]{1,0:T(8,128)(2,1)}, bf16[384,768]{1,0:T(8,128)(2,1)S(1)}, u32[]{:S(2)}, u32[]{:S(2)}) collective-permute-start(bf16[384,768]{1,0:T(8,128)(2,1)} %collective-permute-done.18.rest_21_.rest_17_.rest_18_), channel_id=1, source_target_pairs={{0,8},{8,0},{1,9},{9,1},{2,10},{10,2},{3,11},{11,3},{4,12},{12,4},... | collective-permute-start | bytes 1769480 | tf_op jit(solution)/shard_map/ppermute | solution.py:79
  115.1 16.4 %collective-permute-start.37 = (bf16[384,768]{1,0:T(8,128)(2,1)}, bf16[384,768]{1,0:T(8,128)(2,1)S(1)}, u32[]{:S(2)}, u32[]{:S(2)}) collective-permute-start(bf16[384,768]{1,0:T(8,128)(2,1)} %collective-permute-done.17.rest_27_.rest_23_.rest_24_), channel_id=1, source_target_pairs={{0,8},{8,0},{1,9},{9,1},{2,10},{10,2},{3,11},{11,3},{4,12},{12,4},... | collective-permute-start | bytes 1769480 | tf_op jit(solution)/shard_map/ppermute | solution.py:79
  115.2 16.4 %collective-permute-start.29 = (bf16[384,768]{1,0:T(8,128)(2,1)S(1)}, bf16[384,768]{1,0:T(8,128)(2,1)S(1)}, u32[]{:S(2)}, u32[]{:S(2)}) collective-permute-start(bf16[384,768]{1,0:T(8,128)(2,1)S(1)} %collective-permute-done.27.rest_23_.rest_19_.rest_20_), channel_id=1, source_target_pairs={{2,0},{4,2},{6,4},{7,6},{5,7},{3,5},{1,3},{0,1},{10,8},{12,10},{14... | collective-permute-start | bytes 1769480 | tf_op jit(solution)/shard_map/ppermute | solution.py:1378
  207.8 18.3 %collective-permute-start.47 = (bf16[128,768]{1,0:T(8,128)(2,1)S(1)}, bf16[128,768]{1,0:T(8,128)(2,1)S(1)}, u32[]{:S(2)}, u32[]{:S(2)}) collective-permute-start(bf16[128,768]{1,0:T(8,128)(2,1)S(1)} %get-tuple-element.224), channel_id=1, source_target_pairs={{0,0},{1,1},{2,2},{3,3},{8,4},{9,5},{10,6},{11,7},{4,8},{5,9},{6,1... | collective-permute-start | bytes 589832 | tf_op jit(solution)/shard_map/ppermute | solution.py:1451
  208.5 17.6 %collective-permute-start.48 = (bf16[128,768]{1,0:T(8,128)(2,1)S(1)}, bf16[128,768]{1,0:T(8,128)(2,1)S(1)}, u32[]{:S(2)}, u32[]{:S(2)}) collective-permute-start(bf16[128,768]{1,0:T(8,128)(2,1)S(1)} %get-tuple-element.225), channel_id=1, source_target_pairs={{2,0},{3,1},{0,2},{1,3},{10,4},{11,5},{8,6},{9,7},{6,8},{7,9},{4,1... | collective-permute-start | bytes 589832 | tf_op jit(solution)/shard_map/ppermute | solution.py:1451
  306.8 31.1 %collective-permute-start.74 = (bf16[384,768]{1,0:T(8,128)(2,1)}, bf16[384,768]{1,0:T(8,128)(2,1)S(1)}, u32[]{:S(2)}, u32[]{:S(2)}) collective-permute-start(bf16[384,768]{1,0:T(8,128)(2,1)} %get-tuple-element.191), channel_id=1, source_target_pairs={{2,0},{4,2},{6,4},{7,6},{5,7},{3,5},{1,3},{0,1},{10,8},{12,10},{14... | collective-permute-start | bytes 1769480 | tf_op jit(solution)/shard_map/ppermute | solution.py:1400
  308.2 16.0 %collective-permute-start.56 = (bf16[2,192,128]{2,1,0:T(8,128)(2,1)S(1)}, bf16[2,192,128]{2,1,0:T(8,128)(2,1)S(1)}, u32[]{:S(2)}, u32[]{:S(2)}) collective-permute-start(bf16[2,192,128]{2,1,0:T(8,128)(2,1)S(1)} %copy-done.82), channel_id=1, source_target_pairs={{0,1},{1,0},{2,3},{3,2},{4,5},{5,4},{6,7},{7,6},{8,9},{9,8},{10,11... | collective-permute-start | bytes 294920 | tf_op jit(solution)/shard_map/ppermute | solution.py:1462
  310.1 15.4 %collective-permute-start.58 = (bf16[2,192,128]{2,1,0:T(8,128)(2,1)S(1)}, bf16[2,192,128]{2,1,0:T(8,128)(2,1)S(1)}, u32[]{:S(2)}, u32[]{:S(2)}) collective-permute-start(bf16[2,192,128]{2,1,0:T(8,128)(2,1)S(1)} %copy-done.80), channel_id=1, source_target_pairs={{0,9},{1,8},{2,11},{3,10},{4,13},{5,12},{6,15},{7,14},{8,1},{9,0},... | collective-permute-start | bytes 294920 | tf_op jit(solution)/shard_map/ppermute | solution.py:1464
  338.1 37.3 %collective-permute-start.75 = (bf16[384,768]{1,0:T(8,128)(2,1)}, bf16[384,768]{1,0:T(8,128)(2,1)S(1)}, u32[]{:S(2)}, u32[]{:S(2)}) collective-permute-start(bf16[384,768]{1,0:T(8,128)(2,1)} %get-tuple-element.192), channel_id=1, source_target_pairs={{0,2},{2,4},{4,6},{6,7},{7,5},{5,3},{3,1},{1,0},{8,10},{10,12},{12... | collective-permute-start | bytes 1769480 | tf_op jit(solution)/shard_map/ppermute | solution.py:1407
  338.9 21.2 %collective-permute-start.62 = (bf16[2,576,128]{2,1,0:T(8,128)(2,1)S(1)}, bf16[2,576,128]{2,1,0:T(8,128)(2,1)S(1)}, u32[]{:S(2)}, u32[]{:S(2)}) collective-permute-start(bf16[2,576,128]{2,1,0:T(8,128)(2,1)S(1)} %copy-done.78), channel_id=1, source_target_pairs={{0,9},{1,8},{2,11},{3,10},{4,13},{5,12},{6,15},{7,14},{8,1},{9,0},... | collective-permute-start | bytes 884744 | tf_op jit(solution)/shard_map/ppermute | solution.py:1464
  340.8 25.9 %collective-permute-start.60 = (bf16[2,576,128]{2,1,0:T(8,128)(2,1)S(1)}, bf16[2,576,128]{2,1,0:T(8,128)(2,1)S(1)}, u32[]{:S(2)}, u32[]{:S(2)}) collective-permute-start(bf16[2,576,128]{2,1,0:T(8,128)(2,1)S(1)} %copy-done.77), channel_id=1, source_target_pairs={{0,1},{1,0},{2,3},{3,2},{4,5},{5,4},{6,7},{7,6},{8,9},{9,8},{10,11... | collective-permute-start | bytes 884744 | tf_op jit(solution)/shard_map/ppermute | solution.py:1462
  341.2 34.3 %collective-permute-start.76 = (bf16[384,768]{1,0:T(8,128)(2,1)S(1)}, bf16[384,768]{1,0:T(8,128)(2,1)S(1)}, u32[]{:S(2)}, u32[]{:S(2)}) collective-permute-start(bf16[384,768]{1,0:T(8,128)(2,1)S(1)} %add_convert_fusion.5), channel_id=1, source_target_pairs={{2,0},{4,2},{6,4},{7,6},{5,7},{3,5},{1,3},{0,1},{10,8},{12,10},{14... | collective-permute-start | bytes 1769480 | tf_op jit(solution)/shard_map/ppermute | solution.py:1407
  375.3 16.4 %collective-permute-start.65 = (bf16[256,3072]{1,0:T(8,128)(2,1)}, bf16[256,3072]{1,0:T(8,128)(2,1)S(1)}, u32[]{:S(2)}, u32[]{:S(2)}) collective-permute-start(bf16[256,3072]{1,0:T(8,128)(2,1)} %get-tuple-element.176), channel_id=1, source_target_pairs={{0,8},{8,0},{1,9},{9,1},{2,10},{10,2},{3,11},{11,3},{4,12},{12,4},... | collective-permute-start | bytes 4718600 | tf_op jit(solution)/shard_map/ppermute | solution.py:79
  376.6 22.6 %collective-permute-start.78 = (bf16[384,768]{1,0:T(8,128)(2,1)S(1)}, bf16[384,768]{1,0:T(8,128)(2,1)S(1)}, u32[]{:S(2)}, u32[]{:S(2)}) collective-permute-start(bf16[384,768]{1,0:T(8,128)(2,1)S(1)} %add_convert_fusion.3), channel_id=1, source_target_pairs={{2,0},{4,2},{6,4},{7,6},{5,7},{3,5},{1,3},{0,1},{10,8},{12,10},{14... | collective-permute-start | bytes 1769480 | tf_op jit(solution)/shard_map/ppermute | solution.py:1407
  379.4 22.3 %collective-permute-start.63 = (bf16[128,768]{1,0:T(8,128)(2,1)}, bf16[128,768]{1,0:T(8,128)(2,1)S(1)}, u32[]{:S(2)}, u32[]{:S(2)}) collective-permute-start(bf16[128,768]{1,0:T(8,128)(2,1)} %get-tuple-element.220), channel_id=1, source_target_pairs={{0,0},{1,1},{2,2},{3,3},{8,4},{9,5},{10,6},{11,7},{4,8},{5,9},{6,1... | collective-permute-start | bytes 589832 | tf_op jit(solution)/shard_map/ppermute | solution.py:1451
  381.1 21.2 %collective-permute-start.64 = (bf16[128,768]{1,0:T(8,128)(2,1)}, bf16[128,768]{1,0:T(8,128)(2,1)}, u32[]{:S(2)}, u32[]{:S(2)}) collective-permute-start(bf16[128,768]{1,0:T(8,128)(2,1)} %get-tuple-element.221), channel_id=1, source_target_pairs={{2,0},{3,1},{0,2},{1,3},{10,4},{11,5},{8,6},{9,7},{6,8},{7,9},{4,1... | collective-permute-start | bytes 589832 | tf_op jit(solution)/shard_map/ppermute | solution.py:1451
  399.3 23.2 %collective-permute-start.79 = (bf16[384,768]{1,0:T(8,128)(2,1)S(1)}, bf16[384,768]{1,0:T(8,128)(2,1)S(1)}, u32[]{:S(2)}, u32[]{:S(2)}) collective-permute-start(bf16[384,768]{1,0:T(8,128)(2,1)S(1)} %add_convert_fusion.2), channel_id=1, source_target_pairs={{0,2},{2,4},{4,6},{6,7},{7,5},{5,3},{3,1},{1,0},{8,10},{10,12},{12... | collective-permute-start | bytes 1769480 | tf_op jit(solution)/shard_map/ppermute | solution.py:1407
  401.7 20.8 %collective-permute-start.80 = (bf16[384,768]{1,0:T(8,128)(2,1)S(1)}, bf16[384,768]{1,0:T(8,128)(2,1)S(1)}, u32[]{:S(2)}, u32[]{:S(2)}) collective-permute-start(bf16[384,768]{1,0:T(8,128)(2,1)S(1)} %add_convert_fusion.1), channel_id=1, source_target_pairs={{2,0},{4,2},{6,4},{7,6},{5,7},{3,5},{1,3},{0,1},{10,8},{12,10},{14... | collective-permute-start | bytes 1769480 | tf_op jit(solution)/shard_map/ppermute | solution.py:1407
  401.7 20.6 %collective-permute-start.70 = (bf16[208,768]{1,0:T(8,128)(2,1)S(1)}, bf16[208,768]{1,0:T(8,128)(2,1)S(1)}, u32[]{:S(2)}, u32[]{:S(2)}) collective-permute-start(bf16[208,768]{1,0:T(8,128)(2,1)S(1)} %copy-done.76), channel_id=1, source_target_pairs={{2,0},{4,2},{6,4},{7,6},{5,7},{3,5},{1,3},{0,1},{10,8},{12,10},{14... | collective-permute-start | bytes 958472 | tf_op jit(solution)/shard_map/ppermute | solution.py:1407
  408.8 17.3 %collective-permute-start.67 = (bf16[208,768]{1,0:T(8,128)(2,1)S(1)}, bf16[208,768]{1,0:T(8,128)(2,1)S(1)}, u32[]{:S(2)}, u32[]{:S(2)}) collective-permute-start(bf16[208,768]{1,0:T(8,128)(2,1)S(1)} %add_convert_fusion.11), channel_id=1, source_target_pairs={{0,2},{2,4},{4,6},{6,7},{7,5},{5,3},{3,1},{1,0},{8,10},{10,12},{12... | collective-permute-start | bytes 958472 | tf_op jit(solution)/shard_map/ppermute | solution.py:1407
  (135 other events, 1227.2 us)

commit v3 on v2

--- a/solution.py
+++ b/solution.py
@@ -545,7 +545,7 @@
 VMEM = pl.BlockSpec(memory_space=pltpu.VMEM)
 SMEM = pl.BlockSpec(memory_space=pltpu.SMEM)
 PAIR = 2 * HEAD
-VMEM_LIMIT = 60 * 2**20
+VMEM_LIMIT = 24 * 2**20
 MEMORY_RATE = 3.69e6
 
 
@@ -567,8 +567,11 @@
     return pl.pallas_call(
         body,
         in_specs=specs,
-        out_specs=[VMEM if space is None else ANY for _, _, space in outs],
-        out_shape=[jax.ShapeDtypeStruct(shape, kind) for shape, kind, _ in outs],
+        out_specs=[ANY if space is True else VMEM for _, _, space in outs],
+        out_shape=[
+            {None: jax.ShapeDtypeStruct, True: pltpu.HBM, False: pltpu.VMEM}[space](shape, kind)
+            for shape, kind, space in outs
+        ],
         scratch_shapes=spare + scratch,
         compiler_params=pltpu.CompilerParams(vmem_limit_bytes=VMEM_LIMIT),
         cost_estimate=pl.CostEstimate(
@@ -752,42 +755,71 @@
     return [total[:8]] + lines
 
 
-def project_kernel(count, segment, inputs, hopped, attn, idx, keep):
+def flatten(rings):
+    chunks = [chunk for lists in rings for chunks in lists for chunk in chunks]
+    return [pltpu.with_memory_space_constraint(chunk, pltpu.HBM) for chunk in chunks]
+
+
+def load_projections(loader, idx, count, rows, chunks, wq, wk, wv, notes):
+    first = [(0, rows, wq, 0), (rows, NOTE, notes, 3)]
+    loader.load(idx, count, chunks[:count], chunks[count : 2 * count], [first, [(0, rows, wv, 2)]])
+    loader.load(idx, count, chunks[2 * count : 3 * count], chunks[3 * count :], [[(0, rows, wk, 1)], []])
+
+
+def load_output(loader, idx, count, rows, chunks, wo):
+    loader.load(idx, count, chunks[2 * count : 3 * count], chunks[3 * count : 4 * count], [[], [(0, rows, wo, 5)]])
+
+
+def load_feed(loader, idx, count, rows, chunks, wf, wp):
+    for pair in range(2):
+        own, twin = [chunks[(2 * pair + i) * count : (2 * pair + i + 1) * count] for i in range(2)]
+        loader.load(
+            idx, count, own, twin,
+            [
+                [(i * rows, rows, wf.at[2 * pair + i], 2 * pair + i) for i in range(2)],
+                [(i * rows, rows, wp.at[:, 2 * pair + i], 4) for i in range(2)],
+            ],
+        )
+
+
+def project_kernel(count, segment, inputs, hopped, attn, idx):
     width = inputs[0].shape[1]
     rows = width // count
     given = [] if hopped is None else [hopped]
     tall = block_rows(segment)
+    loading = hopped is None
 
     def body(idx, first, second, *rest):
         arrived, rest = rest[: len(given)], rest[len(given) :]
-        chunks, rest = rest[: 2 * count], rest[2 * count :]
-        outs, rest = rest[:SEATS], rest[SEATS:]
-        vec, chosen, normed, blocks, wq, wk, wv, notes, sems, out_sems = rest
-        loader = Loader(sems)
-        loader.load(
-            idx, count, chunks[:count], chunks[count:],
-            [
-                [(0, rows, wq, 0), (rows, rows, wk, 1), (2 * rows, NOTE, notes, 3)],
-                [(0, rows, wv, 2)],
-            ],
-        )
+        if loading:
+            chunks, rest = rest[: 4 * count], rest[4 * count :]
+            outs, (chosen, wq, wk, wv, vec, blocks, normed, notes, sems, out_sems) = rest[:SEATS], rest[SEATS:]
+            loader = Loader(sems)
+            load_projections(loader, idx, count, rows, chunks, wq, wk, wv, notes)
+        else:
+            (wq, wk, wv, vec), rest = rest[:4], rest[4:]
+            outs, (chosen, normed, blocks, out_sems) = rest[:SEATS], rest[SEATS:]
         values = jnp.concatenate([first[:segment], second[:segment]], axis=0).astype(F32)
         if given:
             values = jnp.where(idx[count + 1] == 0, values, arrived[0][...].astype(F32))
         chosen[...] = values.astype(LOW)
         hat, _ = centre(values)
-        loader.wait(3)
-        lines = read_notes([notes[s] for s in range(count)], count, width)
-        vec[0:8] = lines[0]
-        for b in range(4):
-            vec[8 + b : 9 + b] = lines[1 + b]
+        if loading:
+            loader.wait(3)
+            lines = read_notes([notes[s] for s in range(count)], count, width)
+            vec[0:8] = lines[0]
+            for b in range(4):
+                vec[8 + b : 9 + b] = lines[1 + b]
         low = (hat * vec[0:1] + vec[2:3]).astype(LOW)
         normed[...] = low
-        loader.wait(0)
+        if loading:
+            loader.wait(0)
         queries = mm(low, flat(wq)) + vec[4:5]
-        loader.wait(1)
+        if loading:
+            loader.wait(1)
         keys = mm(low, flat(wk))
-        loader.wait(2)
+        if loading:
+            loader.wait(2)
         values = mm(low, flat(wv)) + vec[5:6]
         for d in range(SEATS):
             (qp, qs), (kp, ks), (vp, vs) = [tiles_of(x, d) for x in (queries, keys, values)]
@@ -799,19 +831,26 @@
                 blocks[d, p, 4 * segment :] = fold(vs[span], d).astype(LOW)
         wait_all(to_seats(blocks, outs, idx, count, out_sems))
 
-    weight = pltpu.VMEM((count, rows, width), LOW)
-    return call(
-        body, 7, [idx, *inputs, *given, *attn[0], *attn[1]],
-        [SMEM, VMEM, VMEM] + [VMEM] * len(given) + [ANY] * (2 * count),
-        [((2, tall, PAIR), LOW, True)] * SEATS
-        + [((12, width), F32, None), ((2 * segment, width), LOW, None)],
-        [
-            pltpu.VMEM((SEATS, 2, tall, PAIR), LOW), weight, weight, weight,
-            pltpu.VMEM((count, NOTE, width), LOW), pltpu.SemaphoreType.DMA((4 * count,)),
-            pltpu.SemaphoreType.DMA((SEATS,)),
-        ],
-        [((2 * segment, width), LOW, None)], keep,
-    )
+    weight = ((count, rows, width), LOW, False)
+    tokens = ((2 * segment, width), LOW, None)
+    stay = ((2 * segment, width), LOW, False)
+    blocks = pltpu.VMEM((SEATS, 2, tall, PAIR), LOW)
+    sent = [((2, tall, PAIR), LOW, True)] * SEATS
+    if loading:
+        out = call(
+            body, 7, [idx, *inputs, *flatten(attn)], [SMEM, VMEM, VMEM] + [ANY] * (4 * count),
+            sent + [tokens, weight, weight, weight, ((12, width), F32, None)],
+            [
+                blocks, pltpu.VMEM((2 * segment, width), LOW), pltpu.VMEM((count, NOTE, width), LOW),
+                pltpu.SemaphoreType.DMA((4 * count,)), pltpu.SemaphoreType.DMA((SEATS,)),
+            ],
+        )
+        return out[:SEATS], out[SEATS], None, out[SEATS + 1 :]
+    out = call(
+        body, 7, [idx, *inputs, *given, *attn], [SMEM] + [VMEM] * (2 + len(given) + 4),
+        sent + [stay, stay], [blocks, pltpu.SemaphoreType.DMA((SEATS,))],
+    )
+    return out[:SEATS], out[SEATS], out[SEATS + 1], attn
 
 
 def read_heads(blocks, segment):
@@ -903,7 +942,7 @@
             pltpu.VMEM((count, tall, PAIR), LOW), pltpu.VMEM((count, short, PAIR), LOW),
             pltpu.SemaphoreType.DMA((2 * SEATS,)), pltpu.SemaphoreType.DMA((2 * SEATS,)),
         ],
-        [((2, length, PAIR), F32, None), ((length, PAIR), F32, None)], keep,
+        [((2, length, PAIR), F32, False), ((length, PAIR), F32, False)], keep,
     )
 
 
@@ -990,60 +1029,55 @@
     )
 
 
-def feed_kernel(count, segment, returned, inputs, vec, attn, ffn, idx, keep):
+def feed_rows(mid, vec, wf, wp, active, slope, wait):
+    width = mid.shape[1]
+    hat, scale = centre(mid)
+    low = (hat * vec[1:2] + vec[3:4]).astype(LOW)
+    for b in range(4):
+        wait(b)
+        span = slice(b * width, (b + 1) * width)
+        u = mm(low, flat(wf.at[b])) + vec[8 + b : 9 + b]
+        square = u * u
+        t = jnp.tanh(u * (GELU_A + GELU_A * GELU_B * square))
+        half = 0.5 + 0.5 * t
+        active[:, span] = (u * half).astype(LOW)
+        if slope is not None:
+            slope[:, span] = (
+                half + u * (0.5 - 0.5 * t * t) * (GELU_A + 3.0 * GELU_A * GELU_B * square)
+            ).astype(LOW)
+    wait(4)
+    return low, hat, scale, (mid + mm(active[...], flat(wp)) + vec[7:8]).astype(LOW)
+
+
+def feed_kernel(count, segment, returned, inputs, vec, rings, idx):
     width = inputs.shape[1]
     rows, tokens = width // count, 2 * segment
     short = segment + segment // 2
 
     def body(idx, x, vec, *rest):
-        back, rest = rest[:SEATS], rest[SEATS:]
-        chunks, rest = rest[: 4 * count], rest[4 * count :]
-        output, attended, middle, normed, slope, active, blocks, wo, wf, wp, sems, in_sems = rest
+        back, chunks, rest = rest[:SEATS], rest[SEATS : SEATS + 8 * count], rest[SEATS + 8 * count :]
+        output, wo, wf, wp, blocks, active, sems, in_sems = rest
+        loader = Loader(sems)
         copies = from_seats(back, blocks, idx, count, in_sems)
-        loader = Loader(sems)
-        loader.load(idx, count, chunks[:count], chunks[count : 2 * count], [[], [(rows, rows, wo, 5)]])
-        loader.load(
-            idx, count, chunks[2 * count : 3 * count], chunks[3 * count :],
-            [[(b * rows, rows, wf.at[b], b) for b in range(4)], [(b * rows, rows, wp.at[:, b], 4) for b in range(4)]],
-        )
+        load_output(loader, idx, count, rows, chunks, wo)
+        load_feed(loader, idx, count, rows, chunks[4 * count :], wf, wp)
         wait_all(copies)
         low = read_returned(blocks, segment).astype(LOW)
-        attended[...] = low
         loader.wait(5)
         mid = x[...].astype(F32) + mm(low, flat(wo)) + vec[6:7]
-        middle[...] = mid
-        hat, _ = centre(mid)
-        low = (hat * vec[1:2] + vec[3:4]).astype(LOW)
-        normed[...] = low
-        for b in range(4):
-            loader.wait(b)
-            span = slice(b * width, (b + 1) * width)
-            u = mm(low, flat(wf.at[b])) + vec[8 + b : 9 + b]
-            square = u * u
-            t = jnp.tanh(u * (GELU_A + GELU_A * GELU_B * square))
-            half = 0.5 + 0.5 * t
-            active[:, span] = (u * half).astype(LOW)
-            if keep:
-                slope[:, span] = (
-                    half + u * (0.5 - 0.5 * t * t) * (GELU_A + 3.0 * GELU_A * GELU_B * square)
-                ).astype(LOW)
-        loader.wait(4)
-        output[...] = (mid + mm(active[...], flat(wp)) + vec[7:8]).astype(LOW)
+        output[...] = feed_rows(mid, vec, wf, wp, active, None, loader.wait)[3]
 
     return call(
-        body, 10, [idx, inputs, vec, *returned, *attn[0], *attn[1], *ffn[0], *ffn[1]],
-        [SMEM, VMEM, VMEM] + [ANY] * (SEATS + 4 * count),
-        [((tokens, width), LOW, None)],
+        body, 10, [idx, inputs, vec, *returned, *flatten(rings)],
+        [SMEM, VMEM, VMEM] + [ANY] * (SEATS + 8 * count),
         [
-            pltpu.VMEM((SEATS, 2, short, PAIR), LOW), pltpu.VMEM((count, rows, width), LOW),
-            pltpu.VMEM((4, count, rows, width), LOW), pltpu.VMEM((count, 4, rows, width), LOW),
+            ((tokens, width), LOW, None), ((count, rows, width), LOW, False),
+            ((4, count, rows, width), LOW, False), ((count, 4, rows, width), LOW, False),
+        ],
+        [
+            pltpu.VMEM((SEATS, 2, short, PAIR), LOW), pltpu.VMEM((tokens, 4 * width), LOW),
             pltpu.SemaphoreType.DMA((9 * count,)), pltpu.SemaphoreType.DMA((SEATS,)),
         ],
-        [
-            ((tokens, width), LOW, None), ((tokens, width), F32, None), ((tokens, width), LOW, None),
-            ((tokens, 4 * width), LOW, None), ((tokens, 4 * width), LOW, None),
-        ],
-        keep,
     )
 
 
@@ -1057,98 +1091,128 @@
     return whole_rows(pairs, singles)
 
 
-def feed_back_kernel(count, segment, grads, hopped, saved, attn, ffn, idx, keep):
+def feed_back_rows(wide, hat, scale, slope, vec, wo, wf, wp, gh, sums, blocks, segment):
+    width = wide.shape[1]
+    branch = wide.astype(LOW)
+    weight = flat(wp)
+    back = jnp.zeros(wide.shape, F32)
+    for b in range(4):
+        span = slice(b * width, (b + 1) * width)
+        ga = mm_nt(branch, weight[span])
+        low = (ga * slope[:, span].astype(F32)).astype(LOW)
+        if sums is not None:
+            gh[:, span] = low
+            sums[3 + b : 4 + b] = jnp.sum(low.astype(F32), axis=0, keepdims=True)
+        back += mm_nt(low, flat(wf.at[b]))
+    total = wide + centre_back(back * vec[1:2], hat, scale)
+    low = total.astype(LOW)
+    values = mm_nt(low, flat(wo))
+    for d in range(SEATS):
+        pair, single = tiles_of(values, d)
+        for p in range(2):
+            part = slice(p * segment, (p + 1) * segment)
+            blocks[d, p, :segment] = pair[part].astype(LOW)
+            blocks[d, p, segment:] = fold(single[part], d).astype(LOW)
+    if sums is not None:
+        sums[0:1] = jnp.sum(back * hat, axis=0, keepdims=True)
+        sums[1:2] = jnp.sum(back, axis=0, keepdims=True)
+        sums[2:3] = jnp.sum(low.astype(F32), axis=0, keepdims=True)
+        sums[7:8] = jnp.sum(wide, axis=0, keepdims=True)
+    return total, low
+
+
+def turn_kernel(count, segment, returned, inputs, vec, weights, grads, idx):
+    width = inputs.shape[1]
+    tokens = 2 * segment
+    short = segment + segment // 2
+
+    def body(idx, x, vec, wo, wf, wp, first, second, *rest):
+        back, outs, rest = rest[:SEATS], rest[SEATS : 2 * SEATS], rest[2 * SEATS :]
+        output, attended, middle, normed, slope, active, grad_middle, blocks, in_sems, out_sems = rest
+        wait_all(from_seats(back, blocks, idx, count, in_sems))
+        low = read_returned(blocks, segment).astype(LOW)
+        attended[...] = low
+        mid = x[...].astype(F32) + mm(low, flat(wo)) + vec[6:7]
+        middle[...] = mid
+        normed[...], hat, scale, output[...] = feed_rows(
+            mid, vec, wf, wp, active, slope, lambda key: None
+        )
+        wide = jnp.concatenate([first[...], second[...]], axis=0).astype(F32)
+        grad_middle[...] = feed_back_rows(
+            wide, hat, scale, slope, vec, wo, wf, wp, None, None, blocks, segment
+        )[0]
+        wait_all(to_seats(blocks, outs, idx, count, out_sems))
+
+    rows = ((tokens, width), LOW, False)
+    return call(
+        body, 10, [idx, inputs, vec, *weights, *grads, *returned],
+        [SMEM] + [VMEM] * 7 + [ANY] * SEATS,
+        [((2, short, PAIR), LOW, True)] * SEATS
+        + [
+            ((tokens, width), LOW, None), rows, ((tokens, width), F32, False), rows,
+            ((tokens, 4 * width), LOW, False), ((tokens, 4 * width), LOW, False),
+            ((tokens, width), F32, False),
+        ],
+        [
+            pltpu.VMEM((SEATS, 2, short, PAIR), LOW), pltpu.SemaphoreType.DMA((SEATS,)),
+            pltpu.SemaphoreType.DMA((SEATS,)),
+        ],
+    )
+
+
+def feed_back_kernel(count, segment, grads, hopped, saved, weights, idx):
     width = grads[0].shape[1]
-    rows, tokens = width // count, 2 * segment
+    tokens = 2 * segment
     short = segment + segment // 2
-    given = [] if hopped is None else [hopped]
-
-    def body(idx, first, second, middle, slope, active, normed, vec, *rest):
-        arrived, rest = rest[: len(given)], rest[len(given) :]
-        chunks, rest = rest[: 4 * count], rest[4 * count :]
+
+    def body(idx, first, second, hopped, middle, slope, active, normed, vec, wo, wf, wp, *rest):
         outs, rest = rest[:SEATS], rest[SEATS:]
-        grad_middle, mine, theirs, sums, grad_out, blocks, wo, wf, wp, gh, sems, out_sems = rest
-        loader = Loader(sems)
-        loader.load(
-            idx, count, chunks[2 * count : 3 * count], chunks[3 * count :],
-            [[(b * rows, rows, wf.at[b], b) for b in range(4)], [(b * rows, rows, wp.at[:, b], 4) for b in range(4)]],
-        )
-        loader.load(idx, count, chunks[:count], chunks[count : 2 * count], [[], [(rows, rows, wo, 5)]])
-        branch = jnp.concatenate([first[...], second[...]], axis=0).astype(F32)
-        if given:
-            branch = jnp.where(idx[count + 1] == 1, branch, arrived[0][...].astype(F32))
-        wide, branch = branch, branch.astype(LOW)
-        loader.wait(4)
-        weight = flat(wp)
-        back = jnp.zeros((tokens, width), F32)
-        for b in range(4):
-            span = slice(b * width, (b + 1) * width)
-            ga = mm_nt(branch, weight[span])
-            low = (ga * slope[:, span].astype(F32)).astype(LOW)
-            gh[:, span] = low
-            if keep:
-                sums[3 + b : 4 + b] = jnp.sum(low.astype(F32), axis=0, keepdims=True)
-            loader.wait(b)
-            back += mm_nt(low, flat(wf.at[b]))
+        grad_middle, mine, theirs, sums, grad_out, blocks, gh, out_sems = rest
+        wide = jnp.concatenate([first[...], second[...]], axis=0).astype(F32)
+        wide = jnp.where(idx[count + 1] == 1, wide, hopped[...].astype(F32))
         hat, scale = centre(middle[...])
-        total = wide + centre_back(back * vec[1:2], hat, scale)
-        grad_middle[...] = total
-        low = total.astype(LOW)
-        grad_out[...] = low
-        loader.wait(5)
-        values = mm_nt(low, flat(wo))
-        for d in range(SEATS):
-            pair, single = tiles_of(values, d)
-            for p in range(2):
-                part = slice(p * segment, (p + 1) * segment)
-                blocks[d, p, :segment] = pair[part].astype(LOW)
-                blocks[d, p, segment:] = fold(single[part], d).astype(LOW)
+        grad_middle[...], grad_out[...] = feed_back_rows(
+            wide, hat, scale, slope, vec, wo, wf, wp, gh, sums, blocks, segment
+        )
         copies = to_seats(blocks, outs, idx, count, out_sems)
-        if keep:
-            sums[0:1] = jnp.sum(back * hat, axis=0, keepdims=True)
-            sums[1:2] = jnp.sum(back, axis=0, keepdims=True)
-            sums[2:3] = jnp.sum(low.astype(F32), axis=0, keepdims=True)
-            sums[7:8] = jnp.sum(wide, axis=0, keepdims=True)
-
-            @pl.when(idx[count] == 0)
-            def _():
-                mine[:, :width] = normed[...]
-                mine[:, width:] = gh[...]
-                theirs[:, :width] = branch
-                theirs[:, width:] = active[...]
-
-            @pl.when(idx[count] == 1)
-            def _():
-                mine[:, :width] = branch
-                mine[:, width:] = active[...]
-                theirs[:, :width] = normed[...]
-                theirs[:, width:] = gh[...]
+        branch = wide.astype(LOW)
+
+        @pl.when(idx[count] == 0)
+        def _():
+            mine[:, :width] = normed[...]
+            mine[:, width:] = gh[...]
+            theirs[:, :width] = branch
+            theirs[:, width:] = active[...]
+
+        @pl.when(idx[count] == 1)
+        def _():
+            mine[:, :width] = branch
+            mine[:, width:] = active[...]
+            theirs[:, :width] = normed[...]
+            theirs[:, width:] = gh[...]
 
         wait_all(copies)
 
     return call(
         body, 14,
         [
-            idx, *grads, saved.middle, saved.slope, saved.active, saved.normed_two, saved.vec,
-            *given, *attn[0], *attn[1], *ffn[0], *ffn[1],
+            idx, *grads, hopped, saved.middle, saved.slope, saved.active, saved.normed_two, saved.vec,
+            *weights,
         ],
-        [SMEM] + [VMEM] * (7 + len(given)) + [ANY] * (4 * count),
-        [((2, short, PAIR), LOW, True)] * SEATS + [((tokens, width), F32, None)],
+        [SMEM] + [VMEM] * 11,
+        [((2, short, PAIR), LOW, True)] * SEATS
+        + [
+            ((tokens, width), F32, None), ((tokens, 5 * width), LOW, None),
+            ((tokens, 5 * width), LOW, None), ((8, width), F32, None), ((tokens, width), LOW, None),
+        ],
         [
-            pltpu.VMEM((SEATS, 2, short, PAIR), LOW), pltpu.VMEM((count, rows, width), LOW),
-            pltpu.VMEM((4, count, rows, width), LOW), pltpu.VMEM((count, 4, rows, width), LOW),
-            pltpu.VMEM((tokens, 4 * width), LOW), pltpu.SemaphoreType.DMA((9 * count,)),
+            pltpu.VMEM((SEATS, 2, short, PAIR), LOW), pltpu.VMEM((tokens, 4 * width), LOW),
             pltpu.SemaphoreType.DMA((SEATS,)),
         ],
-        [
-            ((tokens, 5 * width), LOW, None), ((tokens, 5 * width), LOW, None), ((8, width), F32, None),
-            ((tokens, width), LOW, None),
-        ],
-        keep,
-    )
-
-
-def project_back_kernel(count, segment, returned, grad_middle, grad_out, saved, attn, idx, keep):
+    )
+
+
+def project_back_kernel(count, segment, returned, grad_middle, grad_out, saved, weights, idx, keep):
     tokens, width = grad_middle.shape
     rows = width // count
     tall = block_rows(segment)
@@ -1157,14 +1221,9 @@
     def body(idx, grad_middle, x, vec, *rest):
         held, rest = rest[: len(kept)], rest[len(kept) :]
         back, rest = rest[:SEATS], rest[SEATS:]
-        chunks, rest = rest[: 2 * count], rest[2 * count :]
-        grad_low, grad_in, mine, theirs, sums, blocks, wq, wk, wv, sems, in_sems = rest
+        (wq, wk, wv), rest = rest[:3], rest[3:]
+        grad_low, grad_in, mine, theirs, sums, blocks, in_sems = rest
         copies = from_seats(back, blocks, idx, count, in_sems)
-        loader = Loader(sems)
-        loader.load(
-            idx, count, chunks[:count], chunks[count:],
-            [[(0, rows, wq, 0), (rows, rows, wk, 1)], [(0, rows, wv, 2)]],
-        )
         hat, scale = centre(x[...].astype(F32))
         wait_all(copies)
         pairs, singles = [[], [], []], [[], [], []]
@@ -1182,11 +1241,8 @@
                 jnp.concatenate([unfold(blocks[d, p, 4 * segment :].astype(F32), d) for p in range(2)], axis=0)
             )
         gq, gk, gv = [whole_rows(a, b).astype(LOW) for a, b in zip(pairs, singles)]
-        loader.wait(0)
         total = mm_nt(gq, flat(wq))
-        loader.wait(1)
         total += mm_nt(gk, flat(wk))
-        loader.wait(2)
         total += mm_nt(gv, flat(wv))
         result = grad_middle[...] + centre_back(total * vec[0:1], hat, scale)
         grad_low[...] = result.astype(LOW)
@@ -1218,14 +1274,12 @@
         def _():
             fill(theirs, mine)
 
-    weight = pltpu.VMEM((count, rows, width), LOW)
     return call(
-        body, 8, [idx, grad_middle, saved.inputs, saved.vec, *kept, *returned, *attn[0], *attn[1]],
-        [SMEM] + [VMEM] * (3 + len(kept)) + [ANY] * (SEATS + 2 * count),
+        body, 8, [idx, grad_middle, saved.inputs, saved.vec, *kept, *returned, *weights],
+        [SMEM] + [VMEM] * (3 + len(kept)) + [ANY] * SEATS + [VMEM] * 3,
         [((tokens, width), LOW, None)],
         [
-            pltpu.VMEM((SEATS, 2, tall, PAIR), LOW), weight, weight, weight,
-            pltpu.SemaphoreType.DMA((3 * count,)), pltpu.SemaphoreType.DMA((SEATS,)),
+            pltpu.VMEM((SEATS, 2, tall, PAIR), LOW), pltpu.SemaphoreType.DMA((SEATS,)),
         ],
         [
             ((tokens, width), F32, None), ((tokens, 4 * width), LOW, None),
@@ -1235,74 +1289,72 @@
     )
 
 
-def send_out(scratch, outs, idx, count, blocks, rows, base, sems, start):
-    for k in range(count):
-        for b in range(blocks):
-            if len(outs) == 1:
-                piece, place = outs[0].at[k], k
-            else:
-                piece, place = outs[k], idx[k]
-            copy = pltpu.make_async_copy(
-                scratch.at[pl.ds(pl.multiple_of(b * base + place * rows, 16), rows)],
-                piece.at[pl.ds(b * rows, rows)], sems.at[k * blocks + b],
-            )
-            copy.start() if start else copy.wait()
+def send_out(scratch, pieces, idx, sems, start):
+    for at, (out, to, rows, base, stride, k) in enumerate(pieces):
+        source = pl.ds(pl.multiple_of(base + idx[k] * stride, 16), rows)
+        copy = pltpu.make_async_copy(scratch.at[source], out.at[pl.ds(to, rows)], sems.at[at])
+        copy.start() if start else copy.wait()
 
 
 def ffn_terms_kernel(count, parts, idx):
-    ties = []
     width = parts[0].shape[1] // 5
     rows = width // count
 
-    shape = (4 * rows, width)
-    pieces = [(shape, LOW, True)] * count
-
     def body(idx, *rest):
-        given, rest = rest[: len(parts)], rest[len(parts) + len(ties) :]
-        outs, (scratch, sems) = rest[: len(pieces)], rest[len(pieces) :]
+        given, rest = rest[: len(parts)], rest[len(parts) :]
+        outs, (scratch, sems) = rest[: 2 * count], rest[2 * count :]
         narrow = jnp.concatenate([part[:, :width] for part in given], axis=0)
 
         def wide(b):
             span = slice((1 + b) * width, (2 + b) * width)
             return jnp.concatenate([part[:, span] for part in given], axis=0)
+
+        def pieces(b):
+            return [
+                (outs[b // 2 * count + k], b % 2 * rows, rows, b * width, rows, k) for k in range(count)
+            ]
 
         @pl.when(idx[count] == 0)
         def _():
             for b in range(4):
                 scratch[b * width : (b + 1) * width] = mm_tn(narrow, wide(b)).astype(LOW)
-            send_out(scratch, outs, idx, count, 4, rows, width, sems, True)
-            send_out(scratch, outs, idx, count, 4, rows, width, sems, False)
+                send_out(scratch, pieces(b), idx, sems.at[pl.ds(b * count, count)], True)
+            for b in range(4):
+                send_out(scratch, pieces(b), idx, sems.at[pl.ds(b * count, count)], False)
 
         @pl.when(idx[count] == 1)
         def _():
             for b in range(4):
                 scratch[b * width : (b + 1) * width] = mm_tn(wide(b), narrow).astype(LOW)
-            send_out(scratch, outs, idx, count, 1, 4 * rows, 0, sems, True)
-            send_out(scratch, outs, idx, count, 1, 4 * rows, 0, sems, False)
-
-    return call(
-        body, 8, [idx, *parts, *ties], [SMEM] + [VMEM] * len(parts) + [ANY] * len(ties),
-        pieces,
+            halves = [
+                (outs[ring * count + k], 0, 2 * rows, 2 * rows * ring, 4 * rows, k)
+                for ring in range(2) for k in range(count)
+            ]
+            send_out(scratch, halves, idx, sems, True)
+            send_out(scratch, halves, idx, sems, False)
+
+    outs = call(
+        body, 8, [idx, *parts], [SMEM] + [VMEM] * len(parts),
+        [((2 * rows, width), LOW, True)] * (2 * count),
         [pltpu.VMEM((4 * width, width), LOW), pltpu.SemaphoreType.DMA((4 * count,))],
     )
+    return outs[:count], outs[count:]
 
 
 def attn_terms_kernel(count, parts, sums_one, sums_two, idx):
-    ties = []
     width = parts[0].shape[1] // 4
-    given = len(parts), len(sums_one)
     rows = width // count
 
     def body(idx, *rest):
-        parts, rest = rest[: given[0]], rest[given[0] :]
-        one = sum(ref[...] for ref in rest[: given[1]])
-        two = sum(ref[...] for ref in rest[given[1] : 2 * given[1]])
-        rest = rest[2 * given[1] + len(ties) :]
-        outs, (scratch, notes, sems) = rest[:count], rest[count:]
+        parts_in, (one, two), rest = rest[: len(parts)], rest[len(parts) : len(parts) + 2], rest[len(parts) + 2 :]
+        outs, (scratch, notes, sems, note_sems) = rest[: 2 * count], rest[2 * count :]
 
         def both(b):
             span = slice(b * width, (b + 1) * width)
-            return jnp.concatenate([part[:, span] for part in parts], axis=0)
+            return jnp.concatenate([part[:, span] for part in parts_in], axis=0)
+
+        def pieces(b):
+            return [(outs[b * count + k], 0, rows, b * width, rows, k) for k in range(count)]
 
         flatly = jnp.concatenate(
             [
@@ -1326,25 +1378,43 @@
                 jnp.where((line == NOTE - 1) & (lane < 4 * rows), hidden, 0.0),
             )
             notes[s] = note.astype(LOW)
+        copies = start_all(
+            [
+                pltpu.make_async_copy(
+                    notes.at[idx[k]], outs[k].at[pl.ds(rows, NOTE)], note_sems.at[k]
+                )
+                for k in range(count)
+            ]
+        )
         for b in range(2):
             scratch[b * width : (b + 1) * width] = mm_tn(both(2 * b), both(2 * b + 1)).astype(LOW)
-        for start in (True, False):
-            send_out(scratch, outs, idx, count, 2, rows, width, sems, start)
-            for k in range(count):
-                copy = pltpu.make_async_copy(
-                    notes.at[idx[k]], outs[k].at[pl.ds(2 * rows, NOTE)], sems.at[2 * count + k]
-                )
-                copy.start() if start else copy.wait()
-
-    return call(
-        body, 5, [idx, *parts, *sums_one, *sums_two, *ties],
-        [SMEM] + [VMEM] * (given[0] + 2 * given[1]) + [ANY] * len(ties),
-        [((2 * rows + NOTE, width), LOW, True)] * count,
+            send_out(scratch, pieces(b), idx, sems.at[pl.ds(b * count, count)], True)
+        for b in range(2):
+            send_out(scratch, pieces(b), idx, sems.at[pl.ds(b * count, count)], False)
+        wait_all(copies)
+
+    outs = call(
+        body, 5, [idx, *parts, sums_one, sums_two], [SMEM] + [VMEM] * (len(parts) + 2),
+        [((rows + NOTE, width), LOW, True)] * count + [((rows, width), LOW, True)] * count,
         [
             pltpu.VMEM((2 * width, width), LOW), pltpu.VMEM((count, NOTE, width), LOW),
-            pltpu.SemaphoreType.DMA((3 * count,)),
+            pltpu.SemaphoreType.DMA((2 * count,)), pltpu.SemaphoreType.DMA((count,)),
         ],
     )
+    return outs[:count], outs[count:]
+
+
+class Rings:
+    def __init__(self, rings):
+        self.rings = rings
+
+    def step(self, *after):
+        for ring in self.rings:
+            ring.step(*after)
+
+    @property
+    def last(self):
+        return [v for ring in self.rings for v in ring.last if v is not None]
 
 
 def hold(values, *after):
@@ -1453,12 +1523,12 @@
             )
             for j in range(2)
         ]
-        return jnp.stack([jnp.where(odd == 0, *parts), jnp.where(odd == 0, *parts[::-1])])[None]
+        return jnp.stack([jnp.where(even, *parts), jnp.where(even, *parts[::-1])])[None]
 
     def exchange(parts):
         diagonal = [(r * count + s, (1 - r) * count + (s ^ 1)) for r in range(2) for s in range(count)]
         return [
-            parts[0],
+            pltpu.with_memory_space_constraint(parts[0], pltpu.HBM),
             lax.ppermute(parts[1], SHARD, [(s, s ^ 1) for s in range(count)]),
             swap(parts[2], REPLICA),
             lax.ppermute(parts[3], (REPLICA, SHARD), diagonal),
@@ -1469,60 +1539,51 @@
         axis=0,
     )
     qkv = w_qkv[0]
-    attn_own = jnp.concatenate(
-        [
-            jnp.where(replica == 0, qkv[:, :width], qkv[:, 2 * width :]),
-            jnp.where(replica == 0, qkv[:, width : 2 * width], w_out[0]),
-            note_rows(small, width),
-        ],
-        axis=0,
-    )
-    fc_blocks = jnp.concatenate([w_fc[0][:, b * width : (b + 1) * width] for b in range(4)], axis=0)
-    ffn_own = jnp.where(replica == 0, fc_blocks, w_proj[0])
-
-    attn_ring = GatherRing(attn_own, count, True)
+    attn_own = [
+        jnp.concatenate(
+            [jnp.where(replica == 0, qkv[:, :width], qkv[:, 2 * width :]), note_rows(small, width)], axis=0
+        ),
+        jnp.where(replica == 0, qkv[:, width : 2 * width], w_out[0]),
+    ]
+    ffn_own = [
+        jnp.where(
+            replica == 0,
+            jnp.concatenate([w_fc[0][:, b * width : (b + 1) * width] for b in (2 * i, 2 * i + 1)], axis=0),
+            w_proj[0][2 * i * rows : 2 * (i + 1) * rows],
+        )
+        for i in range(2)
+    ]
+
+    attn_ring = Rings([GatherRing(own, count, i == 0) for i, own in enumerate(attn_own)])
     attn_ring.step()
     order_row = lax.dynamic_index_in_dim(group_order, odd, 0).astype(LOW)
     order_rows = jnp.pad(order_row, ((0, NOTE - 1), (0, width - count)))
     packed = [gather_in(tokens, 0, order_rows), gather_in(tokens, 1)]
+    slot = lax.rem(shard // 2 + jnp.arange(2, dtype=jnp.int32), 2)
+    which = ((4 * (others // 2) + others % 2)[:, None] + 2 * slot[None, :]).reshape(-1)
+    chosen = (which[:, None] == jnp.arange(count, dtype=jnp.int32)[None, :]).astype(jnp.int32)
+    packed, chosen, even = lax.optimization_barrier((packed, chosen, odd == 0))
     blocks_at = packed[0][segment, :count].astype(jnp.int32)
-    pair = shard // 2
-    slot = lax.rem(pair + jnp.arange(2, dtype=jnp.int32), 2)
-    which = (4 * (others // 2) + others % 2)[:, None] + 2 * slot[None, :]
-    at = jnp.sum(
-        jnp.where(
-            which.reshape(-1, 1) == jnp.arange(count, dtype=jnp.int32)[None, :], blocks_at[None, :], 0
-        ),
-        axis=1,
-    )
+    at = jnp.sum(chosen * blocks_at[None, :], axis=1)
     attn_ring.step()
     attn_ring.step()
-    ffn_ring = GatherRing(hold(ffn_own, attn_ring.last), count, False)
+    ffn_ring = Rings(
+        [GatherRing(hold(own, attn_ring.last), count, i == 0) for i, own in enumerate(ffn_own)]
+    )
+    attn_ring.step()
+    attn_lists = [ring.lists() for ring in attn_ring.rings]
     ffn_ring.step()
-    attn_ring.step()
-    attn = attn_ring.lists()
-
-    def forward(hopped, keep, before):
-        *sent, vec, inputs = project_kernel(count, segment, packed, hopped, attn, idx, keep)[: SEATS + 2 + keep]
-        normed = None
-        if keep:
-            vec, inputs, normed = sent.pop(), vec, inputs
-        sent = before[0](sent)
-        arrived = exchange(sent)
-        back = attend_kernel(count, segment, before[1](arrived), at, keep)
-        back, kept = back[:SEATS], back[SEATS:]
-        returned = exchange(before[2](back))
-        fed = feed_kernel(
-            count, segment, before[3](returned), inputs, vec, attn, ffn_ring.lists(), idx, keep
-        )
-        state = Bag(vec=vec, inputs=inputs, normed=normed, arrived=arrived, output=fed[0])
-        if keep:
-            state.attended, state.total = kept
-            state.attended_low, state.middle, state.normed_two, state.slope, state.active = fed[1:]
-        return state
+
+    def forward(hopped, attn, before):
+        sent, inputs, normed, attn = project_kernel(count, segment, packed, hopped, attn, idx)
+        arrived = exchange(before[0](sent))
+        back = attend_kernel(count, segment, before[1](arrived), at, hopped is not None)
+        state = Bag(vec=attn[3], inputs=inputs, normed=normed, arrived=arrived)
+        return state, attn, exchange(before[2](back[:SEATS])), back[SEATS:]
 
     def ring_sent(sent):
         sent = hold(sent, ffn_ring.last)
+        ffn_ring.step()
         ffn_ring.step(sent[1])
         return sent
 
@@ -1533,58 +1594,69 @@
         ffn_ring.step(back[0])
         return back
 
-    def ring_returned(returned):
-        ffn_ring.step(returned[1])
-        return returned
-
     def same(values):
         return values
 
-    first = forward(None, False, [ring_sent, ring_arrived, ring_back, ring_returned])
-    ffn = ffn_ring.lists()
+    first, attn, returned, _ = forward(None, attn_lists, [ring_sent, ring_arrived, ring_back])
+    output, *ffn = feed_kernel(
+        count, segment, returned, first.inputs, first.vec,
+        attn_lists + [ring.lists() for ring in ffn_ring.rings], idx,
+    )
 
     def hop(values, backward):
         return lax.ppermute(values, SECTION, [(1, 0)] if backward else [(0, 1)])
 
-    upstream = [gather_in(hold(cotangent, first.output), j) for j in range(2)]
-    state = forward(
-        hop(first.output, False), True, [same, lambda arrived: hold(arrived, upstream), same, same]
-    )
-    acts = give_back(state.output)
-
-    def backward(hopped, keep, ties, terms, between):
-        out = feed_back_kernel(count, segment, upstream, hopped, state, attn, ffn, idx, keep)
-        sent, grad_middle, kept = out[:SEATS], out[SEATS], out[SEATS + 1 :]
+    upstream = [gather_in(hold(cotangent, output), j) for j in range(2)]
+    state, attn, returned, kept = forward(
+        hop(output, False), attn, [same, lambda arrived: hold(arrived, upstream), same]
+    )
+    state.attended, state.total = kept
+    *sent, output, state.attended_low, state.middle, state.normed_two, state.slope, state.active, grad_middle = (
+        turn_kernel(count, segment, returned, state.inputs, state.vec, ffn, upstream, idx)
+    )
+    acts = give_back(output)
+
+    def backward(sent, grad_middle, grad_out, keep, ties, between):
         arrived = exchange(sent)
-        if keep:
-            ties = ties + terms(kept)
+        ties = ties + between[0](arrived)
         back = attend_back_kernel(
             count, segment, state.arrived, arrived, state.attended, state.total, at, ties
         )
-        returned = exchange(between[0](back))
-        low, *last = project_back_kernel(
-            count, segment, between[1](returned), grad_middle, kept[3] if keep else None, state, attn,
-            idx, keep,
-        )
-        return low, kept, last
-
-    early, _, _ = backward(None, False, [acts], None, [same, same])
+        returned = exchange(between[1](back))
+        return project_back_kernel(
+            count, segment, between[2](returned), grad_middle, grad_out, state, attn[:3], idx, keep
+        )
+
+    early = backward(
+        sent, grad_middle, None, False, [],
+        [lambda arrived: [], same, lambda returned: hold(returned, acts)],
+    )
     rings = []
-
-    def ffn_terms(kept):
-        terms = ffn_terms_kernel(count, [kept[0], swap(kept[1], REPLICA)], idx)
-        rings.append(ScatterRing(terms, count, False))
+    *sent, grad_middle, mine, theirs, sums_two, grad_out = feed_back_kernel(
+        count, segment, upstream, hop(early[0], True), state, ffn, idx
+    )
+
+    def ffn_terms(arrived):
+        terms = ffn_terms_kernel(count, hold([mine, swap(theirs, REPLICA)], arrived), idx)
+        rings.append(Rings([ScatterRing(t, count, i == 0) for i, t in enumerate(terms)]))
         rings[0].step()
-        return [terms[0]]
-
-    def ring_step(values):
-        rings[0].step(values[1])
-        return values
-
-    low, kept, last = backward(hop(early, True), True, [], ffn_terms, [ring_step, ring_step])
-    rings[0].step(low)
-    terms = attn_terms_kernel(count, [last[1], swap(last[2], REPLICA)], [last[3]], [kept[2]], idx)
-    rings.append(ScatterRing(terms, count, True))
+        return [terms[0][0]]
+
+    def ring_back(back):
+        rings[0].step(back[1])
+        return back
+
+    def ring_returned(returned):
+        returned = hold(returned, rings[0].last)
+        rings[0].step(returned[1])
+        return returned
+
+    low, *last = backward(
+        sent, grad_middle, grad_out, True, [], [ffn_terms, ring_back, ring_returned]
+    )
+    terms = attn_terms_kernel(count, [last[1], swap(last[2], REPLICA)], last[3], sums_two, idx)
+    rings[0].step(terms[0][0])
+    rings.append(Rings([ScatterRing(t, count, i == 0) for i, t in enumerate(terms)]))
     for _ in range(half):
         rings[1].step()
     in_grads = give_back(hold(last[0].astype(LOW), low)).astype(F32)
@@ -1597,17 +1669,18 @@
             jnp.where(replica == 0, twin, total).astype(F32),
         )
 
-    ffn_total, attn_total = finished(rings[0]), finished(rings[1])
-    fc_grad = jnp.concatenate([ffn_total[0][b * rows : (b + 1) * rows] for b in range(4)], axis=1)
-    qkv_grad = jnp.concatenate(
-        [attn_total[0][:rows], attn_total[0][rows : 2 * rows], attn_total[1][:rows]], axis=1
-    )
-    note = attn_total[0][2 * rows :] + attn_total[1][2 * rows :]
+    feed_totals, totals = [[finished(ring) for ring in pair.rings] for pair in rings]
+    fc_grad = jnp.concatenate(
+        [half[0][b * rows : (b + 1) * rows] for half in feed_totals for b in range(2)], axis=1
+    )
+    proj_grad = jnp.concatenate([half[1] for half in feed_totals], axis=0)
+    qkv_grad = jnp.concatenate([totals[0][0][:rows], totals[1][0], totals[0][1][:rows]], axis=1)
+    note = totals[0][0][rows:] + totals[0][1][rows:]
     vec = note[:8, :rows]
     return (
         acts, in_grads, vec[0:2][None], vec[2:4][None], qkv_grad[None], vec[4:6][None],
-        attn_total[1][rows : 2 * rows][None], vec[6][None], fc_grad[None],
-        note[NOTE - 1, : 4 * rows][None], ffn_total[1][None], vec[7][None],
+        totals[1][1][None], vec[6][None], fc_grad[None], note[NOTE - 1, : 4 * rows][None],
+        proj_grad[None], vec[7][None],
     )
 
 

time: 455 us -> 396 us (0.87)
  starting transfers between devices: 72 us -> 122 us
  waiting for transfers between devices: 214 us -> 167 us
  Pallas kernels: 125 us -> 80.6 us
  local copies, waits for them, and re-layouts: 20.4 us -> 5.99 us
    pallas_call x14 -> x13, Pallas kernels: 125 us -> 80.6 us  [call(): pl.pallas_call(body, in_specs=specs, out_specs=[ANY if space is True else...]
    ppermute x8, waiting for transfers between devices: 68.2 us -> 26.7 us  [exchange(): lax.ppermute(parts[3], (REPLICA, SHARD), diagonal)]
    ppermute x6 -> x12, waiting for transfers between devices: 0.02 us -> 19.1 us  [step(): far = lax.ppermute(far, SHARD, self.left)]
    ppermute x8, waiting for transfers between devices: 47.4 us -> 30.2 us  [exchange(): lax.ppermute(parts[1], SHARD, [(s, s ^ 1) for s in range(count)])]
    ppermute x6 -> x12, starting transfers between devices: 4.4 us -> 18.4 us  [step(): lax.ppermute(second, SHARD, self.left)]
    ppermute x6 -> x12, waiting for transfers between devices: 21.2 us -> 33.7 us  [step(): lax.ppermute(first, SHARD, self.right)]
    ppermute x6 -> x12, starting transfers between devices: 9.86 us -> 21.5 us  [step(): near = lax.ppermute(near, SHARD, self.right)]
    unnamed x170 -> x182, local copies, waits for them, and re-layouts: 12.8 us -> 2.72 us
  transfers between devices with their start and end apart: 82 -> 128, of which waited for: 39 -> 52; matrix products, arithmetic and copies ran while one was open for 3% -> 3% of each run, Pallas kernels for 11% -> 9%
where the time goes in v3:
time: 396 us; the launch traced here: 390 us
  waiting for transfers between devices  167 us (42%)
  starting transfers between devices  122 us (31%)
  Pallas kernels  80.6 us (20%)
  other arithmetic  12 us (3%)
  local copies, waits for them, and re-layouts  5.99 us (2%)
    pallas_call x13, Pallas kernels, call(): pl.pallas_call(body, in_specs=specs, out_specs=[ANY if space is True else...  80.6 us
    ppermute x12, waiting for transfers between devices, step(): lax.ppermute(first, SHARD, self.right)  33.7 us
    ppermute x8, waiting for transfers between devices, exchange(): lax.ppermute(parts[1], SHARD, [(s, s ^ 1) for s in range(count)])  30.2 us
    ppermute x8, waiting for transfers between devices, exchange(): lax.ppermute(parts[3], (REPLICA, SHARD), diagonal)  26.7 us
    ppermute x12, starting transfers between devices, step(): near = lax.ppermute(near, SHARD, self.right)  21.5 us
    ppermute x2, waiting for transfers between devices, hop(): return lax.ppermute(values, SECTION, [(1, 0)] if backward else [(0, 1)])  20.9 us
    ppermute x46, starting transfers between devices, swap(): return lax.ppermute(x, axis, [(0, 1), (1, 0)])  19.4 us
    ppermute x12, waiting for transfers between devices, step(): far = lax.ppermute(far, SHARD, self.left)  19.1 us
  transfers between devices with their start and end apart: 128, of which 52 were waited for; matrix products, arithmetic and copies ran while one was open for 3% of the time, Pallas kernels for 9%

profile of v3, /device:TPU:0, one launch (start us, length us, event | category | flops | bytes accessed | tf_op | source)
XLA Modules:
  0.0 389.8 jit_solution(10769011477233364046)
XLA Ops:
  13.7 4.3 %collective-permute-done.5.rest_7_.rest_11_ = bf16[112,768]{1,0:T(8,128)(2,1)S(1)} collective-permute-done((bf16[112,768]{1,0:T(8,128)(2,1)S(1)}, bf16[112,768]{1,0:T(8,128)(2,1)S(1)}, u32[]{:S(2)}, u32[]{:S(2)}) %collective-permute-start.5) | collective-permute-done | bytes 172064 | tf_op jit(solution)/shard_map/ppermute | solution.py:1439
  64.6 4.2 %collective-permute-done.42.rest_38_ = bf16[192,768]{1,0:T(8,128)(2,1)} collective-permute-done((bf16[192,768]{1,0:T(8,128)(2,1)S(1)}, bf16[192,768]{1,0:T(8,128)(2,1)}, u32[]{:S(2)}, u32[]{:S(2)}) %collective-permute-start.42) | collective-permute-done | bytes 294944 | tf_op jit(solution)/shard_map/ppermute | solution.py:1440
  71.3 5.3 %shard_map.238 = (bf16[2,576,128]{2,1,0:T(8,128)(2,1)}, bf16[2,576,128]{2,1,0:T(8,128)(2,1)}, bf16[2,576,128]{2,1,0:T(8,128)(2,1)}, bf16[2,576,128]{2,1,0:T(8,12...) custom-call(s32[14]{0:T(128)S(1)} %pad_add_fusion.idx, ...), custom_call_target="tpu_custom_call" | custom-call | bytes 25830000 | tf_op jit(solution)/shard_map/pallas_call | solution.py:567
  81.7 4.8 %collective-permute-done.38.rest_3_ = bf16[2,576,128]{2,1,0:T(8,128)(2,1)S(1)} collective-permute-done((bf16[2,576,128]{2,1,0:T(8,128)(2,1)}, bf16[2,576,128]{2,1,0:T(8,128)(2,1)S(1)}, u32[]{:S(2)}, u32[]{:S(2)}) %collective-permute-start.38) | collective-permute-done | bytes 294944 | tf_op jit(solution)/shard_map/ppermute | solution.py:1534
  88.2 5.2 %collective-permute-done.36.rest_1_ = bf16[2,576,128]{2,1,0:T(8,128)(2,1)S(1)} collective-permute-done((bf16[2,576,128]{2,1,0:T(8,128)(2,1)}, bf16[2,576,128]{2,1,0:T(8,128)(2,1)S(1)}, u32[]{:S(2)}, u32[]{:S(2)}) %collective-permute-start.36) | collective-permute-done | bytes 294944 | tf_op jit(solution)/shard_map/ppermute | solution.py:1532
  93.4 4.6 %collective-permute-done.44.rest_39_ = bf16[192,768]{1,0:T(8,128)(2,1)S(1)} collective-permute-done((bf16[192,768]{1,0:T(8,128)(2,1)}, bf16[192,768]{1,0:T(8,128)(2,1)S(1)}, u32[]{:S(2)}, u32[]{:S(2)}) %collective-permute-start.44) | collective-permute-done | bytes 294944 | tf_op jit(solution)/shard_map/ppermute | solution.py:1440
  98.1 5.9 %shard_map.239 = (bf16[2,192,128]{2,1,0:T(8,128)(2,1)}, bf16[2,192,128]{2,1,0:T(8,128)(2,1)}, bf16[2,192,128]{2,1,0:T(8,128)(2,1)}, bf16[2,192,128]{2,1,0:T(8,128)(2,1)}) custom-call(s32[8]{0:T(128)S(1)} %multiply_reduce_fusion.at, bf16[2,576,128]{2,1,0:T(8,128)(2,1)} %get-tuple-element.160.rest_0_, ...), custom_call_target="tpu_custom_call" | custom-call | bytes 33210000 | tf_op jit(solution)/shard_map/pallas_call | solution.py:567
  114.9 6.6 %collective-permute-done.46.rest_40_ = bf16[192,768]{1,0:T(8,128)(2,1)S(1)} collective-permute-done((bf16[192,768]{1,0:T(8,128)(2,1)S(1)}, bf16[192,768]{1,0:T(8,128)(2,1)S(1)}, u32[]{:S(2)}, u32[]{:S(2)}) %collective-permute-start.46) | collective-permute-done | bytes 294944 | tf_op jit(solution)/shard_map/ppermute | solution.py:1446
  124.2 8.2 %shard_map.240 = (bf16[256,768]{1,0:T(8,128)(2,1)S(1)}, bf16[8,96,768]{2,1,0:T(8,128)(2,1)S(1)}, bf16[4,8,96,768]{3,2,1,0:T(8,128)(2,1)S(1)}, bf16[8,4,96,768]{3,2,1,0:T(8,128)(2,1)S(1)}) custom-call(s32[14]{0:T(128)S(1)} %pad_add_fusion.idx, bf16[256,768]{1,0:T(8,128)(2,1)S(1)} %get-tuple-element.151.x, f32[12,768]{1,0:T(8,128)S(1)} %get-tuple-element.152.vec.rest_4_, ...), custom_call_target="tpu_custom_call" | custom-call | bytes 36900000 | tf_op jit(solution)/shard_map/pallas_call | solution.py:567
  135.8 8.6 %collective-permute-done.68.rest_0_ = bf16[256,768]{1,0:T(8,128)(2,1)S(1)} collective-permute-done((bf16[256,768]{1,0:T(8,128)(2,1)S(1)}, bf16[256,768]{1,0:T(8,128)(2,1)S(1)}, u32[]{:S(2)}, u32[]{:S(2)}) %collective-permute-start.68) | collective-permute-done | bytes 393248 | tf_op jit(solution)/shard_map/ppermute | solution.py:1607
  152.2 4.0 %collective-permute-done.70.second = bf16[128,768]{1,0:T(8,128)(2,1)S(1)} collective-permute-done((bf16[128,768]{1,0:T(8,128)(2,1)S(1)}, bf16[128,768]{1,0:T(8,128)(2,1)S(1)}, u32[]{:S(2)}, u32[]{:S(2)}) %collective-permute-start.70) | collective-permute-done | bytes 196640 | tf_op jit(solution)/shard_map/ppermute | solution.py:1517
  157.7 3.9 collective-permute-done.73.rest_3_
  161.6 6.1 %shard_map.242 = (bf16[2,192,128]{2,1,0:T(8,128)(2,1)}, bf16[2,192,128]{2,1,0:T(8,128)(2,1)}, bf16[2,192,128]{2,1,0:T(8,128)(2,1)}, bf16[2,192,128]{2,1,0:T(8,12...) custom-call(s32[8]{0:T(128)S(1)} %multiply_reduce_fusion.at, ...), custom_call_target="tpu_custom_call" | custom-call | bytes 33210000 | tf_op jit(solution)/shard_map/pallas_call | solution.py:567
  175.7 9.9 %shard_map.243 = (bf16[2,192,128]{2,1,0:T(8,128)(2,1)}, bf16[2,192,128]{2,1,0:T(8,128)(2,1)}, bf16[2,192,128]{2,1,0:T(8,128)(2,1)}, bf16[2,192,128]{2,1,0:T(8,12...) custom-call(s32[14]{0:T(128)S(1)} %pad_add_fusion.idx, ...), custom_call_target="tpu_custom_call" | custom-call | bytes 36900000 | tf_op jit(solution)/shard_map/pallas_call | solution.py:567
  192.4 4.2 %collective-permute-done.81.rest_7_ = bf16[2,192,128]{2,1,0:T(8,128)(2,1)S(1)} collective-permute-done((bf16[2,192,128]{2,1,0:T(8,128)(2,1)}, bf16[2,192,128]{2,1,0:T(8,128)(2,1)S(1)}, u32[]{:S(2)}, u32[]{:S(2)}) %collective-permute-start.81) | collective-permute-done | bytes 98336 | tf_op jit(solution)/shard_map/ppermute | solution.py:1534
  196.6 11.1 %shard_map.244 = (bf16[2,576,128]{2,1,0:T(8,128)(2,1)}, bf16[2,576,128]{2,1,0:T(8,128)(2,1)}, bf16[2,576,128]{2,1,0:T(8,128)(2,1)}, bf16[2,576,128]{2,1,0:T(8,128)(2,1)}) custom-call(s32[8]{0:T(128)S(1)} %multiply_reduce_fusion.at, f32[2,1024,128]{2,1,0:T(8,128)S(1)} %get-tuple-element.197.attended, f32[1024,128]{1,0:T(8,128)S(1)} %get-tuple-element.198.total, ...), custom_call_target="tpu_custom_call" | custom-call | bytes 51660000 | tf_op jit(solution)/shard_map/pallas_call | solution.py:567
  210.7 7.1 %collective-permute-done.82.rest_1_ = bf16[2,576,128]{2,1,0:T(8,128)(2,1)S(1)} collective-permute-done((bf16[2,576,128]{2,1,0:T(8,128)(2,1)}, bf16[2,576,128]{2,1,0:T(8,128)(2,1)S(1)}, u32[]{:S(2)}, u32[]{:S(2)}) %collective-permute-start.82) | collective-permute-done | bytes 294944 | tf_op jit(solution)/shard_map/ppermute | solution.py:1532
  217.8 4.6 %collective-permute-done.84.rest_3_ = bf16[2,576,128]{2,1,0:T(8,128)(2,1)S(1)} collective-permute-done((bf16[2,576,128]{2,1,0:T(8,128)(2,1)}, bf16[2,576,128]{2,1,0:T(8,128)(2,1)S(1)}, u32[]{:S(2)}, u32[]{:S(2)}) %collective-permute-start.84) | collective-permute-done | bytes 294944 | tf_op jit(solution)/shard_map/ppermute | solution.py:1534
  226.9 12.2 %collective-permute-done.85.hopped = bf16[256,768]{1,0:T(8,128)(2,1)S(1)} collective-permute-done((bf16[256,768]{1,0:T(8,128)(2,1)S(1)}, bf16[256,768]{1,0:T(8,128)(2,1)S(1)}, u32[]{:S(2)}, u32[]{:S(2)}) %collective-permute-start.85) | collective-permute-done | bytes 393248 | tf_op jit(solution)/shard_map/ppermute | solution.py:1607
  239.1 5.2 %shard_map.246 = (bf16[2,192,128]{2,1,0:T(8,128)(2,1)}, bf16[2,192,128]{2,1,0:T(8,128)(2,1)}, bf16[2,192,128]{2,1,0:T(8,128)(2,1)}, bf16[2,192,128]{2,1,0:T(8,12...) custom-call(s32[14]{0:T(128)S(1)} %pad_add_fusion.idx, ...), custom_call_target="tpu_custom_call" | custom-call | bytes 51660000 | tf_op jit(solution)/shard_map/pallas_call | solution.py:567
  251.5 4.6 %shard_map.247 = (bf16[192,768]{1,0:T(8,128)(2,1)}, bf16[192,768]{1,0:T(8,128)(2,1)}, bf16[192,768]{1,0:T(8,128)(2,1)}, bf16[192,768]{1,0:T(8,128)(2,1)}, bf16[1...) custom-call(s32[14]{0:T(128)S(1)} %pad_add_fusion.idx, ...), custom_call_target="tpu_custom_call" | custom-call | bytes 29520000 | tf_op jit(solution)/shard_map/pallas_call | solution.py:567
  259.3 11.2 %shard_map.248 = (bf16[2,576,128]{2,1,0:T(8,128)(2,1)}, bf16[2,576,128]{2,1,0:T(8,128)(2,1)}, bf16[2,576,128]{2,1,0:T(8,128)(2,1)}, bf16[2,576,128]{2,1,0:T(8,128)(2,1)}) custom-call(s32[8]{0:T(128)S(1)} %multiply_reduce_fusion.at, f32[2,1024,128]{2,1,0:T(8,128)S(1)} %get-tuple-element.197.attended, f32[1024,128]{1,0:T(8,128)S(1)} %get-tuple-element.198.total, ...), custom_call_target="tpu_custom_call" | custom-call | bytes 51660000 | tf_op jit(solution)/shard_map/pallas_call | solution.py:567
  276.0 4.7 %collective-permute-done.92.rest_6_ = bf16[2,576,128]{2,1,0:T(8,128)(2,1)S(1)} collective-permute-done((bf16[2,576,128]{2,1,0:T(8,128)(2,1)}, bf16[2,576,128]{2,1,0:T(8,128)(2,1)S(1)}, u32[]{:S(2)}, u32[]{:S(2)}) %collective-permute-start.92) | collective-permute-done | bytes 294944 | tf_op jit(solution)/shard_map/ppermute | solution.py:1534
  281.7 5.8 %collective-permute-done.90.rest_4_ = bf16[2,576,128]{2,1,0:T(8,128)(2,1)S(1)} collective-permute-done((bf16[2,576,128]{2,1,0:T(8,128)(2,1)}, bf16[2,576,128]{2,1,0:T(8,128)(2,1)S(1)}, u32[]{:S(2)}, u32[]{:S(2)}) %collective-permute-start.90) | collective-permute-done | bytes 294944 | tf_op jit(solution)/shard_map/ppermute | solution.py:1532
  287.5 6.3 %collective-permute-done.94 = bf16[192,768]{1,0:T(8,128)(2,1)S(1)} collective-permute-done((bf16[192,768]{1,0:T(8,128)(2,1)S(1)}, bf16[192,768]{1,0:T(8,128)(2,1)S(1)}, u32[]{:S(2)}, u32[]{:S(2)}) %collective-permute-start.94) | collective-permute-done | bytes 294944 | tf_op jit(solution)/shard_map/ppermute | solution.py:1477
  293.8 6.1 %collective-permute-done.97 = bf16[192,768]{1,0:T(8,128)(2,1)S(1)} collective-permute-done((bf16[192,768]{1,0:T(8,128)(2,1)S(1)}, bf16[192,768]{1,0:T(8,128)(2,1)S(1)}, u32[]{:S(2)}, u32[]{:S(2)}) %collective-permute-start.97) | collective-permute-done | bytes 294944 | tf_op jit(solution)/shard_map/ppermute | solution.py:1477
  299.9 3.9 %shard_map.249 = (bf16[256,768]{1,0:T(8,128)(2,1)}, f32[256,768]{1,0:T(8,128)S(1)}, bf16[256,3072]{1,0:T(8,128)(2,1)S(1)}, bf16[256,3072]{1,0:T(8,128)(2,1)S(1)}, f32[8,768]{1,0:T(8,128)S(1)}) custom-call(s32[14]{0:T(128)S(1)} %pad_add_fusion.idx, f32[256,768]{1,0:T(8,128)S(1)} %get-tuple-element.215.grad_middle, bf16[256,768]{1,0:T(8,128)(2,1)S(1)} %get-tuple-element.178.x, ...), custom_call_target="tpu_custom_call" | custom-call | bytes 29520000 | tf_op jit(solution)/shard_map/pallas_call | solution.py:567
  305.7 4.5 %collective-permute-start.101 = (bf16[256,3072]{1,0:T(8,128)(2,1)S(1)}, bf16[256,3072]{1,0:T(8,128)(2,1)S(1)}, u32[]{:S(2)}, u32[]{:S(2)}) collective-permute-start(bf16[256,3072]{1,0:T(8,128)(2,1)S(1)} %get-tuple-element.248), channel_id=1, source_target_pairs={{0,8},{8,0},{1,9},{9,1},{2,10},{10,2},{3,11},{11,3},{4,12},{12,4},... | collective-permute-start | bytes 4718600 | tf_op jit(solution)/shard_map/ppermute | solution.py:79
  319.4 3.8 collective-permute-done.119
  337.1 4.8 %collective-permute-start.121 = (bf16[192,768]{1,0:T(8,128)(2,1)S(1)}, bf16[192,768]{1,0:T(8,128)(2,1)S(1)}, u32[]{:S(2)}, u32[]{:S(2)}) collective-permute-start(bf16[192,768]{1,0:T(8,128)(2,1)S(1)} %add_convert_fusion.6), channel_id=1, source_target_pairs={{2,0},{4,2},{6,4},{7,6},{5,7},{3,5},{1,3},{0,1},{10,8},{12,10},{14... | collective-permute-start | bytes 884744 | tf_op jit(solution)/shard_map/ppermute | solution.py:1477
  345.8 10.9 %collective-permute-done.111 = bf16[96,768]{1,0:T(8,128)(2,1)S(1)} collective-permute-done((bf16[96,768]{1,0:T(8,128)(2,1)S(1)}, bf16[96,768]{1,0:T(8,128)(2,1)S(1)}, u32[]{:S(2)}, u32[]{:S(2)}) %collective-permute-start.111) | collective-permute-done | bytes 147488 | tf_op jit(solution)/shard_map/ppermute | solution.py:1477
  358.1 4.1 %collective-permute-done.114 = bf16[96,768]{1,0:T(8,128)(2,1)S(1)} collective-permute-done((bf16[96,768]{1,0:T(8,128)(2,1)S(1)}, bf16[96,768]{1,0:T(8,128)(2,1)S(1)}, u32[]{:S(2)}, u32[]{:S(2)}) %collective-permute-start.114) | collective-permute-done | bytes 147488 | tf_op jit(solution)/shard_map/ppermute | solution.py:1477
  (486 shorter events, 190.3 us)
Async XLA Ops:
  5.3 17.7 %collective-permute-start.1 = (bf16[128,768]{1,0:T(8,128)(2,1)S(1)}, bf16[128,768]{1,0:T(8,128)(2,1)S(1)}, u32[]{:S(2)}, u32[]{:S(2)}) collective-permute-start(bf16[128,768]{1,0:T(8,128)(2,1)S(1)} %get-tuple-element.310), channel_id=1, source_target_pairs={{0,2},{1,3},{2,0},{3,1},{4,10},{5,11},{6,8},{7,9},{8,6},{9,7},{10,... | collective-permute-start | bytes 589832 | tf_op jit(solution)/shard_map/ppermute | solution.py:1517
  7.4 15.7 %collective-permute-start = (bf16[144,768]{1,0:T(8,128)(2,1)S(1)}, bf16[144,768]{1,0:T(8,128)(2,1)S(1)}, u32[]{:S(2)}, u32[]{:S(2)}) collective-permute-start(bf16[144,768]{1,0:T(8,128)(2,1)S(1)} %fusion.5), channel_id=1, source_target_pairs={{0,0},{1,1},{2,2},{3,3},{4,8},{5,9},{6,10},{7,11},{8,4},{9,5},{10,... | collective-permute-start | bytes 663560 | tf_op jit(solution)/shard_map/ppermute | solution.py:1517
  63.4 13.3 %collective-permute-start.48 = (bf16[192,768]{1,0:T(8,128)(2,1)S(1)}, bf16[192,768]{1,0:T(8,128)(2,1)S(1)}, u32[]{:S(2)}, u32[]{:S(2)}) collective-permute-start(bf16[192,768]{1,0:T(8,128)(2,1)S(1)} %collective-permute-done.33.rest_37_), channel_id=1, source_target_pairs={{0,8},{8,0},{1,9},{9,1},{2,10},{10,2},{3,11},{11,3},{4,12},{12,4},... | collective-permute-start | bytes 884744 | tf_op jit(solution)/shard_map/ppermute | solution.py:79
  64.1 12.7 %collective-permute-start.54 = (bf16[192,768]{1,0:T(8,128)(2,1)}, bf16[192,768]{1,0:T(8,128)(2,1)S(1)}, u32[]{:S(2)}, u32[]{:S(2)}) collective-permute-start(bf16[192,768]{1,0:T(8,128)(2,1)} %collective-permute-done.32.rest_43_), channel_id=1, source_target_pairs={{0,8},{8,0},{1,9},{9,1},{2,10},{10,2},{3,11},{11,3},{4,12},{12,4},... | collective-permute-start | bytes 884744 | tf_op jit(solution)/shard_map/ppermute | solution.py:79
  64.1 13.2 %collective-permute-start.61 = (bf16[192,768]{1,0:T(8,128)(2,1)}, bf16[192,768]{1,0:T(8,128)(2,1)S(1)}, u32[]{:S(2)}, u32[]{:S(2)}) collective-permute-start(bf16[192,768]{1,0:T(8,128)(2,1)} %collective-permute-done.35.rest_53_), channel_id=1, source_target_pairs={{0,8},{8,0},{1,9},{9,1},{2,10},{10,2},{3,11},{11,3},{4,12},{12,4},... | collective-permute-start | bytes 884744 | tf_op jit(solution)/shard_map/ppermute | solution.py:79
  77.7 15.7 %collective-permute-start.36 = (bf16[2,576,128]{2,1,0:T(8,128)(2,1)}, bf16[2,576,128]{2,1,0:T(8,128)(2,1)S(1)}, u32[]{:S(2)}, u32[]{:S(2)}) collective-permute-start(bf16[2,576,128]{2,1,0:T(8,128)(2,1)} %get-tuple-element.161), channel_id=1, source_target_pairs={{0,1},{1,0},{2,3},{3,2},{4,5},{5,4},{6,7},{7,6},{8,9},{9,8},{10,11... | collective-permute-start | bytes 884744 | tf_op jit(solution)/shard_map/ppermute | solution.py:1532
  79.0 19.0 %collective-permute-start.44 = (bf16[192,768]{1,0:T(8,128)(2,1)}, bf16[192,768]{1,0:T(8,128)(2,1)S(1)}, u32[]{:S(2)}, u32[]{:S(2)}) collective-permute-start(bf16[192,768]{1,0:T(8,128)(2,1)} %collective-permute-done.42.rest_38_), channel_id=1, source_target_pairs={{2,0},{4,2},{6,4},{7,6},{5,7},{3,5},{1,3},{0,1},{10,8},{12,10},{14... | collective-permute-start | bytes 884744 | tf_op jit(solution)/shard_map/ppermute | solution.py:1440
  79.7 24.4 %collective-permute-start.45 = (bf16[192,768]{1,0:T(8,128)(2,1)}, bf16[192,768]{1,0:T(8,128)(2,1)S(1)}, u32[]{:S(2)}, u32[]{:S(2)}) collective-permute-start(bf16[192,768]{1,0:T(8,128)(2,1)} %collective-permute-done.43.rest_42_), channel_id=1, source_target_pairs={{0,2},{2,4},{4,6},{6,7},{7,5},{5,3},{3,1},{1,0},{8,10},{10,12},{12... | collective-permute-start | bytes 884744 | tf_op jit(solution)/shard_map/ppermute | solution.py:1439
  81.0 25.5 %collective-permute-start.57 = (bf16[192,768]{1,0:T(8,128)(2,1)S(1)}, bf16[192,768]{1,0:T(8,128)(2,1)S(1)}, u32[]{:S(2)}, u32[]{:S(2)}) collective-permute-start(bf16[192,768]{1,0:T(8,128)(2,1)S(1)} %collective-permute-done.55.rest_54_), channel_id=1, source_target_pairs={{2,0},{4,2},{6,4},{7,6},{5,7},{3,5},{1,3},{0,1},{10,8},{12,10},{14... | collective-permute-start | bytes 884744 | tf_op jit(solution)/shard_map/ppermute | solution.py:1440
  86.5 20.3 %collective-permute-start.58 = (bf16[192,768]{1,0:T(8,128)(2,1)S(1)}, bf16[192,768]{1,0:T(8,128)(2,1)S(1)}, u32[]{:S(2)}, u32[]{:S(2)}) collective-permute-start(bf16[192,768]{1,0:T(8,128)(2,1)S(1)} %collective-permute-done.56.rest_58_), channel_id=1, source_target_pairs={{0,2},{2,4},{4,6},{6,7},{7,5},{5,3},{3,1},{1,0},{8,10},{10,12},{12... | collective-permute-start | bytes 884744 | tf_op jit(solution)/shard_map/ppermute | solution.py:1439
  93.4 18.8 %collective-permute-start.49 = (bf16[192,768]{1,0:T(8,128)(2,1)}, bf16[192,768]{1,0:T(8,128)(2,1)S(1)}, u32[]{:S(2)}, u32[]{:S(2)}) collective-permute-start(bf16[192,768]{1,0:T(8,128)(2,1)} %collective-permute-done.42.rest_38_), channel_id=1, source_target_pairs={{0,8},{8,0},{1,9},{9,1},{2,10},{10,2},{3,11},{11,3},{4,12},{12,4},... | collective-permute-start | bytes 884744 | tf_op jit(solution)/shard_map/ppermute | solution.py:79
  98.0 14.2 %collective-permute-start.53 = (bf16[192,768]{1,0:T(8,128)(2,1)}, bf16[192,768]{1,0:T(8,128)(2,1)S(1)}, u32[]{:S(2)}, u32[]{:S(2)}) collective-permute-start(bf16[192,768]{1,0:T(8,128)(2,1)} %collective-permute-done.43.rest_42_), channel_id=1, source_target_pairs={{0,8},{8,0},{1,9},{9,1},{2,10},{10,2},{3,11},{11,3},{4,12},{12,4},... | collective-permute-start | bytes 884744 | tf_op jit(solution)/shard_map/ppermute | solution.py:79
  185.7 24.2 %collective-permute-start.77 = (bf16[128,768]{1,0:T(8,128)(2,1)S(1)}, bf16[128,768]{1,0:T(8,128)(2,1)S(1)}, u32[]{:S(2)}, u32[]{:S(2)}) collective-permute-start(bf16[128,768]{1,0:T(8,128)(2,1)S(1)} %get-tuple-element.306), channel_id=1, source_target_pairs={{0,0},{1,1},{2,2},{3,3},{8,4},{9,5},{10,6},{11,7},{4,8},{5,9},{6,1... | collective-permute-start | bytes 589832 | tf_op jit(solution)/shard_map/ppermute | solution.py:1521
  186.6 23.3 %collective-permute-start.78 = (bf16[128,768]{1,0:T(8,128)(2,1)S(1)}, bf16[128,768]{1,0:T(8,128)(2,1)S(1)}, u32[]{:S(2)}, u32[]{:S(2)}) collective-permute-start(bf16[128,768]{1,0:T(8,128)(2,1)S(1)} %get-tuple-element.307), channel_id=1, source_target_pairs={{2,0},{3,1},{0,2},{1,3},{10,4},{11,5},{8,6},{9,7},{6,8},{7,9},{4,1... | collective-permute-start | bytes 589832 | tf_op jit(solution)/shard_map/ppermute | solution.py:1521
  208.8 13.7 %collective-permute-start.84 = (bf16[2,576,128]{2,1,0:T(8,128)(2,1)}, bf16[2,576,128]{2,1,0:T(8,128)(2,1)S(1)}, u32[]{:S(2)}, u32[]{:S(2)}) collective-permute-start(bf16[2,576,128]{2,1,0:T(8,128)(2,1)} %get-tuple-element.206), channel_id=1, source_target_pairs={{0,9},{1,8},{2,11},{3,10},{4,13},{5,12},{6,15},{7,14},{8,1},{9,0},... | collective-permute-start | bytes 884744 | tf_op jit(solution)/shard_map/ppermute | solution.py:1534
  225.4 13.7 %collective-permute-start.85 = (bf16[256,768]{1,0:T(8,128)(2,1)S(1)}, bf16[256,768]{1,0:T(8,128)(2,1)S(1)}, u32[]{:S(2)}, u32[]{:S(2)}) collective-permute-start(bf16[256,768]{1,0:T(8,128)(2,1)S(1)} %shard_map.245), channel_id=1, source_target_pairs={{16,0},{17,1},{18,2},{19,3},{20,4},{21,5},{22,6},{23,7},{24,8},{25... | collective-permute-start | bytes 1179656 | tf_op jit(solution)/shard_map/ppermute | solution.py:1607
  256.1 17.0 %collective-permute-start.93 = (bf16[192,768]{1,0:T(8,128)(2,1)}, bf16[192,768]{1,0:T(8,128)(2,1)S(1)}, u32[]{:S(2)}, u32[]{:S(2)}) collective-permute-start(bf16[192,768]{1,0:T(8,128)(2,1)} %get-tuple-element.233), channel_id=1, source_target_pairs={{0,2},{2,4},{4,6},{6,7},{7,5},{5,3},{3,1},{1,0},{8,10},{10,12},{12... | collective-permute-start | bytes 884744 | tf_op jit(solution)/shard_map/ppermute | solution.py:1468
  256.1 17.5 %collective-permute-start.96 = (bf16[192,768]{1,0:T(8,128)(2,1)}, bf16[192,768]{1,0:T(8,128)(2,1)S(1)}, u32[]{:S(2)}, u32[]{:S(2)}) collective-permute-start(bf16[192,768]{1,0:T(8,128)(2,1)} %get-tuple-element.239), channel_id=1, source_target_pairs={{2,0},{4,2},{6,4},{7,6},{5,7},{3,5},{1,3},{0,1},{10,8},{12,10},{14... | collective-permute-start | bytes 884744 | tf_op jit(solution)/shard_map/ppermute | solution.py:1470
  272.1 15.4 %collective-permute-start.90 = (bf16[2,576,128]{2,1,0:T(8,128)(2,1)}, bf16[2,576,128]{2,1,0:T(8,128)(2,1)S(1)}, u32[]{:S(2)}, u32[]{:S(2)}) collective-permute-start(bf16[2,576,128]{2,1,0:T(8,128)(2,1)} %get-tuple-element.229), channel_id=1, source_target_pairs={{0,1},{1,0},{2,3},{3,2},{4,5},{5,4},{6,7},{7,6},{8,9},{9,8},{10,11... | collective-permute-start | bytes 884744 | tf_op jit(solution)/shard_map/ppermute | solution.py:1532
  273.2 20.6 %collective-permute-start.94 = (bf16[192,768]{1,0:T(8,128)(2,1)S(1)}, bf16[192,768]{1,0:T(8,128)(2,1)S(1)}, u32[]{:S(2)}, u32[]{:S(2)}) collective-permute-start(bf16[192,768]{1,0:T(8,128)(2,1)S(1)} %add_convert_fusion.11), channel_id=1, source_target_pairs={{0,2},{2,4},{4,6},{6,7},{7,5},{5,3},{3,1},{1,0},{8,10},{10,12},{12... | collective-permute-start | bytes 884744 | tf_op jit(solution)/shard_map/ppermute | solution.py:1477
  273.6 20.2 %collective-permute-start.95 = (bf16[192,768]{1,0:T(8,128)(2,1)S(1)}, bf16[192,768]{1,0:T(8,128)(2,1)S(1)}, u32[]{:S(2)}, u32[]{:S(2)}) collective-permute-start(bf16[192,768]{1,0:T(8,128)(2,1)S(1)} %copy-done.88), channel_id=1, source_target_pairs={{2,0},{4,2},{6,4},{7,6},{5,7},{3,5},{1,3},{0,1},{10,8},{12,10},{14... | collective-permute-start | bytes 884744 | tf_op jit(solution)/shard_map/ppermute | solution.py:1477
  275.4 24.5 %collective-permute-start.97 = (bf16[192,768]{1,0:T(8,128)(2,1)S(1)}, bf16[192,768]{1,0:T(8,128)(2,1)S(1)}, u32[]{:S(2)}, u32[]{:S(2)}) collective-permute-start(bf16[192,768]{1,0:T(8,128)(2,1)S(1)} %copy-done.87), channel_id=1, source_target_pairs={{0,2},{2,4},{4,6},{6,7},{7,5},{5,3},{3,1},{1,0},{8,10},{10,12},{12... | collective-permute-start | bytes 884744 | tf_op jit(solution)/shard_map/ppermute | solution.py:1477
  280.7 19.2 %collective-permute-start.98 = (bf16[192,768]{1,0:T(8,128)(2,1)S(1)}, bf16[192,768]{1,0:T(8,128)(2,1)S(1)}, u32[]{:S(2)}, u32[]{:S(2)}) collective-permute-start(bf16[192,768]{1,0:T(8,128)(2,1)S(1)} %add_convert_fusion.10), channel_id=1, source_target_pairs={{2,0},{4,2},{6,4},{7,6},{5,7},{3,5},{1,3},{0,1},{10,8},{12,10},{14... | collective-permute-start | bytes 884744 | tf_op jit(solution)/shard_map/ppermute | solution.py:1477
  305.7 19.2 %collective-permute-start.101 = (bf16[256,3072]{1,0:T(8,128)(2,1)S(1)}, bf16[256,3072]{1,0:T(8,128)(2,1)S(1)}, u32[]{:S(2)}, u32[]{:S(2)}) collective-permute-start(bf16[256,3072]{1,0:T(8,128)(2,1)S(1)} %get-tuple-element.248), channel_id=1, source_target_pairs={{0,8},{8,0},{1,9},{9,1},{2,10},{10,2},{3,11},{11,3},{4,12},{12,4},... | collective-permute-start | bytes 4718600 | tf_op jit(solution)/shard_map/ppermute | solution.py:79
  313.1 17.7 %collective-permute-start.124 = (bf16[192,768]{1,0:T(8,128)(2,1)S(1)}, bf16[192,768]{1,0:T(8,128)(2,1)S(1)}, u32[]{:S(2)}, u32[]{:S(2)}) collective-permute-start(bf16[192,768]{1,0:T(8,128)(2,1)S(1)} %add_convert_fusion.3), channel_id=1, source_target_pairs={{2,0},{4,2},{6,4},{7,6},{5,7},{3,5},{1,3},{0,1},{10,8},{12,10},{14... | collective-permute-start | bytes 884744 | tf_op jit(solution)/shard_map/ppermute | solution.py:1477
  337.1 27.2 %collective-permute-start.120 = (bf16[192,768]{1,0:T(8,128)(2,1)S(1)}, bf16[192,768]{1,0:T(8,128)(2,1)S(1)}, u32[]{:S(2)}, u32[]{:S(2)}) collective-permute-start(bf16[192,768]{1,0:T(8,128)(2,1)S(1)} %add_convert_fusion.7), channel_id=1, source_target_pairs={{0,2},{2,4},{4,6},{6,7},{7,5},{5,3},{3,1},{1,0},{8,10},{10,12},{12... | collective-permute-start | bytes 884744 | tf_op jit(solution)/shard_map/ppermute | solution.py:1477
  337.1 27.3 %collective-permute-start.121 = (bf16[192,768]{1,0:T(8,128)(2,1)S(1)}, bf16[192,768]{1,0:T(8,128)(2,1)S(1)}, u32[]{:S(2)}, u32[]{:S(2)}) collective-permute-start(bf16[192,768]{1,0:T(8,128)(2,1)S(1)} %add_convert_fusion.6), channel_id=1, source_target_pairs={{2,0},{4,2},{6,4},{7,6},{5,7},{3,5},{1,3},{0,1},{10,8},{12,10},{14... | collective-permute-start | bytes 884744 | tf_op jit(solution)/shard_map/ppermute | solution.py:1477
  342.9 23.7 %collective-permute-start.125 = (bf16[192,768]{1,0:T(8,128)(2,1)S(1)}, bf16[192,768]{1,0:T(8,128)(2,1)S(1)}, u32[]{:S(2)}, u32[]{:S(2)}) collective-permute-start(bf16[192,768]{1,0:T(8,128)(2,1)S(1)} %add_convert_fusion.2), channel_id=1, source_target_pairs={{0,2},{2,4},{4,6},{6,7},{7,5},{5,3},{3,1},{1,0},{8,10},{10,12},{12... | collective-permute-start | bytes 884744 | tf_op jit(solution)/shard_map/ppermute | solution.py:1477
  343.0 23.7 %collective-permute-start.126 = (bf16[192,768]{1,0:T(8,128)(2,1)S(1)}, bf16[192,768]{1,0:T(8,128)(2,1)S(1)}, u32[]{:S(2)}, u32[]{:S(2)}) collective-permute-start(bf16[192,768]{1,0:T(8,128)(2,1)S(1)} %add_convert_fusion.1), channel_id=1, source_target_pairs={{2,0},{4,2},{6,4},{7,6},{5,7},{3,5},{1,3},{0,1},{10,8},{12,10},{14... | collective-permute-start | bytes 884744 | tf_op jit(solution)/shard_map/ppermute | solution.py:1477
  364.4 12.8 %collective-permute-start.112 = (bf16[96,768]{1,0:T(8,128)(2,1)S(1)}, bf16[96,768]{1,0:T(8,128)(2,1)S(1)}, u32[]{:S(2)}, u32[]{:S(2)}) collective-permute-start(bf16[96,768]{1,0:T(8,128)(2,1)S(1)} %add_convert_fusion.22), channel_id=1, source_target_pairs={{0,2},{2,4},{4,6},{6,7},{7,5},{5,3},{3,1},{1,0},{8,10},{10,12},{12... | collective-permute-start | bytes 442376 | tf_op jit(solution)/shard_map/ppermute | solution.py:1477
  366.7 15.8 %collective-permute-start.122 = (bf16[192,768]{1,0:T(8,128)(2,1)S(1)}, bf16[192,768]{1,0:T(8,128)(2,1)S(1)}, u32[]{:S(2)}, u32[]{:S(2)}) collective-permute-start(bf16[192,768]{1,0:T(8,128)(2,1)S(1)} %add_convert_fusion.5), channel_id=1, source_target_pairs={{0,8},{8,0},{1,9},{9,1},{2,10},{10,2},{3,11},{11,3},{4,12},{12,4},... | collective-permute-start | bytes 884744 | tf_op jit(solution)/shard_map/ppermute | solution.py:79
  369.0 13.5 %collective-permute-start.127 = (bf16[192,768]{1,0:T(8,128)(2,1)S(1)}, bf16[192,768]{1,0:T(8,128)(2,1)S(1)}, u32[]{:S(2)}, u32[]{:S(2)}) collective-permute-start(bf16[192,768]{1,0:T(8,128)(2,1)S(1)} %add_convert_fusion), channel_id=1, source_target_pairs={{0,8},{8,0},{1,9},{9,1},{2,10},{10,2},{3,11},{11,3},{4,12},{12,4},... | collective-permute-start | bytes 884744 | tf_op jit(solution)/shard_map/ppermute | solution.py:79
  (187 other events, 2260.4 us)

commit v4 on v3

--- a/solution.py
+++ b/solution.py
@@ -1,3 +1,4 @@
+import functools
 import math
 from types import SimpleNamespace as Bag
 
@@ -1165,7 +1166,7 @@
     tokens = 2 * segment
     short = segment + segment // 2
 
-    def body(idx, first, second, hopped, middle, slope, active, normed, vec, wo, wf, wp, *rest):
+    def body(idx, first, second, hopped, middle, slope, vec, wo, wf, wp, *rest):
         outs, rest = rest[:SEATS], rest[SEATS:]
         grad_middle, mine, theirs, sums, grad_out, blocks, gh, out_sems = rest
         wide = jnp.concatenate([first[...], second[...]], axis=0).astype(F32)
@@ -1177,33 +1178,31 @@
         copies = to_seats(blocks, outs, idx, count, out_sems)
         branch = wide.astype(LOW)
 
-        @pl.when(idx[count] == 0)
-        def _():
-            mine[:, :width] = normed[...]
-            mine[:, width:] = gh[...]
-            theirs[:, :width] = branch
-            theirs[:, width:] = active[...]
-
-        @pl.when(idx[count] == 1)
-        def _():
-            mine[:, :width] = branch
-            mine[:, width:] = active[...]
-            theirs[:, :width] = normed[...]
-            theirs[:, width:] = gh[...]
+        def part(values, core):
+            half = values.shape[1] // 2
+            return values[:, core * half : (core + 1) * half]
+
+        def fill(rep):
+            for ref, core in ((mine, rep), (theirs, 1 - rep)):
+                ref[:, : 2 * width] = part(gh, core)
+                ref[:, 2 * width :] = part(branch, core)
+
+        for rep in range(2):
+            pl.when(idx[count] == rep)(functools.partial(fill, rep))
 
         wait_all(copies)
 
     return call(
         body, 14,
         [
-            idx, *grads, hopped, saved.middle, saved.slope, saved.active, saved.normed_two, saved.vec,
+            idx, *grads, hopped, saved.middle, saved.slope, saved.vec,
             *weights,
         ],
-        [SMEM] + [VMEM] * 11,
+        [SMEM] + [VMEM] * 9,
         [((2, short, PAIR), LOW, True)] * SEATS
         + [
-            ((tokens, width), F32, None), ((tokens, 5 * width), LOW, None),
-            ((tokens, 5 * width), LOW, None), ((8, width), F32, None), ((tokens, width), LOW, None),
+            ((tokens, width), F32, None), ((tokens, 5 * width // 2), LOW, None),
+            ((tokens, 5 * width // 2), LOW, None), ((8, width), F32, None), ((tokens, width), LOW, None),
         ],
         [
             pltpu.VMEM((SEATS, 2, short, PAIR), LOW), pltpu.VMEM((tokens, 4 * width), LOW),
@@ -1216,7 +1215,7 @@
     tokens, width = grad_middle.shape
     rows = width // count
     tall = block_rows(segment)
-    kept = [grad_out, saved.normed, saved.attended_low] if keep else []
+    kept = [grad_out] if keep else []
 
     def body(idx, grad_middle, x, vec, *rest):
         held, rest = rest[: len(kept)], rest[len(kept) :]
@@ -1254,17 +1253,13 @@
         sums[2:3] = jnp.sum(gq.astype(F32), axis=0, keepdims=True)
         sums[3:4] = jnp.sum(gv.astype(F32), axis=0, keepdims=True)
         sums[4:8] = jnp.zeros((4, width), F32)
-        grad_out, normed, attended = held
+        (grad_out,) = held
 
         def fill(first, second):
-            first[:, :width] = normed[...]
-            first[:, width : 2 * width] = gq
-            first[:, 2 * width : 3 * width] = normed[...]
-            first[:, 3 * width :] = gk
-            second[:, :width] = normed[...]
-            second[:, width : 2 * width] = gv
-            second[:, 2 * width : 3 * width] = attended[...]
-            second[:, 3 * width :] = grad_out[...]
+            first[:, :width] = gq
+            first[:, width:] = gk
+            second[:, :width] = gv
+            second[:, width:] = grad_out[...]
 
         @pl.when(idx[count] == 0)
         def _():
@@ -1282,8 +1277,8 @@
             pltpu.VMEM((SEATS, 2, tall, PAIR), LOW), pltpu.SemaphoreType.DMA((SEATS,)),
         ],
         [
-            ((tokens, width), F32, None), ((tokens, 4 * width), LOW, None),
-            ((tokens, 4 * width), LOW, None), ((8, width), F32, None),
+            ((tokens, width), F32, None), ((tokens, 2 * width), LOW, None),
+            ((tokens, 2 * width), LOW, None), ((8, width), F32, None),
         ],
         keep,
     )
@@ -1296,62 +1291,52 @@
         copy.start() if start else copy.wait()
 
 
-def ffn_terms_kernel(count, parts, idx):
-    width = parts[0].shape[1] // 5
+def rows_of(refs, span=slice(None)):
+    return jnp.concatenate([ref[:, span] for ref in refs], axis=0)
+
+
+def ffn_terms_kernel(count, normed, active, late, idx):
+    width = normed[0].shape[1]
+    rows, half = width // count, width // 2
+
+    def body(idx, *rest):
+        normed, active, late, rest = rest[:2], rest[2:4], rest[4:6], rest[6:]
+        outs, (inward, outward, sems) = rest[: 2 * count], rest[2 * count :]
+        narrow = rows_of(normed)
+        pieces = []
+        for b in range(2):
+            inward[b * width : (b + 1) * width] = mm_tn(
+                narrow, rows_of(late, slice(b * width, (b + 1) * width))
+            ).astype(LOW)
+            pieces.append([(outs[k], b * rows, rows, b * width, rows, k) for k in range(count)])
+            send_out(inward, pieces[b], idx, sems.at[pl.ds(b * count, count)], True)
+        branch = rows_of(late, slice(2 * width, 2 * width + half))
+        for b in range(4):
+            span = slice(b * width, (b + 1) * width)
+            outward[span] = mm_tn(rows_of(active, span), branch).astype(LOW)
+        pieces.append([(outs[count + k], 0, 4 * rows, 0, 4 * rows, k) for k in range(count)])
+        send_out(outward, pieces[2], idx, sems.at[pl.ds(2 * count, count)], True)
+        for b, scratch in enumerate((inward, inward, outward)):
+            send_out(scratch, pieces[b], idx, sems.at[pl.ds(b * count, count)], False)
+
+    outs = call(
+        body, 5, [idx, *normed, *active, *late], [SMEM] + [VMEM] * 6,
+        [((2 * rows, width), LOW, True)] * count + [((4 * rows, half), LOW, True)] * count,
+        [
+            pltpu.VMEM((2 * width, width), LOW), pltpu.VMEM((4 * width, half), LOW),
+            pltpu.SemaphoreType.DMA((3 * count,)),
+        ],
+    )
+    return outs[:count], outs[count:]
+
+
+def attn_terms_kernel(count, normed, attended, late, sums_one, sums_two, idx):
+    width = normed[0].shape[1]
     rows = width // count
 
     def body(idx, *rest):
-        given, rest = rest[: len(parts)], rest[len(parts) :]
-        outs, (scratch, sems) = rest[: 2 * count], rest[2 * count :]
-        narrow = jnp.concatenate([part[:, :width] for part in given], axis=0)
-
-        def wide(b):
-            span = slice((1 + b) * width, (2 + b) * width)
-            return jnp.concatenate([part[:, span] for part in given], axis=0)
-
-        def pieces(b):
-            return [
-                (outs[b // 2 * count + k], b % 2 * rows, rows, b * width, rows, k) for k in range(count)
-            ]
-
-        @pl.when(idx[count] == 0)
-        def _():
-            for b in range(4):
-                scratch[b * width : (b + 1) * width] = mm_tn(narrow, wide(b)).astype(LOW)
-                send_out(scratch, pieces(b), idx, sems.at[pl.ds(b * count, count)], True)
-            for b in range(4):
-                send_out(scratch, pieces(b), idx, sems.at[pl.ds(b * count, count)], False)
-
-        @pl.when(idx[count] == 1)
-        def _():
-            for b in range(4):
-                scratch[b * width : (b + 1) * width] = mm_tn(wide(b), narrow).astype(LOW)
-            halves = [
-                (outs[ring * count + k], 0, 2 * rows, 2 * rows * ring, 4 * rows, k)
-                for ring in range(2) for k in range(count)
-            ]
-            send_out(scratch, halves, idx, sems, True)
-            send_out(scratch, halves, idx, sems, False)
-
-    outs = call(
-        body, 8, [idx, *parts], [SMEM] + [VMEM] * len(parts),
-        [((2 * rows, width), LOW, True)] * (2 * count),
-        [pltpu.VMEM((4 * width, width), LOW), pltpu.SemaphoreType.DMA((4 * count,))],
-    )
-    return outs[:count], outs[count:]
-
-
-def attn_terms_kernel(count, parts, sums_one, sums_two, idx):
-    width = parts[0].shape[1] // 4
-    rows = width // count
-
-    def body(idx, *rest):
-        parts_in, (one, two), rest = rest[: len(parts)], rest[len(parts) : len(parts) + 2], rest[len(parts) + 2 :]
+        normed, attended, late, (one, two), rest = rest[:2], rest[2:4], rest[4:6], rest[6:8], rest[8:]
         outs, (scratch, notes, sems, note_sems) = rest[: 2 * count], rest[2 * count :]
-
-        def both(b):
-            span = slice(b * width, (b + 1) * width)
-            return jnp.concatenate([part[:, span] for part in parts_in], axis=0)
 
         def pieces(b):
             return [(outs[b * count + k], 0, rows, b * width, rows, k) for k in range(count)]
@@ -1387,14 +1372,26 @@
             ]
         )
         for b in range(2):
-            scratch[b * width : (b + 1) * width] = mm_tn(both(2 * b), both(2 * b + 1)).astype(LOW)
+            grads = rows_of(late, slice(b * width, (b + 1) * width))
+            if b == 0:
+                scratch[:width] = mm_tn(rows_of(normed), grads).astype(LOW)
+            else:
+
+                @pl.when(idx[count] == 0)
+                def _():
+                    scratch[width:] = mm_tn(rows_of(normed), grads).astype(LOW)
+
+                @pl.when(idx[count] == 1)
+                def _():
+                    scratch[width:] = mm_tn(rows_of(attended), grads).astype(LOW)
+
             send_out(scratch, pieces(b), idx, sems.at[pl.ds(b * count, count)], True)
         for b in range(2):
             send_out(scratch, pieces(b), idx, sems.at[pl.ds(b * count, count)], False)
         wait_all(copies)
 
     outs = call(
-        body, 5, [idx, *parts, sums_one, sums_two], [SMEM] + [VMEM] * (len(parts) + 2),
+        body, 5, [idx, *normed, *attended, *late, sums_one, sums_two], [SMEM] + [VMEM] * 8,
         [((rows + NOTE, width), LOW, True)] * count + [((rows, width), LOW, True)] * count,
         [
             pltpu.VMEM((2 * width, width), LOW), pltpu.VMEM((count, NOTE, width), LOW),
@@ -1427,29 +1424,39 @@
         self.count, self.rightward, self.at = count, rightward, 0
         self.last = (chunk, chunk)
         self.own = {0: chunk}
-        self.twin = {0: swap(chunk, REPLICA)}
-
-    def keep(self, k, chunk):
-        self.own[k], self.twin[k] = chunk, swap(chunk, REPLICA)
+        self.twin = {}
+
+    def pass_on(self, values):
+        places = [self.count - self.at, self.at][: len(values)]
+        if len(values) == 1:
+            places = [self.at]
+        for k, value in zip(places, values):
+            self.twin[k] = swap(value, REPLICA)
 
     def step(self, *after):
+        values = hold(self.last, *after)
+        near, far = values
+        if self.at > 0:
+            self.pass_on(values)
+        if self.at == 1:
+            self.twin[0] = swap(hold(self.own[0], values), REPLICA)
         self.at += 1
-        near, far = hold(self.last, *after)
         if self.at < self.count // 2:
             near = lax.ppermute(near, SHARD, self.right)
             far = lax.ppermute(far, SHARD, self.left)
-            self.keep(self.count - self.at, near)
-            self.keep(self.at, far)
+            self.own[self.count - self.at], self.own[self.at] = near, far
             self.last = (near, far)
         else:
             if self.rightward:
                 last = lax.ppermute(near, SHARD, self.right)
             else:
                 last = lax.ppermute(far, SHARD, self.left)
-            self.keep(self.at, last)
+            self.own[self.at] = last
             self.last = (last,)
 
     def lists(self):
+        if self.at not in self.twin:
+            self.pass_on(self.last)
         return [[side[k] for k in range(self.count)] for side in (self.own, self.twin)]
 
 
@@ -1469,12 +1476,14 @@
             else:
                 self.last = (None, lax.ppermute(far, SHARD, self.left))
         else:
+            last = hold([v for v in self.last if v is not None], *after)
             sides = []
             for piece, term in zip((pieces[self.at], pieces[self.count - self.at]), self.last):
-                sides.append(piece if term is None else add_low(piece, term))
-            first, second = hold(tuple(sides), *after)
+                sides.append(piece if term is None else add_low(piece, last.pop(0)))
+            if len(after) > 0 and None in self.last:
+                sides = hold(sides, *after)
             self.last = (
-                lax.ppermute(first, SHARD, self.right), lax.ppermute(second, SHARD, self.left)
+                lax.ppermute(sides[0], SHARD, self.right), lax.ppermute(sides[1], SHARD, self.left)
             )
         self.at -= 1
 
@@ -1517,12 +1526,14 @@
         return lax.ppermute(own, (REPLICA, SHARD), ways[j])
 
     def give_back(x):
-        parts = [
+        return [
             lax.ppermute(
                 x[j * segment : (j + 1) * segment], (REPLICA, SHARD), [(b, a) for a, b in ways[j]]
             )
             for j in range(2)
         ]
+
+    def by_sequence(parts):
         return jnp.stack([jnp.where(even, *parts), jnp.where(even, *parts[::-1])])[None]
 
     def exchange(parts):
@@ -1558,6 +1569,7 @@
     attn_ring.step()
     order_row = lax.dynamic_index_in_dim(group_order, odd, 0).astype(LOW)
     order_rows = jnp.pad(order_row, ((0, NOTE - 1), (0, width - count)))
+    tokens = hold(tokens, attn_ring.last)
     packed = [gather_in(tokens, 0, order_rows), gather_in(tokens, 1)]
     slot = lax.rem(shard // 2 + jnp.arange(2, dtype=jnp.int32), 2)
     which = ((4 * (others // 2) + others % 2)[:, None] + 2 * slot[None, :]).reshape(-1)
@@ -1570,9 +1582,9 @@
     ffn_ring = Rings(
         [GatherRing(hold(own, attn_ring.last), count, i == 0) for i, own in enumerate(ffn_own)]
     )
+    ffn_ring.step()
     attn_ring.step()
     attn_lists = [ring.lists() for ring in attn_ring.rings]
-    ffn_ring.step()
 
     def forward(hopped, attn, before):
         sent, inputs, normed, attn = project_kernel(count, segment, packed, hopped, attn, idx)
@@ -1582,16 +1594,15 @@
         return state, attn, exchange(before[2](back[:SEATS])), back[SEATS:]
 
     def ring_sent(sent):
-        sent = hold(sent, ffn_ring.last)
-        ffn_ring.step()
         ffn_ring.step(sent[1])
         return sent
 
     def ring_arrived(arrived):
+        ffn_ring.step(arrived[1])
         return arrived
 
     def ring_back(back):
-        ffn_ring.step(back[0])
+        ffn_ring.step(back[1])
         return back
 
     def same(values):
@@ -1614,7 +1625,13 @@
     *sent, output, state.attended_low, state.middle, state.normed_two, state.slope, state.active, grad_middle = (
         turn_kernel(count, segment, returned, state.inputs, state.vec, ffn, upstream, idx)
     )
-    acts = give_back(output)
+    kept_rows = state.normed_two, state.active, state.normed, state.attended_low
+    pairs, acts = [], []
+
+    def aside(back):
+        pairs.extend([own, swap(hold(own, back[0]), REPLICA)] for own in kept_rows)
+        acts.extend(give_back(hold(output, back[0])))
+        return back
 
     def backward(sent, grad_middle, grad_out, keep, ties, between):
         arrived = exchange(sent)
@@ -1629,37 +1646,41 @@
 
     early = backward(
         sent, grad_middle, None, False, [],
-        [lambda arrived: [], same, lambda returned: hold(returned, acts)],
-    )
+        [lambda arrived: [], aside, same],
+    )
+    hopped, acts, pairs = lax.optimization_barrier((hop(early[0], True), acts, pairs))
+    acts = by_sequence(acts)
     rings = []
     *sent, grad_middle, mine, theirs, sums_two, grad_out = feed_back_kernel(
-        count, segment, upstream, hop(early[0], True), state, ffn, idx
+        count, segment, upstream, hopped, state, ffn, idx
     )
 
     def ffn_terms(arrived):
-        terms = ffn_terms_kernel(count, hold([mine, swap(theirs, REPLICA)], arrived), idx)
+        terms = ffn_terms_kernel(
+            count, pairs[0], pairs[1], hold([mine, swap(theirs, REPLICA)], arrived), idx
+        )
         rings.append(Rings([ScatterRing(t, count, i == 0) for i, t in enumerate(terms)]))
         rings[0].step()
         return [terms[0][0]]
 
     def ring_back(back):
-        rings[0].step(back[1])
+        back = hold(back, rings[0].last)
+        rings[0].step(back[0])
         return back
 
-    def ring_returned(returned):
-        returned = hold(returned, rings[0].last)
-        rings[0].step(returned[1])
-        return returned
-
-    low, *last = backward(
-        sent, grad_middle, grad_out, True, [], [ffn_terms, ring_back, ring_returned]
-    )
-    terms = attn_terms_kernel(count, [last[1], swap(last[2], REPLICA)], last[3], sums_two, idx)
+    low, *last = backward(sent, grad_middle, grad_out, True, [], [ffn_terms, ring_back, same])
+    terms = attn_terms_kernel(
+        count, pairs[2], pairs[3], [last[1], swap(last[2], REPLICA)], last[3], sums_two, idx
+    )
+    rings.append(Rings([ScatterRing(t, count, i == 0) for i, t in enumerate(terms)]))
     rings[0].step(terms[0][0])
-    rings.append(Rings([ScatterRing(t, count, i == 0) for i, t in enumerate(terms)]))
-    for _ in range(half):
-        rings[1].step()
-    in_grads = give_back(hold(last[0].astype(LOW), low)).astype(F32)
+    rings[1].step()
+    rings[1].step()
+    rings[0].step()
+    in_grads = give_back(hold(last[0].astype(LOW), rings[1].last))
+    rings[1].step()
+    rings[1].step()
+    in_grads = by_sequence(hold(in_grads, rings[1].last)).astype(F32)
 
     def finished(ring):
         total = ring.total().astype(LOW)
@@ -1671,9 +1692,9 @@
 
     feed_totals, totals = [[finished(ring) for ring in pair.rings] for pair in rings]
     fc_grad = jnp.concatenate(
-        [half[0][b * rows : (b + 1) * rows] for half in feed_totals for b in range(2)], axis=1
-    )
-    proj_grad = jnp.concatenate([half[1] for half in feed_totals], axis=0)
+        [part[b * rows : (b + 1) * rows] for part in feed_totals[0] for b in range(2)], axis=1
+    )
+    proj_grad = jnp.concatenate(feed_totals[1], axis=1)
     qkv_grad = jnp.concatenate([totals[0][0][:rows], totals[1][0], totals[0][1][:rows]], axis=1)
     note = totals[0][0][rows:] + totals[0][1][rows:]
     vec = note[:8, :rows]

time: 396 us -> 383 us (0.967)
  waiting for transfers between devices: 167 us -> 153 us
    ppermute x8, waiting for transfers between devices: 26.7 us -> 13.8 us  [exchange(): lax.ppermute(parts[3], (REPLICA, SHARD), diagonal)]
    ppermute x24, waiting for transfers between devices: 47.3 us -> 38.4 us  [the longest x12 24.2 us: step(): lax.ppermute(sides[0], SHARD, self.right)]
    ppermute x12, starting transfers between devices: 21.5 us -> 13.2 us  [step(): near = lax.ppermute(near, SHARD, self.right)]
    ppermute x24, starting transfers between devices: 31.5 us -> 23.5 us  [the longest x12 13.4 us: step(): lax.ppermute(sides[0], SHARD, self.right)]
    ppermute x12, waiting for transfers between devices: 8.06 us -> 14.2 us  [step(): near = lax.ppermute(near, SHARD, self.right)]
    ppermute x8, starting transfers between devices: 5.06 us -> 10.7 us  [exchange(): lax.ppermute(parts[3], (REPLICA, SHARD), diagonal)]
    ppermute x12, waiting for transfers between devices: 19.1 us -> 14 us  [step(): far = lax.ppermute(far, SHARD, self.left)]
    ppermute x8, waiting for transfers between devices: 30.2 us -> 35.1 us  [exchange(): lax.ppermute(parts[1], SHARD, [(s, s ^ 1) for s in range(count)])]
  transfers between devices with their start and end apart: 128 -> 132, of which waited for: 52 -> 52; matrix products, arithmetic and copies ran while one was open for 3% -> 3% of each run, Pallas kernels for 9% -> 8%
where the time goes in v4:
time: 383 us; the launch traced here: 375 us
  waiting for transfers between devices  153 us (40%)
  starting transfers between devices  120 us (31%)
  Pallas kernels  81.5 us (21%)
  other arithmetic  10.6 us (3%)
  local copies, waits for them, and re-layouts  7.5 us (2%)
    pallas_call x13, Pallas kernels, call(): pl.pallas_call(body, in_specs=specs, out_specs=[ANY if space is True else...  81.5 us
    ppermute x8, waiting for transfers between devices, exchange(): lax.ppermute(parts[1], SHARD, [(s, s ^ 1) for s in range(count)])  35.1 us
    ppermute x12, waiting for transfers between devices, step(): lax.ppermute(sides[0], SHARD, self.right)  24.2 us
    ppermute x50, starting transfers between devices, swap(): return lax.ppermute(x, axis, [(0, 1), (1, 0)])  22.1 us
    ppermute x2, waiting for transfers between devices, hop(): return lax.ppermute(values, SECTION, [(1, 0)] if backward else [(0, 1)])  20.7 us
    ppermute x12, starting transfers between devices, step(): far = lax.ppermute(far, SHARD, self.left)  16.4 us
    ppermute x12, waiting for transfers between devices, step(): near = lax.ppermute(near, SHARD, self.right)  14.2 us
    ppermute x12, waiting for transfers between devices, step(): lax.ppermute(sides[1], SHARD, self.left)  14.2 us
  transfers between devices with their start and end apart: 132, of which 52 were waited for; matrix products, arithmetic and copies ran while one was open for 3% of the time, Pallas kernels for 8%

profile of v4, /device:TPU:0, one launch (start us, length us, event | category | flops | bytes accessed | tf_op | source)
XLA Modules:
  0.0 375.4 jit_solution(7825019264310047993)
XLA Ops:
  32.5 3.9 %collective-permute-start.23 = (bf16[96,768]{1,0:T(8,128)(2,1)S(1)}, bf16[96,768]{1,0:T(8,128)(2,1)S(1)}, u32[]{:S(2)}, u32[]{:S(2)}) collective-permute-start(bf16[96,768]{1,0:T(8,128)(2,1)S(1)} %collective-permute-done.22.rest_22_.rest_26_), channel_id=1, source_target_pairs={{0,2},{2,4},{4,6},{6,7},{7,5},{5,3},{3,1},{1,0},{8,10},{10,12},{12... | collective-permute-start | bytes 442376 | tf_op jit(solution)/shard_map/ppermute | solution.py:1445
  39.7 4.0 %collective-permute-start.21 = (bf16[96,768]{1,0:T(8,128)(2,1)}, bf16[96,768]{1,0:T(8,128)(2,1)S(1)}, u32[]{:S(2)}, u32[]{:S(2)}) collective-permute-start(bf16[96,768]{1,0:T(8,128)(2,1)} %collective-permute-done.20.rest_19_.rest_23_), channel_id=1, source_target_pairs={{2,0},{4,2},{6,4},{7,6},{5,7},{3,5},{1,3},{0,1},{10,8},{12,10},{14... | collective-permute-start | bytes 442376 | tf_op jit(solution)/shard_map/ppermute | solution.py:1453
  56.0 5.2 %shard_map.238 = (bf16[2,576,128]{2,1,0:T(8,128)(2,1)}, bf16[2,576,128]{2,1,0:T(8,128)(2,1)}, bf16[2,576,128]{2,1,0:T(8,128)(2,1)}, bf16[2,576,128]{2,1,0:T(8,12...) custom-call(s32[14]{0:T(128)S(1)} %pad_add_fusion.idx, ...), custom_call_target="tpu_custom_call" | custom-call | bytes 25830000 | tf_op jit(solution)/shard_map/pallas_call | solution.py:568
  67.2 3.7 collective-permute-done.40.rest_38_
  73.4 5.3 %collective-permute-done.32.rest_1_ = bf16[2,576,128]{2,1,0:T(8,128)(2,1)S(1)} collective-permute-done((bf16[2,576,128]{2,1,0:T(8,128)(2,1)}, bf16[2,576,128]{2,1,0:T(8,128)(2,1)S(1)}, u32[]{:S(2)}, u32[]{:S(2)}) %collective-permute-start.32) | collective-permute-done | bytes 294944 | tf_op jit(solution)/shard_map/ppermute | solution.py:1543
  84.4 3.5 collective-permute-done.56.rest_58_
  98.3 5.9 %shard_map.239 = (bf16[2,192,128]{2,1,0:T(8,128)(2,1)}, bf16[2,192,128]{2,1,0:T(8,128)(2,1)}, bf16[2,192,128]{2,1,0:T(8,128)(2,1)}, bf16[2,192,128]{2,1,0:T(8,128)(2,1)}) custom-call(s32[8]{0:T(128)S(1)} %multiply_reduce_fusion.at, bf16[2,576,128]{2,1,0:T(8,128)(2,1)} %get-tuple-element.177.rest_0_, ...), custom_call_target="tpu_custom_call" | custom-call | bytes 33210000 | tf_op jit(solution)/shard_map/pallas_call | solution.py:568
  116.2 6.7 %collective-permute-done.44.rest_40_ = bf16[192,768]{1,0:T(8,128)(2,1)S(1)} collective-permute-done((bf16[192,768]{1,0:T(8,128)(2,1)S(1)}, bf16[192,768]{1,0:T(8,128)(2,1)S(1)}, u32[]{:S(2)}, u32[]{:S(2)}) %collective-permute-start.44) | collective-permute-done | bytes 294944 | tf_op jit(solution)/shard_map/ppermute | solution.py:1451
  126.2 8.2 %shard_map.240 = (bf16[256,768]{1,0:T(8,128)(2,1)S(1)}, bf16[8,96,768]{2,1,0:T(8,128)(2,1)S(1)}, bf16[4,8,96,768]{3,2,1,0:T(8,128)(2,1)S(1)}, bf16[8,4,96,768]{3,2,1,0:T(8,128)(2,1)S(1)}) custom-call(s32[14]{0:T(128)S(1)} %pad_add_fusion.idx, bf16[256,768]{1,0:T(8,128)(2,1)S(1)} %get-tuple-element.174.x, f32[12,768]{1,0:T(8,128)S(1)} %get-tuple-element.175.vec.rest_4_, ...), custom_call_target="tpu_custom_call" | custom-call | bytes 36900000 | tf_op jit(solution)/shard_map/pallas_call | solution.py:568
  137.8 8.6 %collective-permute-done.68.rest_0_ = bf16[256,768]{1,0:T(8,128)(2,1)S(1)} collective-permute-done((bf16[256,768]{1,0:T(8,128)(2,1)S(1)}, bf16[256,768]{1,0:T(8,128)(2,1)S(1)}, u32[]{:S(2)}, u32[]{:S(2)}) %collective-permute-start.68) | collective-permute-done | bytes 393248 | tf_op jit(solution)/shard_map/ppermute | solution.py:1618
  154.1 4.1 %collective-permute-done.70.second = bf16[128,768]{1,0:T(8,128)(2,1)S(1)} collective-permute-done((bf16[128,768]{1,0:T(8,128)(2,1)S(1)}, bf16[128,768]{1,0:T(8,128)(2,1)S(1)}, u32[]{:S(2)}, u32[]{:S(2)}) %collective-permute-start.70) | collective-permute-done | bytes 196640 | tf_op jit(solution)/shard_map/ppermute | solution.py:1526
  163.1 6.1 %shard_map.242 = (bf16[2,192,128]{2,1,0:T(8,128)(2,1)}, bf16[2,192,128]{2,1,0:T(8,128)(2,1)}, bf16[2,192,128]{2,1,0:T(8,128)(2,1)}, bf16[2,192,128]{2,1,0:T(8,12...) custom-call(s32[8]{0:T(128)S(1)} %multiply_reduce_fusion.at, ...), custom_call_target="tpu_custom_call" | custom-call | bytes 33210000 | tf_op jit(solution)/shard_map/pallas_call | solution.py:568
  171.7 3.4 collective-permute-done.74.rest_1_
  177.3 9.8 %shard_map.243 = (bf16[2,192,128]{2,1,0:T(8,128)(2,1)}, bf16[2,192,128]{2,1,0:T(8,128)(2,1)}, bf16[2,192,128]{2,1,0:T(8,128)(2,1)}, bf16[2,192,128]{2,1,0:T(8,12...) custom-call(s32[14]{0:T(128)S(1)} %pad_add_fusion.idx, ...), custom_call_target="tpu_custom_call" | custom-call | bytes 36900000 | tf_op jit(solution)/shard_map/pallas_call | solution.py:568
  189.3 3.7 collective-permute-done.77.rest_5_
  193.4 11.1 %shard_map.244 = (bf16[2,576,128]{2,1,0:T(8,128)(2,1)}, bf16[2,576,128]{2,1,0:T(8,128)(2,1)}, bf16[2,576,128]{2,1,0:T(8,128)(2,1)}, bf16[2,576,128]{2,1,0:T(8,128)(2,1)}) custom-call(s32[8]{0:T(128)S(1)} %multiply_reduce_fusion.at, f32[2,1024,128]{2,1,0:T(8,128)S(1)} %get-tuple-element.223.attended, f32[1024,128]{1,0:T(8,128)S(1)} %get-tuple-element.224.total, ...), custom_call_target="tpu_custom_call" | custom-call | bytes 51660000 | tf_op jit(solution)/shard_map/pallas_call | solution.py:568
  208.5 6.8 %collective-permute-done.80.rest_1_ = bf16[2,576,128]{2,1,0:T(8,128)(2,1)S(1)} collective-permute-done((bf16[2,576,128]{2,1,0:T(8,128)(2,1)}, bf16[2,576,128]{2,1,0:T(8,128)(2,1)S(1)}, u32[]{:S(2)}, u32[]{:S(2)}) %collective-permute-start.80) | collective-permute-done | bytes 294944 | tf_op jit(solution)/shard_map/ppermute | solution.py:1543
  225.3 12.1 %collective-permute-done.83.hopped = bf16[256,768]{1,0:T(8,128)(2,1)S(1)} collective-permute-done((bf16[256,768]{1,0:T(8,128)(2,1)S(1)}, bf16[256,768]{1,0:T(8,128)(2,1)S(1)}, u32[]{:S(2)}, u32[]{:S(2)}) %collective-permute-start.83) | collective-permute-done | bytes 393248 | tf_op jit(solution)/shard_map/ppermute | solution.py:1618
  237.4 5.1 %shard_map.246 = (bf16[2,192,128]{2,1,0:T(8,128)(2,1)}, bf16[2,192,128]{2,1,0:T(8,128)(2,1)}, bf16[2,192,128]{2,1,0:T(8,128)(2,1)}, bf16[2,192,128]{2,1,0:T(8,12...) custom-call(s32[14]{0:T(128)S(1)} %pad_add_fusion.idx, ...), custom_call_target="tpu_custom_call" | custom-call | bytes 51660000 | tf_op jit(solution)/shard_map/pallas_call | solution.py:568
  244.8 3.7 collective-permute-done.90.rest_5_
  249.7 5.3 %shard_map.247 = (bf16[192,768]{1,0:T(8,128)(2,1)}, bf16[192,768]{1,0:T(8,128)(2,1)}, bf16[192,768]{1,0:T(8,128)(2,1)}, bf16[192,768]{1,0:T(8,128)(2,1)}, bf16[1...) custom-call(s32[14]{0:T(128)S(1)} %pad_add_fusion.idx, ...), custom_call_target="tpu_custom_call" | custom-call | bytes 18450000 | tf_op jit(solution)/shard_map/pallas_call | solution.py:568
  258.2 11.1 %shard_map.248 = (bf16[2,576,128]{2,1,0:T(8,128)(2,1)}, bf16[2,576,128]{2,1,0:T(8,128)(2,1)}, bf16[2,576,128]{2,1,0:T(8,128)(2,1)}, bf16[2,576,128]{2,1,0:T(8,128)(2,1)}) custom-call(s32[8]{0:T(128)S(1)} %multiply_reduce_fusion.at, f32[2,1024,128]{2,1,0:T(8,128)S(1)} %get-tuple-element.223.attended, f32[1024,128]{1,0:T(8,128)S(1)} %get-tuple-element.224.total, ...), custom_call_target="tpu_custom_call" | custom-call | bytes 51660000 | tf_op jit(solution)/shard_map/pallas_call | solution.py:568
  271.6 8.0 %collective-permute-done.96.rest_2_ = bf16[2,576,128]{2,1,0:T(8,128)(2,1)S(1)} collective-permute-done((bf16[2,576,128]{2,1,0:T(8,128)(2,1)}, bf16[2,576,128]{2,1,0:T(8,128)(2,1)S(1)}, u32[]{:S(2)}, u32[]{:S(2)}) %collective-permute-start.96) | collective-permute-done | bytes 294944 | tf_op jit(solution)/shard_map/ppermute | solution.py:1543
  279.6 3.7 collective-permute-done.98.rest_4_
  283.3 3.9 %shard_map.249 = (bf16[256,768]{1,0:T(8,128)(2,1)}, f32[256,768]{1,0:T(8,128)S(1)}, bf16[256,1536]{1,0:T(8,128)(2,1)S(1)}, bf16[256,1536]{1,0:T(8,128)(2,1)S(1)}, f32[8,768]{1,0:T(8,128)S(1)}) custom-call(s32[14]{0:T(128)S(1)} %pad_add_fusion.idx, f32[256,768]{1,0:T(8,128)S(1)} %get-tuple-element.248.grad_middle, bf16[256,768]{1,0:T(8,128)(2,1)S(1)} %get-tuple-element.205.x, ...), custom_call_target="tpu_custom_call" | custom-call | bytes 29520000 | tf_op jit(solution)/shard_map/pallas_call | solution.py:568
  293.6 3.8 %shard_map.250 = (bf16[112,768]{1,0:T(8,128)(2,1)}, bf16[112,768]{1,0:T(8,128)(2,1)}, bf16[112,768]{1,0:T(8,128)(2,1)}, bf16[112,768]{1,0:T(8,128)(2,1)}, bf16[1...) custom-call(s32[14]{0:T(128)S(1)} %pad_add_fusion.idx, ...), custom_call_target="tpu_custom_call" | custom-call | bytes 18450000 | tf_op jit(solution)/shard_map/pallas_call | solution.py:568
  297.4 6.5 %collective-permute-done.125 = bf16[384,384]{1,0:T(8,128)(2,1)S(1)} collective-permute-done((bf16[384,384]{1,0:T(8,128)(2,1)S(1)}, bf16[384,384]{1,0:T(8,128)(2,1)S(1)}, u32[]{:S(2)}, u32[]{:S(2)}) %collective-permute-start.125) | collective-permute-done | bytes 294944 | tf_op jit(solution)/shard_map/ppermute | solution.py:1486
  317.6 5.1 %collective-permute-done.122 = bf16[192,768]{1,0:T(8,128)(2,1)S(1)} collective-permute-done((bf16[192,768]{1,0:T(8,128)(2,1)S(1)}, bf16[192,768]{1,0:T(8,128)(2,1)S(1)}, u32[]{:S(2)}, u32[]{:S(2)}) %collective-permute-start.122) | collective-permute-done | bytes 294944 | tf_op jit(solution)/shard_map/ppermute | solution.py:1486
  325.0 6.0 %collective-permute-done.112 = bf16[96,768]{1,0:T(8,128)(2,1)S(1)} collective-permute-done((bf16[96,768]{1,0:T(8,128)(2,1)S(1)}, bf16[96,768]{1,0:T(8,128)(2,1)S(1)}, u32[]{:S(2)}, u32[]{:S(2)}) %collective-permute-start.112) | collective-permute-done | bytes 147488 | tf_op jit(solution)/shard_map/ppermute | solution.py:1486
  342.6 5.4 %collective-permute-done.108 = bf16[112,768]{1,0:T(8,128)(2,1)S(1)} collective-permute-done((bf16[112,768]{1,0:T(8,128)(2,1)S(1)}, bf16[112,768]{1,0:T(8,128)(2,1)S(1)}, u32[]{:S(2)}, u32[]{:S(2)}) %collective-permute-start.108) | collective-permute-done | bytes 172064 | tf_op jit(solution)/shard_map/ppermute | solution.py:1486
  350.1 4.4 %collective-permute-done.115 = bf16[96,768]{1,0:T(8,128)(2,1)S(1)} collective-permute-done((bf16[96,768]{1,0:T(8,128)(2,1)S(1)}, bf16[96,768]{1,0:T(8,128)(2,1)S(1)}, u32[]{:S(2)}, u32[]{:S(2)}) %collective-permute-start.115) | collective-permute-done | bytes 147488 | tf_op jit(solution)/shard_map/ppermute | solution.py:1486
  360.4 4.9 %collective-permute-done.109 = bf16[112,768]{1,0:T(8,128)(2,1)S(1)} collective-permute-done((bf16[112,768]{1,0:T(8,128)(2,1)S(1)}, bf16[112,768]{1,0:T(8,128)(2,1)S(1)}, u32[]{:S(2)}, u32[]{:S(2)}) %collective-permute-start.109) | collective-permute-done | bytes 172064 | tf_op jit(solution)/shard_map/ppermute | solution.py:1486
  (498 shorter events, 183.4 us)
Async XLA Ops:
  19.5 13.0 %collective-permute-start.5 = (bf16[128,768]{1,0:T(8,128)(2,1)S(1)}, bf16[128,768]{1,0:T(8,128)(2,1)S(1)}, u32[]{:S(2)}, u32[]{:S(2)}) collective-permute-start(bf16[128,768]{1,0:T(8,128)(2,1)S(1)} %get-tuple-element.350), channel_id=1, source_target_pairs={{0,2},{1,3},{2,0},{3,1},{4,10},{5,11},{6,8},{7,9},{8,6},{9,7},{10,... | collective-permute-start | bytes 589832 | tf_op jit(solution)/shard_map/ppermute | solution.py:1526
  21.0 15.3 %collective-permute-start.4 = (bf16[144,768]{1,0:T(8,128)(2,1)S(1)}, bf16[144,768]{1,0:T(8,128)(2,1)S(1)}, u32[]{:S(2)}, u32[]{:S(2)}) collective-permute-start(bf16[144,768]{1,0:T(8,128)(2,1)S(1)} %fusion.5), channel_id=1, source_target_pairs={{0,0},{1,1},{2,2},{3,3},{4,8},{5,9},{6,10},{7,11},{8,4},{9,5},{10,... | collective-permute-start | bytes 663560 | tf_op jit(solution)/shard_map/ppermute | solution.py:1526
  24.2 12.2 %collective-permute-start.26 = (bf16[96,768]{1,0:T(8,128)(2,1)S(1)}, bf16[96,768]{1,0:T(8,128)(2,1)S(1)}, u32[]{:S(2)}, u32[]{:S(2)}) collective-permute-start(bf16[96,768]{1,0:T(8,128)(2,1)S(1)} %collective-permute-done.19.rest_18_.rest_22_), channel_id=1, source_target_pairs={{0,8},{8,0},{1,9},{9,1},{2,10},{10,2},{3,11},{11,3},{4,12},{12,4},... | collective-permute-start | bytes 442376 | tf_op jit(solution)/shard_map/ppermute | solution.py:80
  47.8 13.4 %collective-permute-start.39 = (bf16[192,768]{1,0:T(8,128)(2,1)S(1)}, bf16[192,768]{1,0:T(8,128)(2,1)}, u32[]{:S(2)}, u32[]{:S(2)}) collective-permute-start(bf16[192,768]{1,0:T(8,128)(2,1)S(1)} %get-tuple-element.191.rest_36_), channel_id=1, source_target_pairs={{0,2},{2,4},{4,6},{6,7},{7,5},{5,3},{3,1},{1,0},{8,10},{10,12},{12... | collective-permute-start | bytes 884744 | tf_op jit(solution)/shard_map/ppermute | solution.py:1445
  50.2 14.7 %collective-permute-start.54 = (bf16[192,768]{1,0:T(8,128)(2,1)S(1)}, bf16[192,768]{1,0:T(8,128)(2,1)}, u32[]{:S(2)}, u32[]{:S(2)}) collective-permute-start(bf16[192,768]{1,0:T(8,128)(2,1)S(1)} %get-tuple-element.199.rest_52_), channel_id=1, source_target_pairs={{0,2},{2,4},{4,6},{6,7},{7,5},{5,3},{3,1},{1,0},{8,10},{10,12},{12... | collective-permute-start | bytes 884744 | tf_op jit(solution)/shard_map/ppermute | solution.py:1445
  53.2 13.5 %collective-permute-start.53 = (bf16[192,768]{1,0:T(8,128)(2,1)S(1)}, bf16[192,768]{1,0:T(8,128)(2,1)S(1)}, u32[]{:S(2)}, u32[]{:S(2)}) collective-permute-start(bf16[192,768]{1,0:T(8,128)(2,1)S(1)} %get-tuple-element.199.rest_52_), channel_id=1, source_target_pairs={{2,0},{4,2},{6,4},{7,6},{5,7},{3,5},{1,3},{0,1},{10,8},{12,10},{14... | collective-permute-start | bytes 884744 | tf_op jit(solution)/shard_map/ppermute | solution.py:1446
  64.9 13.8 %collective-permute-start.32 = (bf16[2,576,128]{2,1,0:T(8,128)(2,1)}, bf16[2,576,128]{2,1,0:T(8,128)(2,1)S(1)}, u32[]{:S(2)}, u32[]{:S(2)}) collective-permute-start(bf16[2,576,128]{2,1,0:T(8,128)(2,1)} %get-tuple-element.178), channel_id=1, source_target_pairs={{0,1},{1,0},{2,3},{3,2},{4,5},{5,4},{6,7},{7,6},{8,9},{9,8},{10,11... | collective-permute-start | bytes 884744 | tf_op jit(solution)/shard_map/ppermute | solution.py:1543
  87.9 25.6 %collective-permute-start.47 = (bf16[192,768]{1,0:T(8,128)(2,1)S(1)}, bf16[192,768]{1,0:T(8,128)(2,1)S(1)}, u32[]{:S(2)}, u32[]{:S(2)}) collective-permute-start(bf16[192,768]{1,0:T(8,128)(2,1)S(1)} %collective-permute-done.40.rest_38_), channel_id=1, source_target_pairs={{0,8},{8,0},{1,9},{9,1},{2,10},{10,2},{3,11},{11,3},{4,12},{12,4},... | collective-permute-start | bytes 884744 | tf_op jit(solution)/shard_map/ppermute | solution.py:80
  88.0 26.8 %collective-permute-start.51 = (bf16[192,768]{1,0:T(8,128)(2,1)S(1)}, bf16[192,768]{1,0:T(8,128)(2,1)S(1)}, u32[]{:S(2)}, u32[]{:S(2)}) collective-permute-start(bf16[192,768]{1,0:T(8,128)(2,1)S(1)} %collective-permute-done.41.rest_42_), channel_id=1, source_target_pairs={{0,8},{8,0},{1,9},{9,1},{2,10},{10,2},{3,11},{11,3},{4,12},{12,4},... | collective-permute-start | bytes 884744 | tf_op jit(solution)/shard_map/ppermute | solution.py:80
  88.5 15.8 %collective-permute-start.43 = (bf16[192,768]{1,0:T(8,128)(2,1)S(1)}, bf16[192,768]{1,0:T(8,128)(2,1)S(1)}, u32[]{:S(2)}, u32[]{:S(2)}) collective-permute-start(bf16[192,768]{1,0:T(8,128)(2,1)S(1)} %collective-permute-done.41.rest_42_), channel_id=1, source_target_pairs={{0,2},{2,4},{4,6},{6,7},{7,5},{5,3},{3,1},{1,0},{8,10},{10,12},{12... | collective-permute-start | bytes 884744 | tf_op jit(solution)/shard_map/ppermute | solution.py:1445
  92.4 12.7 %collective-permute-start.57 = (bf16[192,768]{1,0:T(8,128)(2,1)S(1)}, bf16[192,768]{1,0:T(8,128)(2,1)S(1)}, u32[]{:S(2)}, u32[]{:S(2)}) collective-permute-start(bf16[192,768]{1,0:T(8,128)(2,1)S(1)} %collective-permute-done.55.rest_54_), channel_id=1, source_target_pairs={{2,0},{4,2},{6,4},{7,6},{5,7},{3,5},{1,3},{0,1},{10,8},{12,10},{14... | collective-permute-start | bytes 884744 | tf_op jit(solution)/shard_map/ppermute | solution.py:1446
  150.7 12.4 %collective-permute-start.73 = (bf16[2,576,128]{2,1,0:T(8,128)(2,1)}, bf16[2,576,128]{2,1,0:T(8,128)(2,1)S(1)}, u32[]{:S(2)}, u32[]{:S(2)}) collective-permute-start(bf16[2,576,128]{2,1,0:T(8,128)(2,1)} %get-tuple-element.213), channel_id=1, source_target_pairs={{0,9},{1,8},{2,11},{3,10},{4,13},{5,12},{6,15},{7,14},{8,1},{9,0},... | collective-permute-start | bytes 884744 | tf_op jit(solution)/shard_map/ppermute | solution.py:1545
  204.5 33.0 %collective-permute-start.87 = (bf16[256,3072]{1,0:T(8,128)(2,1)S(1)}, bf16[256,3072]{1,0:T(8,128)(2,1)S(1)}, u32[]{:S(2)}, u32[]{:S(2)}) collective-permute-start(bf16[256,3072]{1,0:T(8,128)(2,1)S(1)} %get-tuple-element.256.rest_2_), channel_id=1, source_target_pairs={{0,8},{8,0},{1,9},{9,1},{2,10},{10,2},{3,11},{11,3},{4,12},{12,4},... | collective-permute-start | bytes 4718600 | tf_op jit(solution)/shard_map/ppermute | solution.py:80
  206.0 13.9 %collective-permute-start.82 = (bf16[2,576,128]{2,1,0:T(8,128)(2,1)}, bf16[2,576,128]{2,1,0:T(8,128)(2,1)S(1)}, u32[]{:S(2)}, u32[]{:S(2)}) collective-permute-start(bf16[2,576,128]{2,1,0:T(8,128)(2,1)} %get-tuple-element.232), channel_id=1, source_target_pairs={{0,9},{1,8},{2,11},{3,10},{4,13},{5,12},{6,15},{7,14},{8,1},{9,0},... | collective-permute-start | bytes 884744 | tf_op jit(solution)/shard_map/ppermute | solution.py:1545
  207.4 16.1 %collective-permute-start.85 = (bf16[128,768]{1,0:T(8,128)(2,1)S(1)}, bf16[128,768]{1,0:T(8,128)(2,1)S(1)}, u32[]{:S(2)}, u32[]{:S(2)}) collective-permute-start(bf16[128,768]{1,0:T(8,128)(2,1)S(1)} %get-tuple-element.346), channel_id=1, source_target_pairs={{2,0},{3,1},{0,2},{1,3},{10,4},{11,5},{8,6},{9,7},{6,8},{7,9},{4,1... | collective-permute-start | bytes 589832 | tf_op jit(solution)/shard_map/ppermute | solution.py:1530
  223.6 13.8 %collective-permute-start.83 = (bf16[256,768]{1,0:T(8,128)(2,1)S(1)}, bf16[256,768]{1,0:T(8,128)(2,1)S(1)}, u32[]{:S(2)}, u32[]{:S(2)}) collective-permute-start(bf16[256,768]{1,0:T(8,128)(2,1)S(1)} %shard_map.245), channel_id=1, source_target_pairs={{16,0},{17,1},{18,2},{19,3},{20,4},{21,5},{22,6},{23,7},{24,8},{25... | collective-permute-start | bytes 1179656 | tf_op jit(solution)/shard_map/ppermute | solution.py:1618
  255.0 14.4 %collective-permute-start.94 = (bf16[192,768]{1,0:T(8,128)(2,1)}, bf16[192,768]{1,0:T(8,128)(2,1)S(1)}, u32[]{:S(2)}, u32[]{:S(2)}) collective-permute-start(bf16[192,768]{1,0:T(8,128)(2,1)} %get-tuple-element.267), channel_id=1, source_target_pairs={{0,2},{2,4},{4,6},{6,7},{7,5},{5,3},{3,1},{1,0},{8,10},{10,12},{12... | collective-permute-start | bytes 884744 | tf_op jit(solution)/shard_map/ppermute | solution.py:1475
  255.8 13.6 %collective-permute-start.95 = (bf16[384,384]{1,0:T(8,128)(2,1)}, bf16[384,384]{1,0:T(8,128)(2,1)S(1)}, u32[]{:S(2)}, u32[]{:S(2)}) collective-permute-start(bf16[384,384]{1,0:T(8,128)(2,1)} %get-tuple-element.268), channel_id=1, source_target_pairs={{2,0},{4,2},{6,4},{7,6},{5,7},{3,5},{1,3},{0,1},{10,8},{12,10},{14... | collective-permute-start | bytes 884744 | tf_op jit(solution)/shard_map/ppermute | solution.py:1477
  270.0 13.4 %collective-permute-start.98 = (bf16[2,576,128]{2,1,0:T(8,128)(2,1)}, bf16[2,576,128]{2,1,0:T(8,128)(2,1)S(1)}, u32[]{:S(2)}, u32[]{:S(2)}) collective-permute-start(bf16[2,576,128]{2,1,0:T(8,128)(2,1)} %get-tuple-element.272), channel_id=1, source_target_pairs={{0,9},{1,8},{2,11},{3,10},{4,13},{5,12},{6,15},{7,14},{8,1},{9,0},... | collective-permute-start | bytes 884744 | tf_op jit(solution)/shard_map/ppermute | solution.py:1545
  288.6 15.9 %collective-permute-start.118 = (bf16[192,768]{1,0:T(8,128)(2,1)S(1)}, bf16[192,768]{1,0:T(8,128)(2,1)S(1)}, u32[]{:S(2)}, u32[]{:S(2)}) collective-permute-start(bf16[192,768]{1,0:T(8,128)(2,1)S(1)} %add_convert_fusion.11), channel_id=1, source_target_pairs={{0,2},{2,4},{4,6},{6,7},{7,5},{5,3},{3,1},{1,0},{8,10},{10,12},{12... | collective-permute-start | bytes 884744 | tf_op jit(solution)/shard_map/ppermute | solution.py:1486
  289.4 15.2 %collective-permute-start.119 = (bf16[192,768]{1,0:T(8,128)(2,1)S(1)}, bf16[192,768]{1,0:T(8,128)(2,1)S(1)}, u32[]{:S(2)}, u32[]{:S(2)}) collective-permute-start(bf16[192,768]{1,0:T(8,128)(2,1)S(1)} %copy-done.89), channel_id=1, source_target_pairs={{2,0},{4,2},{6,4},{7,6},{5,7},{3,5},{1,3},{0,1},{10,8},{12,10},{14... | collective-permute-start | bytes 884744 | tf_op jit(solution)/shard_map/ppermute | solution.py:1486
  290.7 13.2 %collective-permute-start.125 = (bf16[384,384]{1,0:T(8,128)(2,1)S(1)}, bf16[384,384]{1,0:T(8,128)(2,1)S(1)}, u32[]{:S(2)}, u32[]{:S(2)}) collective-permute-start(bf16[384,384]{1,0:T(8,128)(2,1)S(1)} %copy-done.90), channel_id=1, source_target_pairs={{0,2},{2,4},{4,6},{6,7},{7,5},{5,3},{3,1},{1,0},{8,10},{10,12},{12... | collective-permute-start | bytes 884744 | tf_op jit(solution)/shard_map/ppermute | solution.py:1486
  291.4 13.1 %collective-permute-start.126 = (bf16[384,384]{1,0:T(8,128)(2,1)S(1)}, bf16[384,384]{1,0:T(8,128)(2,1)S(1)}, u32[]{:S(2)}, u32[]{:S(2)}) collective-permute-start(bf16[384,384]{1,0:T(8,128)(2,1)S(1)} %add_convert_fusion.5), channel_id=1, source_target_pairs={{2,0},{4,2},{6,4},{7,6},{5,7},{3,5},{1,3},{0,1},{10,8},{12,10},{14... | collective-permute-start | bytes 884744 | tf_op jit(solution)/shard_map/ppermute | solution.py:1486
  308.7 14.0 %collective-permute-start.122 = (bf16[192,768]{1,0:T(8,128)(2,1)S(1)}, bf16[192,768]{1,0:T(8,128)(2,1)S(1)}, u32[]{:S(2)}, u32[]{:S(2)}) collective-permute-start(bf16[192,768]{1,0:T(8,128)(2,1)S(1)} %add_convert_fusion.8), channel_id=1, source_target_pairs={{2,0},{4,2},{6,4},{7,6},{5,7},{3,5},{1,3},{0,1},{10,8},{12,10},{14... | collective-permute-start | bytes 884744 | tf_op jit(solution)/shard_map/ppermute | solution.py:1486
  312.8 20.4 %collective-permute-start.129 = (bf16[384,384]{1,0:T(8,128)(2,1)S(1)}, bf16[384,384]{1,0:T(8,128)(2,1)S(1)}, u32[]{:S(2)}, u32[]{:S(2)}) collective-permute-start(bf16[384,384]{1,0:T(8,128)(2,1)S(1)} %add_convert_fusion.2), channel_id=1, source_target_pairs={{2,0},{4,2},{6,4},{7,6},{5,7},{3,5},{1,3},{0,1},{10,8},{12,10},{14... | collective-permute-start | bytes 884744 | tf_op jit(solution)/shard_map/ppermute | solution.py:1486
  315.2 19.0 %collective-permute-start.127 = (bf16[384,384]{1,0:T(8,128)(2,1)S(1)}, bf16[384,384]{1,0:T(8,128)(2,1)S(1)}, u32[]{:S(2)}, u32[]{:S(2)}) collective-permute-start(bf16[384,384]{1,0:T(8,128)(2,1)S(1)} %add_convert_fusion.4), channel_id=1, source_target_pairs={{0,2},{2,4},{4,6},{6,7},{7,5},{5,3},{3,1},{1,0},{8,10},{10,12},{12... | collective-permute-start | bytes 884744 | tf_op jit(solution)/shard_map/ppermute | solution.py:1486
  316.5 14.6 %collective-permute-start.112 = (bf16[96,768]{1,0:T(8,128)(2,1)S(1)}, bf16[96,768]{1,0:T(8,128)(2,1)S(1)}, u32[]{:S(2)}, u32[]{:S(2)}) collective-permute-start(bf16[96,768]{1,0:T(8,128)(2,1)S(1)} %add_convert_fusion.22), channel_id=1, source_target_pairs={{0,2},{2,4},{4,6},{6,7},{7,5},{5,3},{3,1},{1,0},{8,10},{10,12},{12... | collective-permute-start | bytes 442376 | tf_op jit(solution)/shard_map/ppermute | solution.py:1486
  331.9 16.1 %collective-permute-start.113 = (bf16[96,768]{1,0:T(8,128)(2,1)S(1)}, bf16[96,768]{1,0:T(8,128)(2,1)S(1)}, u32[]{:S(2)}, u32[]{:S(2)}) collective-permute-start(bf16[96,768]{1,0:T(8,128)(2,1)S(1)} %add_convert_fusion.21), channel_id=1, source_target_pairs={{0,2},{2,4},{4,6},{6,7},{7,5},{5,3},{3,1},{1,0},{8,10},{10,12},{12... | collective-permute-start | bytes 442376 | tf_op jit(solution)/shard_map/ppermute | solution.py:1486
  334.2 20.7 %collective-permute-start.123 = (bf16[192,768]{1,0:T(8,128)(2,1)S(1)}, bf16[192,768]{1,0:T(8,128)(2,1)S(1)}, u32[]{:S(2)}, u32[]{:S(2)}) collective-permute-start(bf16[192,768]{1,0:T(8,128)(2,1)S(1)} %add_convert_fusion.7), channel_id=1, source_target_pairs={{2,0},{4,2},{6,4},{7,6},{5,7},{3,5},{1,3},{0,1},{10,8},{12,10},{14... | collective-permute-start | bytes 884744 | tf_op jit(solution)/shard_map/ppermute | solution.py:1486
  335.1 21.5 %collective-permute-start.121 = (bf16[192,768]{1,0:T(8,128)(2,1)S(1)}, bf16[192,768]{1,0:T(8,128)(2,1)S(1)}, u32[]{:S(2)}, u32[]{:S(2)}) collective-permute-start(bf16[192,768]{1,0:T(8,128)(2,1)S(1)} %add_convert_fusion.9), channel_id=1, source_target_pairs={{0,2},{2,4},{4,6},{6,7},{7,5},{5,3},{3,1},{1,0},{8,10},{10,12},{12... | collective-permute-start | bytes 884744 | tf_op jit(solution)/shard_map/ppermute | solution.py:1486
  338.3 19.2 %collective-permute-start.130 = (bf16[384,384]{1,0:T(8,128)(2,1)S(1)}, bf16[384,384]{1,0:T(8,128)(2,1)S(1)}, u32[]{:S(2)}, u32[]{:S(2)}) collective-permute-start(bf16[384,384]{1,0:T(8,128)(2,1)S(1)} %add_convert_fusion.1), channel_id=1, source_target_pairs={{2,0},{4,2},{6,4},{7,6},{5,7},{3,5},{1,3},{0,1},{10,8},{12,10},{14... | collective-permute-start | bytes 884744 | tf_op jit(solution)/shard_map/ppermute | solution.py:1486
  354.9 13.0 %collective-permute-start.107 = (bf16[128,768]{1,0:T(8,128)(2,1)S(1)}, bf16[128,768]{1,0:T(8,128)(2,1)S(1)}, u32[]{:S(2)}, u32[]{:S(2)}) collective-permute-start(bf16[128,768]{1,0:T(8,128)(2,1)S(1)} %get-tuple-element.342), channel_id=1, source_target_pairs={{2,0},{3,1},{0,2},{1,3},{10,4},{11,5},{8,6},{9,7},{6,8},{7,9},{4,1... | collective-permute-start | bytes 589832 | tf_op jit(solution)/shard_map/ppermute | solution.py:1530
  (193 other events, 2193.7 us)
